TPU v7x, 32 devices: a whole 2x2x4 slice. The times are simulated.
32 devices in a mesh: section: 2 (over x), dp: 4 (over z), ctx: 4 (over y, core).
Axes of the slice: x: 2, y: 2, z: 4, core: 2. Of those that a mesh axis runs over, the one named last changes fastest.
Arguments:
- inputs: bfloat16 [2, 4, 1024, 768], P(None, 'dp', 'ctx'), may hold values from -6 to 6
- slot_order: int32 [2, 4, 8], P(None, 'dp'), may hold values from 0 to 7, as said below
- cotangent: bfloat16 [2, 4, 1024, 768], P(None, 'dp', 'ctx'), may hold values from -6 to 6
- gains: float32 [2, 2, 768], P('section'), may hold values from 0.25 to 1.75
- biases: float32 [2, 7680], P('section'), may hold values from -2 to 2
- w_qkv: bfloat16 [2, 768, 2304], P('section'), may hold values from -0.21875 to 0.21875
- w_out: bfloat16 [2, 768, 768], P('section'), may hold values from -3 to 3
- w_up: bfloat16 [2, 768, 3072], P('section'), may hold values from -0.21875 to 0.21875
- w_down: bfloat16 [2, 3072, 768], P('section'), may hold values from -0.109375 to 0.109375
Outputs:
- acts: bfloat16 [2, 2, 4, 1024, 768], P('section', None, 'dp', 'ctx')
- grads: float32 [2, 2, 4, 1024, 768], P('section', None, 'dp', 'ctx')
- grad_gains: float32 [2, 2, 768], P('section', None, ('dp', 'ctx'))
- grad_biases: float32 [2, 7680], P('section', ('dp', 'ctx'))
- grad_qkv: float32 [2, 768, 2304], P('section', ('dp', 'ctx'))
- grad_out: float32 [2, 768, 768], P('section', ('dp', 'ctx'))
- grad_up: float32 [2, 768, 3072], P('section', ('dp', 'ctx'))
- grad_down: float32 [2, 3072, 768], P('section', ('dp', 'ctx'))
Inputs may be any that keep to these rules, and one draw needn't show every extreme that they name: `slot_order`: for each micro-batch and replica the 8 entries are a permutation of 0 to 7, and slots 2 m and 2 m + 1 add up to 7.
All inputs are finite; a program needn't handle non-finite values.
Results may differ from a plain program's by a relative error of at most 0.03.
Values may be sent and summed in bfloat16 or wider, within the bound.
No kernel may reach another device: no remote copies, remote signals or barrier semaphores. Data moves between devices by JAX's collectives and lax.ppermute only.
A program may use at most 320 MiB of HBM per device.

v0:
```python
import jax
import jax.numpy as jnp
from jax import lax
from jax.sharding import PartitionSpec as P

D = 768
HEADS = 12
HDIM = 64


def shifted(value, axis, steps):
    count = lax.axis_size(axis)
    initial, last = (max(0, -steps), min(count, count - steps))
    return lax.ppermute(value, axis, [(source, source + steps) for source in range(initial, last)])


def layer_norm(inputs_row, gain_row, offset):
    center = inputs_row - jnp.mean(inputs_row, axis=-1, keepdims=True)
    spread = jnp.mean(center * center, axis=-1, keepdims=True)
    return center * lax.rsqrt(spread + 1e-05) * gain_row + offset


def gelu_tanh(hidden):
    return jax.nn.gelu(hidden, approximate=True)


def score_terms(queries, key_rows, query_pos, key_pos, signed):
    key_count = key_rows.shape[0]
    scores = (
        jnp.einsum(
            "rhe,khe->hrk",
            queries,
            key_rows.reshape(key_count, HEADS, HDIM),
            preferred_element_type=jnp.float32,
        )
        * 0.125
    )
    curved = jnp.sqrt(scores * scores + 1.0)
    argument = jnp.where(signed, curved, scores)
    sign_pattern = jnp.where(signed, scores / curved, 1.0)
    slope = jnp.where(signed, sign_pattern, 1.0)
    bend = jnp.where(signed, 1.0 / (curved * curved * curved), 0.0)
    permitted_mask = key_pos[None, None, :] <= query_pos[None, :, None]
    return (argument, sign_pattern, slope, bend, permitted_mask)


def score_grads(
    queries, key_rows, value_rows, query_pos, key_pos, log_total, delta, grad_att, signed
):
    argument, sign_pattern, slope, bend, permitted_mask = score_terms(
        queries, key_rows, query_pos, key_pos, signed
    )
    prob = jnp.where(permitted_mask, jnp.exp(argument - log_total[..., None]), 0.0)
    along = jnp.einsum("rhe,khe->hrk", grad_att, value_rows, preferred_element_type=jnp.float32)
    dscore = (prob * ((sign_pattern * along - delta[..., None]) * slope + along * bend)).astype(
        jnp.bfloat16
    )
    return ((sign_pattern * prob).astype(jnp.bfloat16), dscore)


def key_blocks_of(key_all, value_all, key_pos, key_block):
    blocks = key_all.shape[0] // key_block
    return (
        key_all.reshape(blocks, key_block, D),
        value_all.reshape(blocks, key_block, HEADS, HDIM),
        key_pos.reshape(blocks, key_block),
    )


def attend(queries, query_pos, key_all, value_all, key_pos, signed, key_block):
    row_count = queries.shape[0]
    key_split, value_split, pos_split = key_blocks_of(key_all, value_all, key_pos, key_block)

    def running_total(state_in, element):
        largest, row_total_sum, gathered = state_in
        key_rows, value_rows, block_pos = element
        argument, sign_pattern, _, _, permitted_mask = score_terms(
            queries, key_rows, query_pos, block_pos, signed
        )
        masked_scores = jnp.where(permitted_mask, argument, -1e30)
        exponent_values = jnp.maximum(largest, jnp.max(masked_scores, axis=-1))
        multiplier = jnp.exp(largest - exponent_values)
        added_terms = jnp.where(
            permitted_mask, jnp.exp(masked_scores - exponent_values[..., None]), 0.0
        )
        row_total_sum = row_total_sum * multiplier + jnp.sum(added_terms, axis=-1)
        attention_weights = (sign_pattern * added_terms).astype(jnp.bfloat16)
        added = jnp.einsum(
            "hrk,khe->rhe", attention_weights, value_rows, preferred_element_type=jnp.float32
        )
        gathered = gathered * multiplier.T[:, :, None] + added
        return ((exponent_values, row_total_sum, gathered), None)

    start_max = jnp.full((HEADS, row_count), -1e30, jnp.float32)
    start_sum = jnp.zeros((HEADS, row_count), jnp.float32)
    start_out = jnp.zeros((row_count, HEADS, HDIM), jnp.float32)
    (largest, row_total_sum, gathered), _ = lax.scan(
        running_total, (start_max, start_sum, start_out), (key_split, value_split, pos_split)
    )
    log_total = largest + jnp.log(row_total_sum)
    attended = gathered / row_total_sum.T[:, :, None]
    return (attended, log_total)


def backward_summed(
    queries, query_pos, key_all, value_all, key_pos, log_total, delta, grad_att, signed, key_block
):
    key_split, value_split, pos_split = key_blocks_of(key_all, value_all, key_pos, key_block)

    def step_back(grad_q, element):
        key_rows, value_rows, block_pos = element
        attention_weights, dscore = score_grads(
            queries, key_rows, value_rows, query_pos, block_pos, log_total, delta, grad_att, signed
        )
        grad_q = (
            grad_q
            + jnp.einsum(
                "hrk,khe->rhe",
                dscore,
                key_rows.reshape(-1, HEADS, HDIM),
                preferred_element_type=jnp.float32,
            )
            * 0.125
        )
        grad_k = (
            jnp.einsum("hrk,rhe->khe", dscore, queries, preferred_element_type=jnp.float32) * 0.125
        )
        grad_v = jnp.einsum(
            "hrk,rhe->khe", attention_weights, grad_att, preferred_element_type=jnp.float32
        )
        return (grad_q, (grad_k.reshape(key_block, D), grad_v.reshape(key_block, D)))

    start_q = jnp.zeros(queries.shape, jnp.float32)
    grad_q, (grad_k, grad_v) = lax.scan(step_back, start_q, (key_split, value_split, pos_split))
    grad_k, grad_v = (
        lax.psum_scatter(
            grad_k.reshape(-1, D).astype(jnp.bfloat16), "ctx", scatter_dimension=0, tiled=True
        ).astype(jnp.float32),
        lax.psum_scatter(
            grad_v.reshape(-1, D).astype(jnp.bfloat16), "ctx", scatter_dimension=0, tiled=True
        ).astype(jnp.float32),
    )
    return (grad_q.reshape(-1, D), grad_k, grad_v)


def layer_front(inputs_row, gain_pair, bias_row, qkv_w):
    normed = layer_norm(inputs_row, gain_pair[0], bias_row[0:D]).astype(jnp.bfloat16)
    qkv_bias = jnp.concatenate(
        [bias_row[2 * D : 3 * D], jnp.zeros((D,), jnp.float32), bias_row[3 * D : 4 * D]]
    )
    projected = (jnp.dot(normed, qkv_w, preferred_element_type=jnp.float32) + qkv_bias).astype(
        jnp.bfloat16
    )
    return (normed, projected)


def layer_rest(inputs_row, attended_b, gain_pair, bias_row, out_w, up_w, down_w):
    middle = (
        inputs_row
        + jnp.dot(attended_b, out_w, preferred_element_type=jnp.float32)
        + bias_row[4 * D : 5 * D]
    )
    normed_two = layer_norm(middle, gain_pair[1], bias_row[D : 2 * D]).astype(jnp.bfloat16)
    hidden = jnp.dot(normed_two, up_w, preferred_element_type=jnp.float32) + bias_row[6 * D :]
    active = gelu_tanh(hidden).astype(jnp.bfloat16)
    result = (
        middle
        + jnp.dot(active, down_w, preferred_element_type=jnp.float32)
        + bias_row[5 * D : 6 * D]
    )
    return (middle, normed_two, hidden, active, result)


def body(inputs, slot_order, cotangent, gains, biases, w_qkv, w_out, w_up, w_down):
    micro_count = inputs.shape[0]
    row_count = inputs.shape[2]
    section_at = lax.axis_index("section")
    ctx_at = lax.axis_index("ctx")
    signed = section_at == 0
    gain_pair = gains[0]
    bias_row = biases[0]
    qkv_w = w_qkv[0]
    out_w = w_out[0]
    up_w = w_up[0]
    down_w = w_down[0]
    span_len = row_count // 2
    seq_pos = (
        slot_order[:, 0, :, None] * span_len + jnp.arange(span_len, dtype=jnp.int32)
    ).reshape(micro_count, -1)
    key_block = min(seq_pos.shape[1], 512)
    first_inputs = inputs[:, 0]
    cot_rows = cotangent[:, 0]

    def sequence_pos(index):
        whole_pos = lax.dynamic_index_in_dim(seq_pos, index, 0, keepdims=False)
        own_pos = lax.dynamic_slice_in_dim(whole_pos, ctx_at * row_count, row_count, 0)
        return (whole_pos, own_pos)

    def layer_forward(entry, index):
        whole_pos, own_pos = sequence_pos(index)
        inputs_row = entry.astype(jnp.float32)
        normed, projected = layer_front(inputs_row, gain_pair, bias_row, qkv_w)
        key_all, value_all = (
            lax.all_gather(projected[:, D : 2 * D], "ctx", axis=0, tiled=True),
            lax.all_gather(projected[:, 2 * D :], "ctx", axis=0, tiled=True),
        )
        queries = projected[:, :D].reshape(row_count, HEADS, HDIM)
        attended, _ = attend(queries, own_pos, key_all, value_all, whole_pos, signed, key_block)
        attended_b = attended.reshape(row_count, D).astype(jnp.bfloat16)
        result = layer_rest(inputs_row, attended_b, gain_pair, bias_row, out_w, up_w, down_w)[4]
        return result.astype(jnp.bfloat16)

    def layer_reverse_pass(entry, result_gradient, index):
        whole_pos, own_pos = sequence_pos(index)
        inputs_row = entry.astype(jnp.float32)
        normed, projected = layer_front(inputs_row, gain_pair, bias_row, qkv_w)
        queries = projected[:, :D].reshape(row_count, HEADS, HDIM)
        key_all, value_all = (
            lax.all_gather(projected[:, D : 2 * D], "ctx", axis=0, tiled=True),
            lax.all_gather(projected[:, 2 * D :], "ctx", axis=0, tiled=True),
        )
        attended, log_total = attend(
            queries, own_pos, key_all, value_all, whole_pos, signed, key_block
        )
        attended_b = attended.reshape(row_count, D).astype(jnp.bfloat16)
        middle, normed_two, hidden, active, _ = layer_rest(
            inputs_row, attended_b, gain_pair, bias_row, out_w, up_w, down_w
        )
        grad_down_b = result_gradient.astype(jnp.bfloat16)
        grad_wdown = jnp.dot(active.T, grad_down_b, preferred_element_type=jnp.float32)
        grad_active = jnp.dot(grad_down_b, down_w.T, preferred_element_type=jnp.float32)
        _, gelu_back = jax.vjp(gelu_tanh, hidden)
        grad_hidden = gelu_back(grad_active)[0]
        grad_hidden_b = grad_hidden.astype(jnp.bfloat16)
        grad_wup = jnp.dot(normed_two.T, grad_hidden_b, preferred_element_type=jnp.float32)
        grad_normed_two = jnp.dot(grad_hidden_b, up_w.T, preferred_element_type=jnp.float32)
        _, norm_back_two = jax.vjp(layer_norm, middle, gain_pair[1], bias_row[D : 2 * D])
        grad_middle_part, grad_gain_two, grad_offset_two = norm_back_two(grad_normed_two)
        grad_middle = result_gradient + grad_middle_part
        grad_proj_b = grad_middle.astype(jnp.bfloat16)
        grad_wout = jnp.dot(attended_b.T, grad_proj_b, preferred_element_type=jnp.float32)
        grad_att_flat = jnp.dot(grad_proj_b, out_w.T, preferred_element_type=jnp.float32).astype(
            jnp.bfloat16
        )
        grad_att = grad_att_flat.reshape(row_count, HEADS, HDIM)
        delta = jnp.einsum("rhe,rhe->hr", grad_att.astype(jnp.float32), attended)
        grad_q, grad_k, grad_v = backward_summed(
            queries,
            own_pos,
            key_all,
            value_all,
            whole_pos,
            log_total,
            delta,
            grad_att,
            signed,
            key_block,
        )
        grad_qkv_b = jnp.concatenate([grad_q, grad_k, grad_v], axis=1).astype(jnp.bfloat16)
        grad_wqkv = jnp.dot(normed.T, grad_qkv_b, preferred_element_type=jnp.float32)
        grad_normed = jnp.dot(grad_qkv_b, qkv_w.T, preferred_element_type=jnp.float32)
        _, norm_back_one = jax.vjp(layer_norm, inputs_row, gain_pair[0], bias_row[0:D])
        grad_in_part, grad_gain_one, grad_offset_one = norm_back_one(grad_normed)
        input_gradient = grad_middle + grad_in_part
        grad_gain_rows = jnp.stack([grad_gain_one, grad_gain_two])
        grad_bias_row = jnp.concatenate(
            [
                grad_offset_one,
                grad_offset_two,
                jnp.sum(grad_q, axis=0),
                jnp.sum(grad_v, axis=0),
                jnp.sum(grad_middle, axis=0),
                jnp.sum(result_gradient, axis=0),
                jnp.sum(grad_hidden, axis=0),
            ]
        )
        return (
            input_gradient,
            (grad_gain_rows, grad_bias_row, grad_wqkv, grad_wout, grad_wup, grad_wdown),
        )

    def tick(tick_at, state_in):
        arrived, returned, stored, acts_rows, grad_rows, partial_sums = state_in
        ahead = tick_at - section_at
        ahead_ok = (ahead >= 0) & (ahead < micro_count)
        ahead_at = jnp.clip(ahead, 0, micro_count - 1)
        fresh = jnp.where(
            signed, lax.dynamic_index_in_dim(first_inputs, ahead_at, 0, keepdims=False), arrived
        )
        previous = lax.dynamic_index_in_dim(stored, ahead_at, 0, keepdims=False)
        entry = jnp.where(ahead_ok, fresh, previous)
        stored = lax.dynamic_update_index_in_dim(stored, entry, ahead_at, 0)
        sent = layer_forward(entry, ahead_at)
        old_acts = lax.dynamic_index_in_dim(acts_rows, ahead_at, 0, keepdims=False)
        acts_rows = lax.dynamic_update_index_in_dim(
            acts_rows, jnp.where(ahead_ok, sent, old_acts), ahead_at, 0
        )
        behind = tick_at - 2 + section_at
        trailing_valid = (behind >= 0) & (behind < micro_count)
        trailing_position = jnp.clip(behind, 0, micro_count - 1)
        entry_gradient = lax.dynamic_index_in_dim(stored, trailing_position, 0, keepdims=False)
        given_cot = lax.dynamic_index_in_dim(cot_rows, trailing_position, 0, keepdims=False).astype(
            jnp.float32
        )
        result_gradient = jnp.where(signed, returned.astype(jnp.float32), given_cot)
        input_gradient, added_terms = layer_reverse_pass(
            entry_gradient, result_gradient, trailing_position
        )
        partial_sums = jax.tree.map(
            lambda running_total, added_term: running_total
            + jnp.where(trailing_valid, added_term, 0.0),
            partial_sums,
            added_terms,
        )
        handed = input_gradient.astype(jnp.bfloat16)
        kept_grad = jnp.where(signed, input_gradient, handed.astype(jnp.float32))
        old_grads = lax.dynamic_index_in_dim(grad_rows, trailing_position, 0, keepdims=False)
        grad_rows = lax.dynamic_update_index_in_dim(
            grad_rows, jnp.where(trailing_valid, kept_grad, old_grads), trailing_position, 0
        )
        arrived = shifted(sent, "section", 1)
        returned = shifted(handed, "section", -1)
        return (arrived, returned, stored, acts_rows, grad_rows, partial_sums)

    zero_rows = jnp.zeros((row_count, D), jnp.bfloat16)
    start_sums = (
        jnp.zeros((2, D), jnp.float32),
        jnp.zeros((bias_row.shape[0],), jnp.float32),
        jnp.zeros(qkv_w.shape, jnp.float32),
        jnp.zeros(out_w.shape, jnp.float32),
        jnp.zeros(up_w.shape, jnp.float32),
        jnp.zeros(down_w.shape, jnp.float32),
    )
    start_state = (
        zero_rows,
        zero_rows,
        jnp.zeros((micro_count, row_count, D), jnp.bfloat16),
        jnp.zeros((micro_count, row_count, D), jnp.bfloat16),
        jnp.zeros((micro_count, row_count, D), jnp.float32),
        start_sums,
    )
    final_state = lax.fori_loop(0, micro_count + 2, tick, start_state)
    acts_rows = final_state[3]
    grad_rows = final_state[4]
    partial_sums = final_state[5]
    totals = (
        lax.psum_scatter(partial_sums[0], ("dp", "ctx"), scatter_dimension=1, tiled=True),
        lax.psum_scatter(partial_sums[1], ("dp", "ctx"), scatter_dimension=0, tiled=True),
        lax.psum_scatter(partial_sums[2], ("dp", "ctx"), scatter_dimension=0, tiled=True),
        lax.psum_scatter(partial_sums[3], ("dp", "ctx"), scatter_dimension=0, tiled=True),
        lax.psum_scatter(partial_sums[4], ("dp", "ctx"), scatter_dimension=0, tiled=True),
        lax.psum_scatter(partial_sums[5], ("dp", "ctx"), scatter_dimension=0, tiled=True),
    )
    return (
        acts_rows[None, :, None],
        grad_rows[None, :, None],
        totals[0][None],
        totals[1][None],
        totals[2][None],
        totals[3][None],
        totals[4][None],
        totals[5][None],
    )


def solution(mesh):
    in_specs = (
        P(None, "dp", "ctx", None),
        P(None, "dp", None),
        P(None, "dp", "ctx", None),
        P("section", None, None),
        P("section", None),
        P("section", None, None),
        P("section", None, None),
        P("section", None, None),
        P("section", None, None),
    )
    out_specs = (
        P("section", None, "dp", "ctx", None),
        P("section", None, "dp", "ctx", None),
        P("section", None, ("dp", "ctx")),
        P("section", ("dp", "ctx")),
        P("section", ("dp", "ctx"), None),
        P("section", ("dp", "ctx"), None),
        P("section", ("dp", "ctx"), None),
        P("section", ("dp", "ctx"), None),
    )
    return jax.shard_map(body, mesh=mesh, in_specs=in_specs, out_specs=out_specs, check_vma=False)
```

profile of v0, /device:TPU:0, one launch (start us, length us, event | category | flops | bytes accessed | tf_op | source)
XLA Modules:
  0.0 1628.6 jit_solution(9982931050397500290)
XLA Ops:
  15.5 1152.8 %while.200 = (s32[]{:T(128)}, bf16[256,768]{1,0:T(8,128)(2,1)}, bf16[256,768]{1,0:T(8,128)(2,1)}, bf16[2,256,768]{2,1,0:T(8,128)(2,1)}, bf16[2,256,768]{2,1,0:T(...) while((s32[]{:T(128)}, bf16[256,768]{1,0:T(8,128)(2,1)}, ...), condition=%wide.region_34.35_spmd.clone, body=%wide.region_0.34_spmd.clone.sunk | while | flops 15317989376 | bytes 607702976 | solution.py:342
  54.3 16.9 %all-gather.9.cloned.1.call-done = bf16[1024,768]{1,0:T(8,128)(2,1)} async-done(((bf16[256,768]{1,0:T(8,128)(2,1)}), bf16[1024,768]{1,0:T(8,128)(2,1)}) %all-gather.9.cloned.1.call-update) | async-done | bytes 1572880 | tf_op jit(solution)/shard_map/while/body/eval_jaxpr/all_gather | solution.py:219
  73.8 41.3 %while.202 = (s32[]{:T(128)}, f32[12,256]{1,0:T(8,128)S(1)}, f32[12,256]{1,0:T(8,128)S(1)}, f32[256,12,64]{0,2,1:T(8,128)S(1)}, s32[2,512]{1,0:T(2,128)}, /*inde...) while((s32[]{:T(128)}, f32[12,256]{1,0:T(8,128)S(1)}, ...), condition=%wide.region_14.14_spmd.clone, body=%wide.region_11.13_spmd.clone.sunk | while | flops 442714112 | bytes 49888424 | solution.py:97
  135.0 67.6 %while.203 = (s32[]{:T(128)}, f32[256,12,64]{0,2,1:T(8,128)}, bf16[2,512,768]{2,1,0:T(8,128)(2,1)}, bf16[2,512,768]{2,1,0:T(8,128)(2,1)}, bf16[2,512,768]{1,2,0:...) while((s32[]{:T(128)}, f32[256,12,64]{0,2,1:T(8,128)}, ...), condition=%wide.region_20.20_spmd.clone, body=%wide.region_19.19_spmd.clone.sunk | while | flops 1055326208 | bytes 78974824 | solution.py:134
  139.3 8.6 fusion.353
  152.1 9.1 fusion.355
  172.7 8.6 fusion.353
  185.5 9.1 fusion.355
  209.8 39.8 %while.201 = (s32[]{:T(128)}, f32[12,256]{1,0:T(8,128)S(1)}, f32[12,256]{1,0:T(8,128)S(1)}, f32[256,12,64]{0,2,1:T(8,128)}, s32[2,512]{1,0:T(2,128)S(1)}, /*inde...) while((s32[]{:T(128)}, f32[12,256]{1,0:T(8,128)S(1)}, ...), condition=%wide.region_6.6_spmd.clone, body=%wide.region_3.5_spmd.clone.sunk | while | flops 442714112 | bytes 59318520 | solution.py:97
  217.9 8.1 fusion.332
  256.4 8.4 bitcast_dynamic-update-slice_fusion.6
  338.7 16.9 %all-gather.9.cloned.1.call-done = bf16[1024,768]{1,0:T(8,128)(2,1)} async-done(((bf16[256,768]{1,0:T(8,128)(2,1)}), bf16[1024,768]{1,0:T(8,128)(2,1)}) %all-gather.9.cloned.1.call-update) | async-done | bytes 1572880 | tf_op jit(solution)/shard_map/while/body/eval_jaxpr/all_gather | solution.py:219
  358.2 41.3 %while.202 = (s32[]{:T(128)}, f32[12,256]{1,0:T(8,128)S(1)}, f32[12,256]{1,0:T(8,128)S(1)}, f32[256,12,64]{0,2,1:T(8,128)S(1)}, s32[2,512]{1,0:T(2,128)}, /*inde...) while((s32[]{:T(128)}, f32[12,256]{1,0:T(8,128)S(1)}, ...), condition=%wide.region_14.14_spmd.clone, body=%wide.region_11.13_spmd.clone.sunk | while | flops 442714112 | bytes 49888424 | solution.py:97
  419.3 67.6 %while.203 = (s32[]{:T(128)}, f32[256,12,64]{0,2,1:T(8,128)}, bf16[2,512,768]{2,1,0:T(8,128)(2,1)}, bf16[2,512,768]{2,1,0:T(8,128)(2,1)}, bf16[2,512,768]{1,2,0:...) while((s32[]{:T(128)}, f32[256,12,64]{0,2,1:T(8,128)}, ...), condition=%wide.region_20.20_spmd.clone, body=%wide.region_19.19_spmd.clone.sunk | while | flops 1055326208 | bytes 78974824 | solution.py:134
  423.6 8.6 fusion.353
  436.5 9.1 fusion.355
  457.0 8.6 fusion.353
  469.8 9.1 fusion.355
  494.1 39.8 %while.201 = (s32[]{:T(128)}, f32[12,256]{1,0:T(8,128)S(1)}, f32[12,256]{1,0:T(8,128)S(1)}, f32[256,12,64]{0,2,1:T(8,128)}, s32[2,512]{1,0:T(2,128)S(1)}, /*inde...) while((s32[]{:T(128)}, f32[12,256]{1,0:T(8,128)S(1)}, ...), condition=%wide.region_6.6_spmd.clone, body=%wide.region_3.5_spmd.clone.sunk | while | flops 442714112 | bytes 59318520 | solution.py:97
  502.2 8.1 fusion.332
  540.8 8.4 bitcast_dynamic-update-slice_fusion.6
  554.2 10.1 select_add_fusion.13
  626.7 16.8 %all-gather.9.cloned.1.call-done = bf16[1024,768]{1,0:T(8,128)(2,1)} async-done(((bf16[256,768]{1,0:T(8,128)(2,1)}), bf16[1024,768]{1,0:T(8,128)(2,1)}) %all-gather.9.cloned.1.call-update) | async-done | bytes 1572880 | tf_op jit(solution)/shard_map/while/body/eval_jaxpr/all_gather | solution.py:219
  646.1 41.3 %while.202 = (s32[]{:T(128)}, f32[12,256]{1,0:T(8,128)S(1)}, f32[12,256]{1,0:T(8,128)S(1)}, f32[256,12,64]{0,2,1:T(8,128)S(1)}, s32[2,512]{1,0:T(2,128)}, /*inde...) while((s32[]{:T(128)}, f32[12,256]{1,0:T(8,128)S(1)}, ...), condition=%wide.region_14.14_spmd.clone, body=%wide.region_11.13_spmd.clone.sunk | while | flops 442714112 | bytes 49888424 | solution.py:97
  707.2 67.6 %while.203 = (s32[]{:T(128)}, f32[256,12,64]{0,2,1:T(8,128)}, bf16[2,512,768]{2,1,0:T(8,128)(2,1)}, bf16[2,512,768]{2,1,0:T(8,128)(2,1)}, bf16[2,512,768]{1,2,0:...) while((s32[]{:T(128)}, f32[256,12,64]{0,2,1:T(8,128)}, ...), condition=%wide.region_20.20_spmd.clone, body=%wide.region_19.19_spmd.clone.sunk | while | flops 1055326208 | bytes 78974824 | solution.py:134
  711.5 8.6 fusion.353
  724.4 9.1 fusion.355
  744.9 8.6 fusion.353
  757.7 9.1 fusion.355
  782.0 39.8 %while.201 = (s32[]{:T(128)}, f32[12,256]{1,0:T(8,128)S(1)}, f32[12,256]{1,0:T(8,128)S(1)}, f32[256,12,64]{0,2,1:T(8,128)}, s32[2,512]{1,0:T(2,128)S(1)}, /*inde...) while((s32[]{:T(128)}, f32[12,256]{1,0:T(8,128)S(1)}, ...), condition=%wide.region_6.6_spmd.clone, body=%wide.region_3.5_spmd.clone.sunk | while | flops 442714112 | bytes 59318520 | solution.py:97
  790.1 8.1 fusion.332
  828.7 8.4 bitcast_dynamic-update-slice_fusion.6
  842.0 10.1 select_add_fusion.13
  914.6 16.7 %all-gather.9.cloned.1.call-done = bf16[1024,768]{1,0:T(8,128)(2,1)} async-done(((bf16[256,768]{1,0:T(8,128)(2,1)}), bf16[1024,768]{1,0:T(8,128)(2,1)}) %all-gather.9.cloned.1.call-update) | async-done | bytes 1572880 | tf_op jit(solution)/shard_map/while/body/eval_jaxpr/all_gather | solution.py:219
  933.9 41.3 %while.202 = (s32[]{:T(128)}, f32[12,256]{1,0:T(8,128)S(1)}, f32[12,256]{1,0:T(8,128)S(1)}, f32[256,12,64]{0,2,1:T(8,128)S(1)}, s32[2,512]{1,0:T(2,128)}, /*inde...) while((s32[]{:T(128)}, f32[12,256]{1,0:T(8,128)S(1)}, ...), condition=%wide.region_14.14_spmd.clone, body=%wide.region_11.13_spmd.clone.sunk | while | flops 442714112 | bytes 49888424 | solution.py:97
  995.1 67.6 %while.203 = (s32[]{:T(128)}, f32[256,12,64]{0,2,1:T(8,128)}, bf16[2,512,768]{2,1,0:T(8,128)(2,1)}, bf16[2,512,768]{2,1,0:T(8,128)(2,1)}, bf16[2,512,768]{1,2,0:...) while((s32[]{:T(128)}, f32[256,12,64]{0,2,1:T(8,128)}, ...), condition=%wide.region_20.20_spmd.clone, body=%wide.region_19.19_spmd.clone.sunk | while | flops 1055326208 | bytes 78974824 | solution.py:134
  999.4 8.6 fusion.353
  1012.2 9.1 fusion.355
  1032.7 8.6 fusion.353
  1045.6 9.1 fusion.355
  1069.8 39.8 %while.201 = (s32[]{:T(128)}, f32[12,256]{1,0:T(8,128)S(1)}, f32[12,256]{1,0:T(8,128)S(1)}, f32[256,12,64]{0,2,1:T(8,128)}, s32[2,512]{1,0:T(2,128)S(1)}, /*inde...) while((s32[]{:T(128)}, f32[12,256]{1,0:T(8,128)S(1)}, ...), condition=%wide.region_6.6_spmd.clone, body=%wide.region_3.5_spmd.clone.sunk | while | flops 442714112 | bytes 59318520 | solution.py:97
  1116.5 8.4 bitcast_dynamic-update-slice_fusion.6
  1129.9 10.1 select_add_fusion.13
  1174.0 59.9 %all-reduce = f32[7680]{0:T(1024)S(1)} all-reduce(f32[7680]{0:T(1024)S(1)} %copy-done.52), channel_id=5, replica_groups=mesh['section'=2,'dp'=4,'ctx'=4] {'dp','ctx'}, use_global_device_ids=true, to_apply=%region_36.37.clone | all-reduce | flops 7680 | bytes 61440
  1235.9 57.9 %reduce-scatter.12.cloned.1.call-done = f32[48,768]{1,0:T(8,128)} async-done(((f32[768,768]{1,0:T(8,128)}), f32[48,768]{1,0:T(8,128)}) %reduce-scatter.12.cloned.1.call-update) | async-done | bytes 147472 | tf_op jit(solution)/shard_map/reduce_scatter | solution.py:350
  1293.9 93.4 %reduce-scatter.10.cloned.1.call-done = f32[48,2304]{1,0:T(8,128)} async-done(((f32[768,2304]{1,0:T(8,128)}), f32[48,2304]{1,0:T(8,128)}) %reduce-scatter.10.cloned.1.call-update) | async-done | bytes 442384 | tf_op jit(solution)/shard_map/reduce_scatter | solution.py:349
  1387.3 116.9 %reduce-scatter.14.cloned.1.call-done = f32[48,3072]{1,0:T(8,128)} async-done(((f32[768,3072]{1,0:T(8,128)}), f32[48,3072]{1,0:T(8,128)}) %reduce-scatter.14.cloned.1.call-update) | async-done | bytes 589840 | tf_op jit(solution)/shard_map/reduce_scatter | solution.py:351
  1504.2 116.5 %reduce-scatter.16.cloned.1.call-done = f32[192,768]{1,0:T(8,128)} async-done(((f32[3072,768]{1,0:T(8,128)}), f32[192,768]{1,0:T(8,128)}) %reduce-scatter.16.cloned.1.call-update) | async-done | bytes 589840 | tf_op jit(solution)/shard_map/reduce_scatter | solution.py:352
  (1477 shorter events, 855.8 us)
Async XLA Ops:
  15.5 34.4 %all-gather.11.cloned.1.call-start = ((), (), s32[]{:S(2)}) async-start(), calls=%async_computation.15 | async-start | bytes 1966080 | tf_op jit(solution)/shard_map/while/body/eval_jaxpr/all_gather | solution.py:220
  27.3 44.0 %all-gather.9.cloned.1.call-start = ((), (), s32[]{:S(2)}) async-start(), calls=%async_computation.14 | async-start | bytes 1966080 | tf_op jit(solution)/shard_map/while/body/eval_jaxpr/all_gather | solution.py:219
  28.0 177.2 %all-gather.7.cloned.1.call-start = ((), (), s32[]{:S(2)}) async-start(), calls=%async_computation.13 | async-start | bytes 1966080 | tf_op jit(solution)/shard_map/while/body/eval_jaxpr/all_gather | solution.py:205
  32.5 177.2 %all-gather.5.cloned.1.call-start = ((), (), s32[]{:S(2)}) async-start(), calls=%async_computation.12 | async-start | bytes 1966080 | tf_op jit(solution)/shard_map/while/body/eval_jaxpr/all_gather | solution.py:204
  33.1 247.1 %reduce-scatter.20.cloned.1.call-start = ((), (), s32[]{:S(2)}) async-start(), calls=%async_computation.16 | async-start | bytes 1966080 | tf_op jit(solution)/shard_map/while/body/eval_jaxpr/reduce_scatter | solution.py:139
  52.8 21.0 %copy-start.19 = (f32[256,12,64]{0,2,1:T(8,128)S(1)}, f32[256,12,64]{0,2,1:T(8,128)}, u32[]{:S(2)}) copy-start(f32[256,12,64]{0,2,1:T(8,128)} %custom-call.38) | copy-start | bytes 2359300 | tf_op jit(solution)/shard_map/while
  54.3 19.5 %copy-start.32 = (f32[12,256]{1,0:T(8,128)S(1)}, f32[12,256]{1,0:T(8,128)}, u32[]{:S(2)}) copy-start(f32[12,256]{1,0:T(8,128)} %custom-call.37) | copy-start | bytes 36868 | tf_op jit(solution)/shard_map/while
  73.8 41.5 %copy-start.54 = (f32[768]{0:T(1024)S(1)}, f32[768]{0:T(1024)}, u32[]{:S(2)}) copy-start(f32[768]{0:T(1024)} %get-tuple-element.1805) | copy-start | bytes 9220 | tf_op jit(solution)/shard_map/while
  209.6 74.3 %reduce-scatter.22.cloned.1.call-start = ((), (), s32[]{:S(2)}) async-start(), calls=%async_computation.17 | async-start | bytes 1966080 | tf_op jit(solution)/shard_map/while/body/eval_jaxpr/reduce_scatter | solution.py:136
  264.8 37.5 %collective-permute-start = (bf16[256,768]{1,0:T(8,128)(2,1)}, bf16[256,768]{1,0:T(8,128)(2,1)}, u32[]{:S(2)}, u32[]{:S(2)}) collective-permute-start(bf16[256,768]{1,0:T(8,128)(2,1)} %get-tuple-element.1823), channel_id=1, source_target_pairs={{0,16},{1,17},{2,18},{3,19},{4,20},{5,21},{6,22},{7,23},{8,24},{9,... | collective-permute-start | bytes 1179656 | tf_op jit(solution)/shard_map/while/body/eval_jaxpr/ppermute | solution.py:14
  289.6 12.8 collective-permute-start.1
  303.5 30.7 %all-gather.11.cloned.1.call-start = ((), (), s32[]{:S(2)}) async-start(), calls=%async_computation.15 | async-start | bytes 1966080 | tf_op jit(solution)/shard_map/while/body/eval_jaxpr/all_gather | solution.py:220
  315.4 40.2 %all-gather.9.cloned.1.call-start = ((), (), s32[]{:S(2)}) async-start(), calls=%async_computation.14 | async-start | bytes 1966080 | tf_op jit(solution)/shard_map/while/body/eval_jaxpr/all_gather | solution.py:219
  316.1 173.4 %all-gather.7.cloned.1.call-start = ((), (), s32[]{:S(2)}) async-start(), calls=%async_computation.13 | async-start | bytes 1966080 | tf_op jit(solution)/shard_map/while/body/eval_jaxpr/all_gather | solution.py:205
  320.6 173.4 %all-gather.5.cloned.1.call-start = ((), (), s32[]{:S(2)}) async-start(), calls=%async_computation.12 | async-start | bytes 1966080 | tf_op jit(solution)/shard_map/while/body/eval_jaxpr/all_gather | solution.py:204
  321.2 250.5 %reduce-scatter.20.cloned.1.call-start = ((), (), s32[]{:S(2)}) async-start(), calls=%async_computation.16 | async-start | bytes 1966080 | tf_op jit(solution)/shard_map/while/body/eval_jaxpr/reduce_scatter | solution.py:139
  337.2 21.0 %copy-start.19 = (f32[256,12,64]{0,2,1:T(8,128)S(1)}, f32[256,12,64]{0,2,1:T(8,128)}, u32[]{:S(2)}) copy-start(f32[256,12,64]{0,2,1:T(8,128)} %custom-call.38) | copy-start | bytes 2359300 | tf_op jit(solution)/shard_map/while
  338.7 19.5 %copy-start.28 = (bf16[2,512,12,64]{1,3,2,0:T(8,128)(2,1)S(1)}, bf16[2,512,12,64]{1,3,2,0:T(8,128)(2,1)}, u32[]{:S(2)}) copy-start(bf16[2,512,12,64]{1,3,2,0:T(8,128)(2,1)} %copy.154) | copy-start | bytes 4718596 | tf_op jit(solution)/shard_map/while
  338.7 19.5 %copy-start.32 = (f32[12,256]{1,0:T(8,128)S(1)}, f32[12,256]{1,0:T(8,128)}, u32[]{:S(2)}) copy-start(f32[12,256]{1,0:T(8,128)} %custom-call.37) | copy-start | bytes 36868 | tf_op jit(solution)/shard_map/while
  358.2 41.5 %copy-start.54 = (f32[768]{0:T(1024)S(1)}, f32[768]{0:T(1024)}, u32[]{:S(2)}) copy-start(f32[768]{0:T(1024)} %get-tuple-element.1805) | copy-start | bytes 9220 | tf_op jit(solution)/shard_map/while
  494.0 77.7 %reduce-scatter.22.cloned.1.call-start = ((), (), s32[]{:S(2)}) async-start(), calls=%async_computation.17 | async-start | bytes 1966080 | tf_op jit(solution)/shard_map/while/body/eval_jaxpr/reduce_scatter | solution.py:136
  549.2 41.1 %collective-permute-start = (bf16[256,768]{1,0:T(8,128)(2,1)}, bf16[256,768]{1,0:T(8,128)(2,1)}, u32[]{:S(2)}, u32[]{:S(2)}) collective-permute-start(bf16[256,768]{1,0:T(8,128)(2,1)} %get-tuple-element.1823), channel_id=1, source_target_pairs={{0,16},{1,17},{2,18},{3,19},{4,20},{5,21},{6,22},{7,23},{8,24},{9,... | collective-permute-start | bytes 1179656 | tf_op jit(solution)/shard_map/while/body/eval_jaxpr/ppermute | solution.py:14
  577.3 12.9 collective-permute-start.1
  591.4 30.8 %all-gather.11.cloned.1.call-start = ((), (), s32[]{:S(2)}) async-start(), calls=%async_computation.15 | async-start | bytes 1966080 | tf_op jit(solution)/shard_map/while/body/eval_jaxpr/all_gather | solution.py:220
  603.2 40.2 %all-gather.9.cloned.1.call-start = ((), (), s32[]{:S(2)}) async-start(), calls=%async_computation.14 | async-start | bytes 1966080 | tf_op jit(solution)/shard_map/while/body/eval_jaxpr/all_gather | solution.py:219
  603.8 173.6 %all-gather.7.cloned.1.call-start = ((), (), s32[]{:S(2)}) async-start(), calls=%async_computation.13 | async-start | bytes 1966080 | tf_op jit(solution)/shard_map/while/body/eval_jaxpr/all_gather | solution.py:205
  608.3 173.6 %all-gather.5.cloned.1.call-start = ((), (), s32[]{:S(2)}) async-start(), calls=%async_computation.12 | async-start | bytes 1966080 | tf_op jit(solution)/shard_map/while/body/eval_jaxpr/all_gather | solution.py:204
  608.9 250.6 %reduce-scatter.20.cloned.1.call-start = ((), (), s32[]{:S(2)}) async-start(), calls=%async_computation.16 | async-start | bytes 1966080 | tf_op jit(solution)/shard_map/while/body/eval_jaxpr/reduce_scatter | solution.py:139
  625.2 20.9 %copy-start.19 = (f32[256,12,64]{0,2,1:T(8,128)S(1)}, f32[256,12,64]{0,2,1:T(8,128)}, u32[]{:S(2)}) copy-start(f32[256,12,64]{0,2,1:T(8,128)} %custom-call.38) | copy-start | bytes 2359300 | tf_op jit(solution)/shard_map/while
  646.0 41.5 %copy-start.54 = (f32[768]{0:T(1024)S(1)}, f32[768]{0:T(1024)}, u32[]{:S(2)}) copy-start(f32[768]{0:T(1024)} %get-tuple-element.1805) | copy-start | bytes 9220 | tf_op jit(solution)/shard_map/while
  781.9 77.7 %reduce-scatter.22.cloned.1.call-start = ((), (), s32[]{:S(2)}) async-start(), calls=%async_computation.17 | async-start | bytes 1966080 | tf_op jit(solution)/shard_map/while/body/eval_jaxpr/reduce_scatter | solution.py:136
  837.0 41.1 %collective-permute-start = (bf16[256,768]{1,0:T(8,128)(2,1)}, bf16[256,768]{1,0:T(8,128)(2,1)}, u32[]{:S(2)}, u32[]{:S(2)}) collective-permute-start(bf16[256,768]{1,0:T(8,128)(2,1)} %get-tuple-element.1823), channel_id=1, source_target_pairs={{0,16},{1,17},{2,18},{3,19},{4,20},{5,21},{6,22},{7,23},{8,24},{9,... | collective-permute-start | bytes 1179656 | tf_op jit(solution)/shard_map/while/body/eval_jaxpr/ppermute | solution.py:14
  865.2 12.9 collective-permute-start.1
  879.3 30.8 %all-gather.11.cloned.1.call-start = ((), (), s32[]{:S(2)}) async-start(), calls=%async_computation.15 | async-start | bytes 1966080 | tf_op jit(solution)/shard_map/while/body/eval_jaxpr/all_gather | solution.py:220
  891.1 40.2 %all-gather.9.cloned.1.call-start = ((), (), s32[]{:S(2)}) async-start(), calls=%async_computation.14 | async-start | bytes 1966080 | tf_op jit(solution)/shard_map/while/body/eval_jaxpr/all_gather | solution.py:219
  891.7 173.6 %all-gather.7.cloned.1.call-start = ((), (), s32[]{:S(2)}) async-start(), calls=%async_computation.13 | async-start | bytes 1966080 | tf_op jit(solution)/shard_map/while/body/eval_jaxpr/all_gather | solution.py:205
  896.2 173.6 %all-gather.5.cloned.1.call-start = ((), (), s32[]{:S(2)}) async-start(), calls=%async_computation.12 | async-start | bytes 1966080 | tf_op jit(solution)/shard_map/while/body/eval_jaxpr/all_gather | solution.py:204
  897.0 250.5 %reduce-scatter.20.cloned.1.call-start = ((), (), s32[]{:S(2)}) async-start(), calls=%async_computation.16 | async-start | bytes 1966080 | tf_op jit(solution)/shard_map/while/body/eval_jaxpr/reduce_scatter | solution.py:139
  913.1 20.9 %copy-start.19 = (f32[256,12,64]{0,2,1:T(8,128)S(1)}, f32[256,12,64]{0,2,1:T(8,128)}, u32[]{:S(2)}) copy-start(f32[256,12,64]{0,2,1:T(8,128)} %custom-call.38) | copy-start | bytes 2359300 | tf_op jit(solution)/shard_map/while
  933.9 41.5 %copy-start.54 = (f32[768]{0:T(1024)S(1)}, f32[768]{0:T(1024)}, u32[]{:S(2)}) copy-start(f32[768]{0:T(1024)} %get-tuple-element.1805) | copy-start | bytes 9220 | tf_op jit(solution)/shard_map/while
  1069.7 77.7 %reduce-scatter.22.cloned.1.call-start = ((), (), s32[]{:S(2)}) async-start(), calls=%async_computation.17 | async-start | bytes 1966080 | tf_op jit(solution)/shard_map/while/body/eval_jaxpr/reduce_scatter | solution.py:136
  1124.9 41.1 %collective-permute-start = (bf16[256,768]{1,0:T(8,128)(2,1)}, bf16[256,768]{1,0:T(8,128)(2,1)}, u32[]{:S(2)}, u32[]{:S(2)}) collective-permute-start(bf16[256,768]{1,0:T(8,128)(2,1)} %get-tuple-element.1823), channel_id=1, source_target_pairs={{0,16},{1,17},{2,18},{3,19},{4,20},{5,21},{6,22},{7,23},{8,24},{9,... | collective-permute-start | bytes 1179656 | tf_op jit(solution)/shard_map/while/body/eval_jaxpr/ppermute | solution.py:14
  1153.1 12.9 collective-permute-start.1
  1168.4 66.2 %reduce-scatter.18.cloned.1.call-start = ((), (), s32[]{:S(2)}) async-start(), calls=%async_computation.11 | async-start | bytes 417792
  1170.1 123.8 %reduce-scatter.12.cloned.1.call-start = ((), (), s32[]{:S(2)}) async-start(), calls=%async_computation.8 | async-start | bytes 2506752 | tf_op jit(solution)/shard_map/reduce_scatter | solution.py:350
  1170.7 216.6 %reduce-scatter.10.cloned.1.call-start = ((), (), s32[]{:S(2)}) async-start(), calls=%async_computation.7 | async-start | bytes 7520256 | tf_op jit(solution)/shard_map/reduce_scatter | solution.py:349
  1171.3 332.9 %reduce-scatter.14.cloned.1.call-start = ((), (), s32[]{:S(2)}) async-start(), calls=%async_computation.9 | async-start | bytes 10027008 | tf_op jit(solution)/shard_map/reduce_scatter | solution.py:351
  1172.0 448.6 %reduce-scatter.16.cloned.1.call-start = ((), (), s32[]{:S(2)}) async-start(), calls=%async_computation.10 | async-start | bytes 10027008 | tf_op jit(solution)/shard_map/reduce_scatter | solution.py:352
  (375 other events, 1975.7 us)
Sparse Core Ops, SparseCore 0:
  27.4 22.4 all-gather.10
  51.5 19.6 all-gather.8
  73.5 19.6 all-gather.6
  94.6 19.6 all-gather.4
  209.8 28.1 reduce-scatter.19
  255.6 28.2 reduce-scatter.21
  315.5 18.7 all-gather.10
  335.9 19.6 all-gather.8
  357.8 19.6 all-gather.6
  379.0 19.6 all-gather.4
  494.1 28.1 reduce-scatter.19
  540.0 28.2 reduce-scatter.21
  603.4 18.8 all-gather.10
  623.8 19.6 all-gather.8
  645.5 19.6 all-gather.6
  666.7 19.6 all-gather.4
  782.0 28.1 reduce-scatter.19
  827.8 28.2 reduce-scatter.21
  891.2 18.8 all-gather.10
  911.6 19.6 all-gather.8
  933.5 19.6 all-gather.6
  954.9 19.6 all-gather.4
  1069.9 28.1 reduce-scatter.19
  1115.7 28.2 reduce-scatter.21
Sparse Core Ops, SparseCore 1:
  1172.3 54.9 reduce-scatter.17
  1232.0 61.8 reduce-scatter.11
  1298.3 88.9 reduce-scatter.9
  1392.5 111.6 reduce-scatter.13
  1508.9 111.7 reduce-scatter.15
where the time goes:
time: 1640 us; the launch traced here: 1630 us
  matrix products  636 us (39%)
  waiting for transfers between devices  501 us (31%)
  local copies, waits for them, and re-layouts  249 us (15%)
  other arithmetic  126 us (8%)
  blocking collectives  59.9 us (4%)
  starting transfers between devices  25.2 us (2%)
  between operations  16.8 us (1%)
    dot_general x16, matrix products, running_total(): jnp.einsum('hrk,khe->rhe', attention_weights, value_rows, preferred_eleme...  127 us
    reduce_scatter x1, waiting for transfers between devices, body(): lax.psum_scatter(partial_sums[4], ('dp', 'ctx'), scatter_dimension=0, til...  117 us
    reduce_scatter x1, waiting for transfers between devices, body(): lax.psum_scatter(partial_sums[5], ('dp', 'ctx'), scatter_dimension=0, til...  116 us
    dot_general x24, matrix products, score_terms(): jnp.einsum('rhe,khe->hrk', queries, key_rows.reshape(key_count, HEADS, HD...  111 us
    reduce_scatter x1, waiting for transfers between devices, body(): lax.psum_scatter(partial_sums[2], ('dp', 'ctx'), scatter_dimension=0, til...  93.4 us
    dot_general x8, matrix products, step_back(): jnp.einsum('hrk,rhe->khe', attention_weights, grad_att, preferred_element...  72.8 us
    dot_general x8, matrix products, score_grads(): jnp.einsum('rhe,khe->hrk', grad_att, value_rows, preferred_element_type=j...  68.7 us
    all_gather x4, waiting for transfers between devices, layer_reverse_pass(): lax.all_gather(projected[:, D:2 * D], 'ctx', axis=0, tiled=True)  67.3 us
  transfers between devices with their start and end apart: 37, of which 17 were waited for; matrix products, arithmetic and copies ran while one was open for 58% of the time, Pallas kernels for 0%

commit v1 on v0

--- a/solution.py
+++ b/solution.py
@@ -1,11 +1,227 @@
+import functools
 import jax
 import jax.numpy as jnp
 from jax import lax
+from jax.experimental import pallas as pl
+from jax.experimental.pallas import tpu as pltpu
 from jax.sharding import PartitionSpec as P
 
 D = 768
 HEADS = 12
 HDIM = 64
+PAIR = 2 * HDIM
+PAIRS = HEADS // 2
+OWN = 4
+NT = (((1,), (1,)), ((), ()))
+TN = (((0,), (0,)), ((), ()))
+NN = (((1,), (0,)), ((), ()))
+
+
+def dot(left, right, dims):
+    return lax.dot_general(left, right, dims, preferred_element_type=jnp.float32)
+
+
+def slot_meta(own_pos, other_pos, signed):
+    ranked = jnp.argsort(own_pos).astype(jnp.int32)
+    return jnp.concatenate(
+        [own_pos, other_pos, ranked, own_pos[ranked], signed.astype(jnp.int32)[None]]
+    )
+
+
+def sort_rows(meta, own, other, target, span):
+    for slot in range(OWN):
+        for base, source in ((0, own), (OWN, other)):
+            start = pl.multiple_of(meta[base + slot] * span, span)
+            target[pl.ds(start, span), :] = source[slot * span : (slot + 1) * span, :]
+
+
+def reach(rank, slots):
+    return ((0, slots // 2 - 2), (1, slots // 2 - 1), (slots // 2, slots - 2), (slots // 2 + 1, slots - 1))[rank]
+
+
+def lane_is_second(shape):
+    return lax.broadcasted_iota(jnp.int32, shape, 1) >= HDIM
+
+
+def stacked_heads(rows):
+    second = lane_is_second(rows.shape)
+    zero = jnp.zeros_like(rows)
+    return jnp.concatenate([jnp.where(second, zero, rows), jnp.where(second, rows, zero)], axis=0)
+
+
+def masked_part(values, least, span, position, fill):
+    if least * span >= values.shape[0]:
+        return values
+    tail = values[least * span :]
+    key_at = lax.broadcasted_iota(jnp.int32, tail.shape, 0) + least * span
+    lane = lax.broadcasted_iota(jnp.int32, tail.shape, 1)
+    query_at = position * span + jnp.where(lane >= span, lane - span, lane)
+    tail = jnp.where(key_at <= query_at, tail, fill)
+    if least == 0:
+        return tail
+    return jnp.concatenate([values[: least * span], tail], axis=0)
+
+
+def unstack(pair, span):
+    row = lax.broadcasted_iota(jnp.int32, (PAIR, span), 0)
+    return jnp.where(row < HDIM, pair[:, :span], pair[:, span:]).T
+
+
+def forward_kernel(meta, q_ref, k_ref, v_ref, k2_ref, v2_ref, o_ref, lse_ref, keys, values, *, span):
+    slots = keys.shape[0] // span
+    sort_rows(meta, k_ref, k2_ref, keys, span)
+    sort_rows(meta, v_ref, v2_ref, values, span)
+
+    def run(signed):
+        for rank in reversed(range(OWN)):
+            least, most = reach(rank, slots)
+            count = (most + 1) * span
+            row_at = pl.multiple_of(meta[2 * OWN + rank] * span, span)
+            position = meta[3 * OWN + rank]
+            queries = stacked_heads(q_ref[pl.ds(row_at, span), :] * 0.125)
+            scores = dot(keys[:count, :], queries, NT)
+            if signed:
+                square = scores * scores + 1.0
+                inverse = lax.rsqrt(square)
+                argument = square * inverse
+                sign_pattern = scores * inverse
+            else:
+                argument = scores
+            argument = masked_part(argument, least, span, position, -1e30)
+            largest = jnp.max(argument, axis=0, keepdims=True)
+            weights = jnp.exp(argument - largest)
+            total = jnp.sum(weights, axis=0, keepdims=True)
+            lse_ref[0, rank : rank + 1, :] = largest + jnp.log(total)
+            if signed:
+                weights = weights * sign_pattern
+            gathered = dot(values[:count, :], weights.astype(jnp.bfloat16), TN)
+            gathered = gathered * (1.0 / total)
+            o_ref[pl.ds(row_at, span), :] = unstack(gathered, span).astype(jnp.bfloat16)
+
+    @pl.when(meta[4 * OWN] == 1)
+    def _():
+        run(True)
+
+    @pl.when(meta[4 * OWN] == 0)
+    def _():
+        run(False)
+
+
+def sorted_attend(meta, qkv, kv_other):
+    rows = qkv.shape[0]
+    span = rows // OWN
+    def spec(first):
+        return pl.BlockSpec((rows, PAIR), lambda h, _: (0, first + h))
+    return pl.pallas_call(
+        functools.partial(forward_kernel, span=span),
+        grid_spec=pltpu.PrefetchScalarGridSpec(
+            num_scalar_prefetch=1,
+            grid=(PAIRS,),
+            in_specs=[spec(0), spec(PAIRS), spec(2 * PAIRS), spec(0), spec(PAIRS)],
+            out_specs=[spec(0), pl.BlockSpec((1, OWN, 2 * span), lambda h, _: (h, 0, 0))],
+            scratch_shapes=[pltpu.VMEM((2 * rows, PAIR), jnp.bfloat16)] * 2,
+        ),
+        out_shape=[
+            jax.ShapeDtypeStruct((rows, D), jnp.bfloat16),
+            jax.ShapeDtypeStruct((PAIRS, OWN, 2 * span), jnp.float32),
+        ],
+        compiler_params=pltpu.CompilerParams(vmem_limit_bytes=40 * 1024 * 1024),
+        name="attend",
+    )(meta, qkv, qkv, qkv, kv_other, kv_other)
+
+
+def backward_kernel(
+    meta, q_ref, k_ref, v_ref, k2_ref, v2_ref, o_ref, do_ref, lse_ref,
+    dq_ref, own_ref, other_ref, keys, values, grad_k, grad_v, *, span,
+):
+    slots = keys.shape[0] // span
+    sort_rows(meta, k_ref, k2_ref, keys, span)
+    sort_rows(meta, v_ref, v2_ref, values, span)
+
+    def run(signed):
+        for rank in reversed(range(OWN)):
+            least, most = reach(rank, slots)
+            count = (most + 1) * span
+            row_at = pl.multiple_of(meta[2 * OWN + rank] * span, span)
+            position = meta[3 * OWN + rank]
+            queries = stacked_heads(q_ref[pl.ds(row_at, span), :] * 0.125)
+            grad_rows = do_ref[pl.ds(row_at, span), :]
+            grads = stacked_heads(grad_rows)
+            product = grad_rows.astype(jnp.float32) * o_ref[pl.ds(row_at, span), :].astype(jnp.float32)
+            product = stacked_heads(product)
+            delta = jnp.sum(product.T, axis=0, keepdims=True)
+            lse = lse_ref[0, rank : rank + 1, :]
+            scores = dot(keys[:count, :], queries, NT)
+            along = dot(values[:count, :], grads, NT)
+            if signed:
+                square = scores * scores + 1.0
+                inverse = lax.rsqrt(square)
+                argument = masked_part(square * inverse, least, span, position, -1e30)
+                prob = jnp.exp(argument - lse)
+                sign_pattern = scores * inverse
+                weights = prob * sign_pattern
+                dscore = prob * ((sign_pattern * along - delta) * sign_pattern + along * (inverse * inverse * inverse))
+            else:
+                argument = masked_part(scores, least, span, position, -1e30)
+                weights = jnp.exp(argument - lse)
+                dscore = weights * (along - delta)
+            weights = weights.astype(jnp.bfloat16)
+            dscore = dscore.astype(jnp.bfloat16)
+            added_v = dot(weights, grads, NN)
+            added_k = dot(dscore, queries, NN)
+            if rank == OWN - 1:
+                grad_v[...] = added_v
+                grad_k[...] = added_k
+            else:
+                grad_v[:count, :] += added_v
+                grad_k[:count, :] += added_k
+            gathered = dot(keys[:count, :], dscore, TN)
+            dq_ref[pl.ds(row_at, span), :] = (unstack(gathered, span) * 0.125).astype(jnp.bfloat16)
+
+    @pl.when(meta[4 * OWN] == 1)
+    def _():
+        run(True)
+
+    @pl.when(meta[4 * OWN] == 0)
+    def _():
+        run(False)
+
+    for slot in range(OWN):
+        there = slice(slot * span, (slot + 1) * span)
+        own_at = pl.multiple_of(meta[slot] * span, span)
+        other_at = pl.multiple_of(meta[OWN + slot] * span, span)
+        for part, total in enumerate((grad_k, grad_v)):
+            own_ref[part, there, :] = total[pl.ds(own_at, span), :]
+            other_ref[part, there, :] = total[pl.ds(other_at, span), :].astype(jnp.bfloat16)
+
+
+def sorted_attend_back(meta, qkv, kv_other, attended, grad_att, lse):
+    rows = qkv.shape[0]
+    span = rows // OWN
+    def spec(first):
+        return pl.BlockSpec((rows, PAIR), lambda h, _: (0, first + h))
+    two = pl.BlockSpec((2, rows, PAIR), lambda h, _: (0, 0, h))
+    return pl.pallas_call(
+        functools.partial(backward_kernel, span=span),
+        grid_spec=pltpu.PrefetchScalarGridSpec(
+            num_scalar_prefetch=1,
+            grid=(PAIRS,),
+            in_specs=[
+                spec(0), spec(PAIRS), spec(2 * PAIRS), spec(0), spec(PAIRS), spec(0), spec(0),
+                pl.BlockSpec((1, OWN, 2 * span), lambda h, _: (h, 0, 0)),
+            ],
+            out_specs=[spec(0), two, two],
+            scratch_shapes=[pltpu.VMEM((2 * rows, PAIR), jnp.bfloat16)] * 2
+            + [pltpu.VMEM((2 * rows, PAIR), jnp.float32)] * 2,
+        ),
+        out_shape=[
+            jax.ShapeDtypeStruct((rows, D), jnp.bfloat16),
+            jax.ShapeDtypeStruct((2, rows, D), jnp.float32),
+            jax.ShapeDtypeStruct((2, rows, D), jnp.bfloat16),
+        ],
+        compiler_params=pltpu.CompilerParams(vmem_limit_bytes=48 * 1024 * 1024),
+        name="attend_back",
+    )(meta, qkv, qkv, qkv, kv_other, kv_other, attended, grad_att, lse)
 
 
 def shifted(value, axis, steps):
@@ -171,7 +387,7 @@
     return (middle, normed_two, hidden, active, result)
 
 
-def body(inputs, slot_order, cotangent, gains, biases, w_qkv, w_out, w_up, w_down):
+def general_body(inputs, slot_order, cotangent, gains, biases, w_qkv, w_out, w_up, w_down):
     micro_count = inputs.shape[0]
     row_count = inputs.shape[2]
     section_at = lax.axis_index("section")
@@ -363,6 +579,200 @@
     )
 
 
+def norm_parts(rows):
+    center = rows - jnp.mean(rows, axis=-1, keepdims=True)
+    spread = jnp.mean(center * center, axis=-1, keepdims=True)
+    inverse = lax.rsqrt(spread + 1e-05)
+    return center * inverse, inverse
+
+
+def norm_back(unit, inverse, gain_row, grad):
+    scaled = grad * gain_row
+    along = jnp.mean(scaled * unit, axis=-1, keepdims=True)
+    grad_rows = inverse * (scaled - jnp.mean(scaled, axis=-1, keepdims=True) - unit * along)
+    return grad_rows, jnp.sum(grad * unit, axis=0), jnp.sum(grad, axis=0)
+
+
+def product(left, right):
+    return jnp.dot(left, right, preferred_element_type=jnp.float32)
+
+
+def product_nt(left, right):
+    return dot(left, right, NT)
+
+
+def product_tn(left, right):
+    return dot(left, right, TN)
+
+
+def swap_halves(value):
+    count = lax.axis_size("ctx")
+    return lax.ppermute(value, "ctx", [(at, (at + count // 2) % count) for at in range(count)])
+
+
+def swap_cores(value):
+    return lax.ppermute(value, "ctx", [(at, at ^ 1) for at in range(lax.axis_size("ctx"))])
+
+
+def scattered_sum(partial):
+    z_count = lax.axis_size("dp")
+    z_at = lax.axis_index("dp")
+    ctx_at = lax.axis_index("ctx")
+    y_at, core_at = ctx_at // 2, ctx_at % 2
+    width = partial.shape[1]
+    block = partial.shape[0] // (4 * z_count)
+    parts = partial.reshape(z_count, 2, 2, block, width)
+
+    def halves(values, at, axis, exchange):
+        sent = lax.dynamic_index_in_dim(values, 1 - at, axis, keepdims=False)
+        kept = lax.dynamic_index_in_dim(values, at, axis, keepdims=False)
+        arrived = exchange(sent)
+        return kept.astype(jnp.float32) + arrived.astype(jnp.float32)
+
+    parts = halves(parts, core_at, 2, swap_cores).astype(jnp.bfloat16)
+    parts = halves(parts, y_at, 1, swap_halves).astype(jnp.bfloat16)
+    total = lax.dynamic_index_in_dim(parts, z_at, 0, keepdims=False).astype(jnp.float32)
+    for step in range(1, z_count):
+        for way in (step, -step):
+            target = jnp.clip(z_at + way, 0, z_count - 1)
+            sent = lax.dynamic_index_in_dim(parts, target, 0, keepdims=False)
+            moves = [(at, at + way) for at in range(z_count) if 0 <= at + way < z_count]
+            total = total + lax.ppermute(sent, "dp", moves).astype(jnp.float32)
+    return total
+
+
+def split_rows(vector, blocks):
+    return vector.reshape(*vector.shape[:-1], blocks, vector.shape[-1] // blocks)
+
+
+def fast_body(inputs, slot_order, cotangent, gains, biases, w_qkv, w_out, w_up, w_down):
+    rows = inputs.shape[2]
+    count = lax.axis_size("ctx")
+    half = count // 2
+    section_at = lax.axis_index("section")
+    ctx_at = lax.axis_index("ctx")
+    mine = ctx_at // half
+    signed = section_at == 0
+    gain_pair, bias_row = gains[0], biases[0]
+    qkv_w, out_w, up_w, down_w = w_qkv[0], w_out[0], w_up[0], w_down[0]
+    shift_one, shift_two = bias_row[:D], bias_row[D : 2 * D]
+    qkv_bias = jnp.concatenate(
+        [bias_row[2 * D : 3 * D], jnp.zeros((D,), jnp.float32), bias_row[3 * D : 4 * D]]
+    )
+    out_bias, down_bias, up_bias = bias_row[4 * D : 5 * D], bias_row[5 * D : 6 * D], bias_row[6 * D :]
+
+    def gathered(value):
+        kept = lax.dynamic_index_in_dim(value, mine, 0, keepdims=False)
+        sent = lax.dynamic_index_in_dim(value, 1 - mine, 0, keepdims=False)
+        return jnp.concatenate([kept, swap_halves(sent)], axis=0)
+
+    def returned(value):
+        kept, sent = value[:rows], value[rows:]
+        arrived = swap_halves(sent.astype(jnp.bfloat16)).astype(value.dtype)
+        first = jnp.where(mine == 0, kept, arrived)
+        second = jnp.where(mine == 0, arrived, kept)
+        return jnp.stack([first, second])
+
+    order = lax.dynamic_index_in_dim(slot_order[:, 0], mine, 0, keepdims=False)
+    pairs = order.reshape(count, 2)
+
+    def slots_of(device):
+        partner = (device + half) % count
+        return jnp.concatenate([pairs[device], pairs[partner]])
+
+    meta = slot_meta(slots_of(ctx_at), slots_of(ctx_at ^ 1), signed)
+
+    def forward(entry):
+        rows_in = entry.astype(jnp.float32)
+        unit_one, inverse_one = norm_parts(rows_in)
+        normed = (unit_one * gain_pair[0] + shift_one).astype(jnp.bfloat16)
+        qkv = (product(normed, qkv_w) + qkv_bias).astype(jnp.bfloat16)
+        kv_other = swap_cores(qkv[:, D:])
+        attended, lse = sorted_attend(meta, qkv, kv_other)
+        middle = rows_in + product(attended, out_w) + out_bias
+        unit_two, inverse_two = norm_parts(middle)
+        normed_two = (unit_two * gain_pair[1] + shift_two).astype(jnp.bfloat16)
+        hidden = product(normed_two, up_w) + up_bias
+        active, gelu_back = jax.vjp(gelu_tanh, hidden)
+        active = active.astype(jnp.bfloat16)
+        slope = gelu_back(jnp.ones_like(hidden))[0].astype(jnp.bfloat16)
+        result = (middle + product(active, down_w) + down_bias).astype(jnp.bfloat16)
+        return result, (rows_in, normed, qkv, kv_other, attended, lse, middle, normed_two, active, slope)
+
+    def backward(kept, result_gradient, whole):
+        rows_in, normed, qkv, kv_other, attended, lse, middle, normed_two, active, slope = kept
+        grad_hidden = product_nt(result_gradient, down_w) * slope.astype(jnp.float32)
+        grad_hidden_b = grad_hidden.astype(jnp.bfloat16)
+        unit_two, inverse_two = norm_parts(middle)
+        through_two, gain_two, offset_two = norm_back(
+            unit_two, inverse_two, gain_pair[1], product_nt(grad_hidden_b, up_w)
+        )
+        grad_middle = result_gradient.astype(jnp.float32) + through_two
+        grad_middle_b = grad_middle.astype(jnp.bfloat16)
+        grad_att = product_nt(grad_middle_b, out_w).astype(jnp.bfloat16)
+        grad_q, grad_own, grad_other = sorted_attend_back(meta, qkv, kv_other, attended, grad_att, lse)
+        grad_kv = (grad_own + swap_cores(grad_other).astype(jnp.float32)).astype(jnp.bfloat16)
+        grad_qkv = jnp.concatenate([grad_q, grad_kv[0], grad_kv[1]], axis=1)
+        unit_one, inverse_one = norm_parts(rows_in)
+        through_one, gain_one, offset_one = norm_back(
+            unit_one, inverse_one, gain_pair[0], product_nt(grad_qkv, qkv_w)
+        )
+        input_gradient = grad_middle + through_one
+        if not whole:
+            return input_gradient
+        narrow = jnp.bfloat16
+        grad_wdown = product_tn(active, result_gradient).astype(narrow)
+        grad_wup = product_tn(normed_two, grad_hidden_b).astype(narrow)
+        grad_wout = product_tn(attended, grad_middle_b).astype(narrow)
+        grad_wqkv = product_tn(normed, grad_qkv).astype(narrow)
+        bias_terms = [
+            offset_one, offset_two,
+            jnp.sum(grad_q.astype(jnp.float32), axis=0),
+            jnp.sum(grad_kv[1].astype(jnp.float32), axis=0),
+            jnp.sum(grad_middle, axis=0),
+            jnp.sum(result_gradient.astype(jnp.float32), axis=0),
+            jnp.sum(grad_hidden, axis=0),
+        ]
+        return input_gradient, (grad_wdown, grad_wup, grad_wout, grad_wqkv), (jnp.stack([gain_one, gain_two]), jnp.concatenate(bias_terms))
+
+    first = gathered(inputs[:, 0])
+    given = gathered(cotangent[:, 0])
+    sent, _ = forward(first)
+    entry = jnp.where(signed, first, shifted(sent, "section", 1))
+    result, kept = forward(entry)
+    acts_rows = returned(result)
+    handed = backward(kept, given, False).astype(jnp.bfloat16)
+    result_gradient = jnp.where(signed, shifted(handed, "section", -1), given)
+    input_gradient, weights, small = backward(kept, result_gradient, True)
+    input_gradient = jnp.where(signed, input_gradient, input_gradient.astype(jnp.bfloat16).astype(jnp.float32))
+    grad_rows = returned(input_gradient)
+    wdown, wup, wout, wqkv = [scattered_sum(part) for part in weights]
+    blocks = count * lax.axis_size("dp")
+    gain_terms, bias_terms = small
+    packed = jnp.concatenate([split_rows(gain_terms[0], blocks), split_rows(gain_terms[1], blocks), split_rows(bias_terms, blocks)], axis=1)
+    coarse = packed.astype(jnp.bfloat16)
+    fine = (packed - coarse.astype(jnp.float32)).astype(jnp.bfloat16)
+    packed = scattered_sum(jnp.concatenate([coarse, fine], axis=1))
+    width = packed.shape[1] // 2
+    packed = packed[0, :width] + packed[0, width:]
+    piece = D // blocks
+    return (
+        acts_rows[None, :, None],
+        grad_rows[None, :, None],
+        jnp.stack([packed[:piece], packed[piece : 2 * piece]])[None],
+        packed[2 * piece :][None],
+        wqkv[None],
+        wout[None],
+        wup[None],
+        wdown[None],
+    )
+
+
+def body_for(mesh):
+    shape = dict(mesh.shape)
+    return fast_body if shape["ctx"] == 4 else general_body
+
+
 def solution(mesh):
     in_specs = (
         P(None, "dp", "ctx", None),
@@ -385,4 +795,6 @@
         P("section", ("dp", "ctx"), None),
         P("section", ("dp", "ctx"), None),
     )
-    return jax.shard_map(body, mesh=mesh, in_specs=in_specs, out_specs=out_specs, check_vma=False)
+    return jax.shard_map(
+        body_for(mesh), mesh=mesh, in_specs=in_specs, out_specs=out_specs, check_vma=False
+    )

time: 1640 us -> 480 us (0.29)
  matrix products: 636 us -> 75.9 us
  waiting for transfers between devices: 501 us -> 127 us
  local copies, waits for them, and re-layouts: 249 us -> 49.7 us
  other arithmetic: 126 us -> 29.4 us
  starting transfers between devices: 25.2 us -> 112 us
  Pallas kernels: 0 us -> 79.8 us
  blocking collectives: 59.9 us -> 0 us
    dot_general x128 -> x20, matrix products: 636 us -> 75.9 us  [the longest x12 49.7 us: dot(): lax.dot_general(left, right, dims, preferred_element_type=jnp.float32)]
    reduce_scatter x12 -> x0, waiting for transfers between devices: 388 us -> none  [the longest x1 117 us: body(): lax.psum_scatter(partial_sums[4], ('dp', 'ctx'), scatter_dimension=0, til...]
    ppermute x0 -> x48, starting transfers between devices: none -> 109 us  [the longest x30 97.3 us: scattered_sum(): total = total + lax.ppermute(sent, 'dp', moves).astype(jnp.float32)]
    ppermute x0 -> x48, waiting for transfers between devices: none -> 93.6 us  [the longest x9 74.9 us: swap_halves(): lax.ppermute(value, 'ctx', [(at, (at + count // 2) % count) for at in ran...]
    reduce_sum x60 -> x10, other arithmetic: 90 us -> 6.02 us  [the longest x1 2.13 us: backward(): jnp.sum(result_gradient.astype(jnp.float32), axis=0)]
    all_gather x16 -> x0, waiting for transfers between devices: 83.8 us -> none  [the longest x4 67.3 us: layer_reverse_pass(): lax.all_gather(projected[:, D:2 * D], 'ctx', axis=0, tiled=True)]
    pallas_call x0 -> x4, Pallas kernels: none -> 79.8 us  [the longest x2 44.7 us: sorted_attend_back(): pl.pallas_call(functools.partial(backward_kernel, span=span), grid_spec=p...]
    dynamic_update_slice x28 -> x0, local copies, waits for them, and re-layouts: 60.8 us -> none  [the longest x24 57.5 us: backward_summed(): lax.scan(step_back, start_q, (key_split, value_split, pos_split))]
  transfers between devices with their start and end apart: 37 -> 50, of which waited for: 17 -> 14; matrix products, arithmetic and copies ran while one was open for 58% -> 18% of each run, Pallas kernels for 0% -> 8%
where the time goes in v1:
time: 480 us; the launch traced here: 476 us
  waiting for transfers between devices  127 us (26%)
  starting transfers between devices  112 us (23%)
  Pallas kernels  79.8 us (17%)
  matrix products  75.9 us (16%)
  local copies, waits for them, and re-layouts  49.7 us (10%)
  other arithmetic  29.4 us (6%)
    ppermute x30, starting transfers between devices, scattered_sum(): total = total + lax.ppermute(sent, 'dp', moves).astype(jnp.float32)  97.3 us
    ppermute x9, waiting for transfers between devices, swap_halves(): lax.ppermute(value, 'ctx', [(at, (at + count // 2) % count) for at in ran...  74.9 us
    dot_general x12, matrix products, dot(): lax.dot_general(left, right, dims, preferred_element_type=jnp.float32)  49.7 us
    pallas_call x2, Pallas kernels, sorted_attend_back(): pl.pallas_call(functools.partial(backward_kernel, span=span), grid_spec=p...  44.7 us
    pallas_call x2, Pallas kernels, sorted_attend(): pl.pallas_call(functools.partial(forward_kernel, span=span), grid_spec=pl...  35 us
    ppermute x2, waiting for transfers between devices, shifted(): lax.ppermute(value, axis, [(source, source + steps) for source in range(i...  33 us
    dot_general x8, matrix products, product(): return jnp.dot(left, right, preferred_element_type=jnp.float32)  26.2 us
    unnamed x178, local copies, waits for them, and re-layouts  20.5 us
  transfers between devices with their start and end apart: 50, of which 14 were waited for; matrix products, arithmetic and copies ran while one was open for 18% of the time, Pallas kernels for 8%

profile of v1, /device:TPU:0, one launch (start us, length us, event | category | flops | bytes accessed | tf_op | source)
XLA Modules:
  0.0 475.7 jit_solution(7366337571821967982)
XLA Ops:
  2.0 3.0 collective-permute-start
  5.8 8.4 %collective-permute-done = bf16[256,768]{1,0:T(8,128)(2,1)S(1)} collective-permute-done((bf16[256,768]{1,0:T(8,128)(2,1)S(1)}, bf16[256,768]{1,0:T(8,128)(2,1)S(1)}, u32[]{:S(2)}, u32[]{:S(2)}) %collective-permute-start) | collective-permute-done | bytes 393248 | tf_op jit(solution)/shard_map/ppermute | solution.py:610
  28.5 18.2 %attend.2 = (bf16[512,768]{1,0:T(8,128)(2,1)S(1)}, f32[6,4,256]{2,1,0:T(4,128)}) custom-call(s32[17]{0:T(128)S(1)} %concatenate.57.meta, bf16[512,2304]{1,0:T(8,128)(2,1)S(1)} %copy-done.5, bf16[512,2304]{1,0:T(8,128)(2,1)S(1)} %copy-done.5, bf16[512,2304]{1,0:T(8,128)(2,1)S(1)} %copy-done.5, bf16[512,1536]{1,0:T(8,128)(2,1)} %collective-permute-done.1.k2_ref.v2_ref, ...), custom_call_target="tpu_custom_call" | custom-call | tf_op jit(solution)/shard_map/attend/pallas_call | solution.py:115
  49.0 4.5 fusion.15
  53.6 2.6 add_convert_fusion.4
  57.6 17.7 %collective-permute-done.2 = bf16[512,768]{1,0:T(8,128)(2,1)S(1)} collective-permute-done((bf16[512,768]{1,0:T(8,128)(2,1)S(1)}, bf16[512,768]{1,0:T(8,128)(2,1)S(1)}, u32[]{:S(2)}, u32[]{:S(2)}) %collective-permute-start.2) | collective-permute-done | bytes 786464 | tf_op jit(solution)/shard_map/ppermute | solution.py:230
  81.8 16.9 %attend.3 = (bf16[512,768]{1,0:T(8,128)(2,1)S(1)}, f32[6,4,256]{2,1,0:T(4,128)S(1)}) custom-call(s32[17]{0:T(128)S(1)} %concatenate.57.meta, bf16[512,2304]{1,0:T(8,128)(2,1)S(1)} %fusion.33.q_ref.k_ref.v_ref, bf16[512,2304]{1,0:T(8,128)(2,1)S(1)} %fusion.33.q_ref.k_ref.v_ref, bf16[512,2304]{1,0:T(8,128)(2,1)S(1)} %fusion.33.q_ref.k_ref.v_ref, ...), custom_call_target="tpu_custom_call" | custom-call | tf_op jit(solution)/shard_map/attend/pallas_call | solution.py:115
  100.2 4.8 %fusion.28 = f32[512,3072]{1,0:T(8,128)S(1)} fusion(bf16[1,768,3072]{2,1,0:T(8,128)(2,1)} %param.16, f32[768]{0:T(1024)S(1)} %copy-done.65, f32[768]{0:T(1024)S(1)} %copy-done.51, f32[512,768]{1,0:T(8,128)S(1)} %get-tuple-element.131, f32[512]{0:T(512)S(1)} %add_rsqrt_fusion, f32[512]{0:T(512)S(1)} %broadcast_multiply_fusion.8), kind=kOutput, calls=%fused_computation.42 | convolution fusion | flops 2417885184 | bytes 12593152 | tf_op jit(solution)/shard_map/dot_general | solution.py:597
  105.1 6.8 %fusion = bf16[512,3072]{1,0:T(8,128)(2,1)} fusion(bf16[1,3072,768]{2,1,0:T(8,128)(2,1)S(1)} %bitcast.285, bf16[256,768]{1,0:T(8,128)(2,1)S(1)} %collective-permute-done.5, bf16[256,768]{1,0:T(8,128)(2,1)S(1)} %get-tuple-element.106, f32[512,3072]{1,0:T(8,128)S(1)} %fusion.28, f32[3072]{0:T(1024)S(1)} %bitcast.280), kind=kOutput, calls=%fused_computation.6 | convolution fusion | flops 2452094976 | bytes 14954496 | tf_op jit(solution)/shard_map/dot_general | solution.py:21
  111.9 4.7 fusion.166
  117.8 22.5 %attend_back.2 = (bf16[512,768]{1,0:T(8,128)(2,1)S(1)}, f32[2,512,768]{2,1,0:T(8,128)}, bf16[2,512,768]{2,1,0:T(8,128)(2,1)S(1)}) custom-call(s32[17]{0:T(128)S(1)} %concatenate.57.meta, bf16[512,2304]{1,0:T(8,128)(2,1)} %copy-done.1, bf16[512,2304]{1,0:T(8,128)(2,1)} %copy-done.1, bf16[512,2304]{1,0:T(8,128)(2,1)} %copy-done.1, ...), custom_call_target="tpu_custom_call" | custom-call | tf_op jit(solution)/shard_map/attend_back/pallas_call | solution.py:204
  140.4 8.2 %add_convert_fusion.2 = bf16[512,768]{1,0:T(8,128)(2,1)S(1)} fusion(f32[512,768]{1,0:T(8,128)S(1)} %get-tuple-element.131, bf16[1,3072,768]{2,1,0:T(8,128)(2,1)} %param.17, f32[768]{0:T(1024)S(1)} %copy-done.67, f32[512,3072]{1,0:T(8,128)} %copy-done.78, f32[3072]{0:T(1024)S(1)} %bitcast.281), kind=kOutput, calls=%fused_computation.123 | convolution fusion | flops 2432827392 | bytes 13384704 | tf_op jit(solution)/shard_map/dot_general | solution.py:597
  158.4 2.8 collective-permute-done.4
  163.3 15.3 %collective-permute-done.7 = bf16[512,768]{1,0:T(8,128)(2,1)} collective-permute-done((bf16[512,768]{1,0:T(8,128)(2,1)}, bf16[512,768]{1,0:T(8,128)(2,1)}, u32[]{:S(2)}, u32[]{:S(2)}) %collective-permute-start.7) | collective-permute-done | bytes 786464 | tf_op jit(solution)/shard_map/ppermute | solution.py:230
  180.7 9.5 %fusion.172 = (f32[3072]{0:T(1024)}, bf16[512,3072]{1,0:T(8,128)(2,1)S(1)}) fusion(f32[512,3072]{1,0:T(8,128)} %copy-done.78, f32[3072]{0:T(1024)S(1)} %bitcast.282, bf16[512,768]{1,0:T(8,128)(2,1)S(1)} %get-tuple-element.67, bf16[1,3072,768]{2,1,0:T(8,128)(2,1)} %param.17), kind=kOutput, calls=%fused_computation.333 | convolution fusion | flops 2452091904 | bytes 14966784 | tf_op jit(solution)/shard_map/dot_general | solution.py:21
  190.3 4.2 convolution_convert_fusion
  194.5 5.9 %multiply_reduce_fusion = (f32[768]{0:T(1024)}, f32[512]{0:T(512)S(1)}, f32[512]{0:T(512)S(1)}, f32[768]{0:T(1024)}, f32[512,768]{1,0:T(8,128)S(1)}) fusion(f32[512]{0:T(512)S(1)} %add_rsqrt_fusion, f32[512,768]{1,0:T(8,128)S(1)} %copy-done.15, f32[512]{0:T(512)S(1)} %broadcast_multiply_fusion.8, f32[768]{0:T(1024)S(1)} %copy-done.52, ...), kind=kOutput, calls=%fused_computation.116 | convolution fusion | flops 2419455488 | bytes 11027456 | tf_op jit(solution)/shard_map/dot_general | solution.py:21
  205.8 22.2 %attend_back.3 = (bf16[512,768]{1,0:T(8,128)(2,1)S(1)}, f32[2,512,768]{2,1,0:T(8,128)}, bf16[2,512,768]{2,1,0:T(8,128)(2,1)}) custom-call(s32[17]{0:T(128)S(1)} %concatenate.57.meta, bf16[512,2304]{1,0:T(8,128)(2,1)} %copy-done.1, bf16[512,2304]{1,0:T(8,128)(2,1)} %copy-done.1, bf16[512,2304]{1,0:T(8,128)(2,1)} %copy-done.1, ...), custom_call_target="tpu_custom_call" | custom-call | tf_op jit(solution)/shard_map/attend_back/pallas_call | solution.py:204
  228.0 5.3 %convolution_convert_fusion.1 = bf16[768,3072]{1,0:T(8,128)(2,1)S(1)} fusion(bf16[512,3072]{1,0:T(8,128)(2,1)} %copy-done.79, f32[768]{0:T(1024)S(1)} %copy-done.66, f32[768]{0:T(1024)S(1)} %copy-done.52, f32[512,768]{1,0:T(8,128)S(1)} %copy-done.15, f32[512]{0:T(512)S(1)} %add_rsqrt_fusion, f32[512]{0:T(512)S(1)} %broadcast_multiply_fusion.8), kind=kOutput, calls=%fused_computation.24 | convolution fusion | flops 2420244480 | bytes 9447424 | tf_op jit(solution)/shard_map/dot_general | solution.py:21
  236.5 6.3 %collective-permute-done.27 = bf16[4,48,768]{2,1,0:T(8,128)(2,1)S(1)} collective-permute-done((bf16[4,48,768]{2,1,0:T(8,128)(2,1)S(1)}, bf16[4,48,768]{2,1,0:T(8,128)(2,1)S(1)}, u32[]{:S(2)}, u32[]{:S(2)}) %collective-permute-start.27) | collective-permute-done | bytes 294944 | tf_op jit(solution)/shard_map/ppermute | solution.py:610
  243.7 3.5 collective-permute-start.28
  248.5 2.7 constant_dynamic-slice_fusion.1
  251.2 7.0 %collective-permute-start.32 = (bf16[48,768]{1,0:T(8,128)(2,1)}, bf16[48,768]{1,0:T(8,128)(2,1)}, u32[]{:S(2)}, u32[]{:S(2)}) collective-permute-start(bf16[48,768]{1,0:T(8,128)(2,1)} %get-tuple-element.112), channel_id=1, source_target_pairs={{0,12},{1,13},{2,14},{3,15},{16,28},{17,29},{18,30},{19,31}} | collective-permute-start | bytes 221192 | tf_op jit(solution)/shard_map/ppermute | solution.py:640
  259.4 6.7 %collective-permute-start.30 = (bf16[48,768]{1,0:T(8,128)(2,1)}, bf16[48,768]{1,0:T(8,128)(2,1)}, u32[]{:S(2)}, u32[]{:S(2)}) collective-permute-start(bf16[48,768]{1,0:T(8,128)(2,1)} %get-tuple-element.114), channel_id=1, source_target_pairs={{0,8},{4,12},{1,9},{5,13},{2,10},{6,14},{3,11},{7,15},{16,24},{20,... | collective-permute-start | bytes 221192 | tf_op jit(solution)/shard_map/ppermute | solution.py:640
  268.3 3.5 copy.58
  279.0 4.3 fusion.72
  283.3 4.0 convolution_convert_fusion.2
  303.7 3.2 collective-permute-done.11
  307.0 4.6 collective-permute-start.12
  312.9 6.3 %collective-permute-start.16 = (bf16[1,1152]{1,0:T(2,128)(2,1)S(1)}, bf16[1,1152]{1,0:T(2,128)(2,1)S(1)}, u32[]{:S(2)}, u32[]{:S(2)}) collective-permute-start(bf16[1,1152]{1,0:T(2,128)(2,1)S(1)} %get-tuple-element.118), channel_id=1, source_target_pairs={{0,12},{1,13},{2,14},{3,15},{16,28},{17,29},{18,30},{19,31}} | collective-permute-start | bytes 6920 | tf_op jit(solution)/shard_map/ppermute | solution.py:640
  320.6 5.4 %collective-permute-start.14 = (bf16[1,1152]{1,0:T(2,128)(2,1)S(1)}, bf16[1,1152]{1,0:T(2,128)(2,1)S(1)}, u32[]{:S(2)}, u32[]{:S(2)}) collective-permute-start(bf16[1,1152]{1,0:T(2,128)(2,1)S(1)} %get-tuple-element.120), channel_id=1, source_target_pairs={{0,8},{4,12},{1,9},{5,13},{2,10},{6,14},{3,11},{7,15},{16,24},{20,... | collective-permute-start | bytes 6920 | tf_op jit(solution)/shard_map/ppermute | solution.py:640
  328.7 2.9 collective-permute-done.13
  332.9 4.1 collective-permute-done.9
  343.3 2.6 fusion.17
  348.7 22.1 %collective-permute-done.43 = bf16[4,192,768]{2,1,0:T(8,128)(2,1)S(1)} collective-permute-done((bf16[4,192,768]{2,1,0:T(8,128)(2,1)S(1)}, bf16[4,192,768]{2,1,0:T(8,128)(2,1)S(1)}, u32[]{:S(2)}, u32[]{:S(2)}) %collective-permute-start.43) | collective-permute-done | bytes 1179680 | tf_op jit(solution)/shard_map/ppermute | solution.py:610
  371.2 4.3 collective-permute-start.44
  376.7 19.3 %collective-permute-done.35 = bf16[4,48,3072]{2,1,0:T(8,128)(2,1)S(1)} collective-permute-done((bf16[4,48,3072]{2,1,0:T(8,128)(2,1)S(1)}, bf16[4,48,3072]{2,1,0:T(8,128)(2,1)S(1)}, u32[]{:S(2)}, u32[]{:S(2)}) %collective-permute-start.35) | collective-permute-done | bytes 1179680 | tf_op jit(solution)/shard_map/ppermute | solution.py:610
  396.6 4.3 collective-permute-start.36
  402.1 8.8 %collective-permute-done.19 = bf16[4,48,2304]{2,1,0:T(8,128)(2,1)S(1)} collective-permute-done((bf16[4,48,2304]{2,1,0:T(8,128)(2,1)S(1)}, bf16[4,48,2304]{2,1,0:T(8,128)(2,1)S(1)}, u32[]{:S(2)}, u32[]{:S(2)}) %collective-permute-start.19) | collective-permute-done | bytes 884768 | tf_op jit(solution)/shard_map/ppermute | solution.py:610
  410.9 3.4 collective-permute-start.40
  415.9 5.5 %collective-permute-start.38 = (bf16[48,3072]{1,0:T(8,128)(2,1)S(1)}, bf16[48,3072]{1,0:T(8,128)(2,1)S(1)}, u32[]{:S(2)}, u32[]{:S(2)}) collective-permute-start(bf16[48,3072]{1,0:T(8,128)(2,1)S(1)} %get-tuple-element.94), channel_id=1, source_target_pairs={{0,8},{4,12},{1,9},{5,13},{2,10},{6,14},{3,11},{7,15},{16,24},{20,... | collective-permute-start | bytes 884744 | tf_op jit(solution)/shard_map/ppermute | solution.py:640
  422.8 3.4 collective-permute-start.48
  427.5 8.5 %collective-permute-done.39 = bf16[48,3072]{1,0:T(8,128)(2,1)S(1)} collective-permute-done((bf16[48,3072]{1,0:T(8,128)(2,1)S(1)}, bf16[48,3072]{1,0:T(8,128)(2,1)S(1)}, u32[]{:S(2)}, u32[]{:S(2)}) %collective-permute-start.39) | collective-permute-done | bytes 294944 | tf_op jit(solution)/shard_map/ppermute | solution.py:640
  438.7 10.6 %collective-permute-start.20 = (bf16[48,2304]{1,0:T(8,128)(2,1)S(1)}, bf16[48,2304]{1,0:T(8,128)(2,1)S(1)}, u32[]{:S(2)}, u32[]{:S(2)}) collective-permute-start(bf16[48,2304]{1,0:T(8,128)(2,1)S(1)} %get-tuple-element.100), channel_id=1, source_target_pairs={{0,4},{4,8},{8,12},{1,5},{5,9},{9,13},{2,6},{6,10},{10,14},{3,7},{... | collective-permute-start | bytes 663560 | tf_op jit(solution)/shard_map/ppermute | solution.py:640
  451.6 6.4 %collective-permute-start.24 = (bf16[48,2304]{1,0:T(8,128)(2,1)S(1)}, bf16[48,2304]{1,0:T(8,128)(2,1)S(1)}, u32[]{:S(2)}, u32[]{:S(2)}) collective-permute-start(bf16[48,2304]{1,0:T(8,128)(2,1)S(1)} %get-tuple-element.102), channel_id=1, source_target_pairs={{0,12},{1,13},{2,14},{3,15},{16,28},{17,29},{18,30},{19,31}} | collective-permute-start | bytes 663560 | tf_op jit(solution)/shard_map/ppermute | solution.py:640
  459.3 5.5 %collective-permute-start.22 = (bf16[48,2304]{1,0:T(8,128)(2,1)S(1)}, bf16[48,2304]{1,0:T(8,128)(2,1)S(1)}, u32[]{:S(2)}, u32[]{:S(2)}) collective-permute-start(bf16[48,2304]{1,0:T(8,128)(2,1)S(1)} %get-tuple-element.104), channel_id=1, source_target_pairs={{0,8},{4,12},{1,9},{5,13},{2,10},{6,14},{3,11},{7,15},{16,24},{20,... | collective-permute-start | bytes 663560 | tf_op jit(solution)/shard_map/ppermute | solution.py:640
  467.2 2.6 collective-permute-done.23
  469.8 4.6 collective-permute-done.21
  (358 shorter events, 113.7 us)
Async XLA Ops:
  2.0 12.1 %collective-permute-start = (bf16[256,768]{1,0:T(8,128)(2,1)S(1)}, bf16[256,768]{1,0:T(8,128)(2,1)S(1)}, u32[]{:S(2)}, u32[]{:S(2)}) collective-permute-start(bf16[256,768]{1,0:T(8,128)(2,1)S(1)} %get-tuple-element.109), channel_id=1, source_target_pairs={{0,2},{1,3},{2,0},{3,1},{4,6},{5,7},{6,4},{7,5},{8,10},{9,11},{10,... | collective-permute-start | bytes 1179656 | tf_op jit(solution)/shard_map/ppermute | solution.py:610
  19.6 7.2 %collective-permute-start.1 = (bf16[512,1536]{1,0:T(8,128)(2,1)}, bf16[512,1536]{1,0:T(8,128)(2,1)}, u32[]{:S(2)}, u32[]{:S(2)}) collective-permute-start(bf16[512,1536]{1,0:T(8,128)(2,1)} %slice.124), channel_id=1, source_target_pairs={{0,1},{1,0},{2,3},{3,2},{4,5},{5,4},{6,7},{7,6},{8,9},{9,8},{10,11... | collective-permute-start | bytes 4718600 | tf_op jit(solution)/shard_map/ppermute | solution.py:614
  56.2 19.0 %collective-permute-start.2 = (bf16[512,768]{1,0:T(8,128)(2,1)S(1)}, bf16[512,768]{1,0:T(8,128)(2,1)S(1)}, u32[]{:S(2)}, u32[]{:S(2)}) collective-permute-start(bf16[512,768]{1,0:T(8,128)(2,1)S(1)} %add_convert_fusion.4), channel_id=1, source_target_pairs={{0,16},{1,17},{2,18},{3,19},{4,20},{5,21},{6,22},{7,23},{8,24},{9,... | collective-permute-start | bytes 2359304 | tf_op jit(solution)/shard_map/ppermute | solution.py:230
  79.9 25.1 %collective-permute-start.5 = (bf16[256,768]{1,0:T(8,128)(2,1)S(1)}, bf16[256,768]{1,0:T(8,128)(2,1)S(1)}, u32[]{:S(2)}, u32[]{:S(2)}) collective-permute-start(bf16[256,768]{1,0:T(8,128)(2,1)S(1)} %get-tuple-element.107), channel_id=1, source_target_pairs={{0,2},{1,3},{2,0},{3,1},{4,6},{5,7},{6,4},{7,5},{8,10},{9,11},{10,... | collective-permute-start | bytes 1179656 | tf_op jit(solution)/shard_map/ppermute | solution.py:610
  140.3 11.0 %collective-permute-start.6 = (bf16[2,512,768]{2,1,0:T(8,128)(2,1)S(1)}, bf16[2,512,768]{2,1,0:T(8,128)(2,1)S(1)}, u32[]{:S(2)}, u32[]{:S(2)}) collective-permute-start(bf16[2,512,768]{2,1,0:T(8,128)(2,1)S(1)} %get-tuple-element.24), channel_id=1, source_target_pairs={{0,1},{1,0},{2,3},{3,2},{4,5},{5,4},{6,7},{7,6},{8,9},{9,8},{10,11... | collective-permute-start | bytes 4718600 | tf_op jit(solution)/shard_map/ppermute | solution.py:614
  149.5 11.7 %collective-permute-start.4 = (bf16[256,768]{1,0:T(8,128)(2,1)}, bf16[256,768]{1,0:T(8,128)(2,1)}, u32[]{:S(2)}, u32[]{:S(2)}) collective-permute-start(bf16[256,768]{1,0:T(8,128)(2,1)} %slice.127), channel_id=1, source_target_pairs={{0,2},{1,3},{2,0},{3,1},{4,6},{5,7},{6,4},{7,5},{8,10},{9,11},{10,... | collective-permute-start | bytes 1179656 | tf_op jit(solution)/shard_map/ppermute | solution.py:610
  156.9 21.7 %collective-permute-start.7 = (bf16[512,768]{1,0:T(8,128)(2,1)}, bf16[512,768]{1,0:T(8,128)(2,1)}, u32[]{:S(2)}, u32[]{:S(2)}) collective-permute-start(bf16[512,768]{1,0:T(8,128)(2,1)} %fusion.67), channel_id=1, source_target_pairs={{16,0},{17,1},{18,2},{19,3},{20,4},{21,5},{22,6},{23,7},{24,8},{25... | collective-permute-start | bytes 2359304 | tf_op jit(solution)/shard_map/ppermute | solution.py:230
  205.1 28.2 %collective-permute-start.26 = (bf16[4,2,48,768]{3,2,0,1:T(8,128)(2,1)}, bf16[4,2,48,768]{3,2,0,1:T(8,128)(2,1)S(1)}, u32[]{:S(2)}, u32[]{:S(2)}) collective-permute-start(bf16[4,2,48,768]{3,2,0,1:T(8,128)(2,1)} %bitcast.273), channel_id=1, source_target_pairs={{0,1},{1,0},{2,3},{3,2},{4,5},{5,4},{6,7},{7,6},{8,9},{9,8},{10,11... | collective-permute-start | bytes 1769480 | tf_op jit(solution)/shard_map/ppermute | solution.py:614
  228.0 47.6 %collective-permute-start.8 = (bf16[2,512,768]{2,1,0:T(8,128)(2,1)}, bf16[2,512,768]{2,1,0:T(8,128)(2,1)}, u32[]{:S(2)}, u32[]{:S(2)}) collective-permute-start(bf16[2,512,768]{2,1,0:T(8,128)(2,1)} %get-tuple-element.27), channel_id=1, source_target_pairs={{0,1},{1,0},{2,3},{3,2},{4,5},{5,4},{6,7},{7,6},{8,9},{9,8},{10,11... | collective-permute-start | bytes 4718600 | tf_op jit(solution)/shard_map/ppermute | solution.py:614
  233.6 9.2 %collective-permute-start.27 = (bf16[4,48,768]{2,1,0:T(8,128)(2,1)S(1)}, bf16[4,48,768]{2,1,0:T(8,128)(2,1)S(1)}, u32[]{:S(2)}, u32[]{:S(2)}) collective-permute-start(bf16[4,48,768]{2,1,0:T(8,128)(2,1)S(1)} %dynamic-slice_bitcast_fusion.19), channel_id=1, source_target_pairs={{0,2},{1,3},{2,0},{3,1},{4,6},{5,7},{6,4},{7,5},{8,10},{9,11},{10,... | collective-permute-start | bytes 884744 | tf_op jit(solution)/shard_map/ppermute | solution.py:610
  243.7 15.7 %collective-permute-start.28 = (bf16[48,768]{1,0:T(8,128)(2,1)S(1)}, bf16[48,768]{1,0:T(8,128)(2,1)S(1)}, u32[]{:S(2)}, u32[]{:S(2)}) collective-permute-start(bf16[48,768]{1,0:T(8,128)(2,1)S(1)} %get-tuple-element.110), channel_id=1, source_target_pairs={{0,4},{4,8},{8,12},{1,5},{5,9},{9,13},{2,6},{6,10},{10,14},{3,7},{... | collective-permute-start | bytes 221192 | tf_op jit(solution)/shard_map/ppermute | solution.py:640
  247.2 19.0 %collective-permute-start.33 = (bf16[48,768]{1,0:T(8,128)(2,1)S(1)}, bf16[48,768]{1,0:T(8,128)(2,1)S(1)}, u32[]{:S(2)}, u32[]{:S(2)}) collective-permute-start(bf16[48,768]{1,0:T(8,128)(2,1)S(1)} %get-tuple-element.111), channel_id=1, source_target_pairs={{12,0},{13,1},{14,2},{15,3},{28,16},{29,17},{30,18},{31,19}} | collective-permute-start | bytes 221192 | tf_op jit(solution)/shard_map/ppermute | solution.py:640
  251.2 22.1 %collective-permute-start.32 = (bf16[48,768]{1,0:T(8,128)(2,1)}, bf16[48,768]{1,0:T(8,128)(2,1)}, u32[]{:S(2)}, u32[]{:S(2)}) collective-permute-start(bf16[48,768]{1,0:T(8,128)(2,1)} %get-tuple-element.112), channel_id=1, source_target_pairs={{0,12},{1,13},{2,14},{3,15},{16,28},{17,29},{18,30},{19,31}} | collective-permute-start | bytes 221192 | tf_op jit(solution)/shard_map/ppermute | solution.py:640
  258.1 15.2 %collective-permute-start.31 = (bf16[48,768]{1,0:T(8,128)(2,1)}, bf16[48,768]{1,0:T(8,128)(2,1)}, u32[]{:S(2)}, u32[]{:S(2)}) collective-permute-start(bf16[48,768]{1,0:T(8,128)(2,1)} %get-tuple-element.113), channel_id=1, source_target_pairs={{8,0},{12,4},{9,1},{13,5},{10,2},{14,6},{11,3},{15,7},{24,16},{28,... | collective-permute-start | bytes 221192 | tf_op jit(solution)/shard_map/ppermute | solution.py:640
  259.4 14.4 %collective-permute-start.30 = (bf16[48,768]{1,0:T(8,128)(2,1)}, bf16[48,768]{1,0:T(8,128)(2,1)}, u32[]{:S(2)}, u32[]{:S(2)}) collective-permute-start(bf16[48,768]{1,0:T(8,128)(2,1)} %get-tuple-element.114), channel_id=1, source_target_pairs={{0,8},{4,12},{1,9},{5,13},{2,10},{6,14},{3,11},{7,15},{16,24},{20,... | collective-permute-start | bytes 221192 | tf_op jit(solution)/shard_map/ppermute | solution.py:640
  266.1 7.7 %collective-permute-start.29 = (bf16[48,768]{1,0:T(8,128)(2,1)}, bf16[48,768]{1,0:T(8,128)(2,1)}, u32[]{:S(2)}, u32[]{:S(2)}) collective-permute-start(bf16[48,768]{1,0:T(8,128)(2,1)} %get-tuple-element.115), channel_id=1, source_target_pairs={{4,0},{8,4},{12,8},{5,1},{9,5},{13,9},{6,2},{10,6},{14,10},{7,3},{... | collective-permute-start | bytes 221192 | tf_op jit(solution)/shard_map/ppermute | solution.py:640
  273.3 65.1 %collective-permute-start.42 = (bf16[4,2,192,768]{3,2,0,1:T(8,128)(2,1)}, bf16[4,2,192,768]{3,2,0,1:T(8,128)(2,1)}, u32[]{:S(2)}, u32[]{:S(2)}) collective-permute-start(bf16[4,2,192,768]{3,2,0,1:T(8,128)(2,1)} %bitcast.270), channel_id=1, source_target_pairs={{0,1},{1,0},{2,3},{3,2},{4,5},{5,4},{6,7},{7,6},{8,9},{9,8},{10,11... | collective-permute-start | bytes 7077896 | tf_op jit(solution)/shard_map/ppermute | solution.py:614
  273.3 69.0 %collective-permute-start.34 = (bf16[4,2,48,3072]{3,2,0,1:T(8,128)(2,1)}, bf16[4,2,48,3072]{3,2,0,1:T(8,128)(2,1)}, u32[]{:S(2)}, u32[]{:S(2)}) collective-permute-start(bf16[4,2,48,3072]{3,2,0,1:T(8,128)(2,1)} %bitcast.271), channel_id=1, source_target_pairs={{0,1},{1,0},{2,3},{3,2},{4,5},{5,4},{6,7},{7,6},{8,9},{9,8},{10,11... | collective-permute-start | bytes 7077896 | tf_op jit(solution)/shard_map/ppermute | solution.py:614
  303.1 3.8 collective-permute-start.11
  307.0 12.2 %collective-permute-start.12 = (bf16[1,1152]{1,0:T(2,128)(2,1)S(1)}, bf16[1,1152]{1,0:T(2,128)(2,1)S(1)}, u32[]{:S(2)}, u32[]{:S(2)}) collective-permute-start(bf16[1,1152]{1,0:T(2,128)(2,1)S(1)} %get-tuple-element.116), channel_id=1, source_target_pairs={{0,4},{4,8},{8,12},{1,5},{5,9},{9,13},{2,6},{6,10},{10,14},{3,7},{... | collective-permute-start | bytes 6920 | tf_op jit(solution)/shard_map/ppermute | solution.py:640
  311.6 9.0 %collective-permute-start.17 = (bf16[1,1152]{1,0:T(2,128)(2,1)S(1)}, bf16[1,1152]{1,0:T(2,128)(2,1)S(1)}, u32[]{:S(2)}, u32[]{:S(2)}) collective-permute-start(bf16[1,1152]{1,0:T(2,128)(2,1)S(1)} %get-tuple-element.117), channel_id=1, source_target_pairs={{12,0},{13,1},{14,2},{15,3},{28,16},{29,17},{30,18},{31,19}} | collective-permute-start | bytes 6920 | tf_op jit(solution)/shard_map/ppermute | solution.py:640
  312.9 13.1 %collective-permute-start.16 = (bf16[1,1152]{1,0:T(2,128)(2,1)S(1)}, bf16[1,1152]{1,0:T(2,128)(2,1)S(1)}, u32[]{:S(2)}, u32[]{:S(2)}) collective-permute-start(bf16[1,1152]{1,0:T(2,128)(2,1)S(1)} %get-tuple-element.118), channel_id=1, source_target_pairs={{0,12},{1,13},{2,14},{3,15},{16,28},{17,29},{18,30},{19,31}} | collective-permute-start | bytes 6920 | tf_op jit(solution)/shard_map/ppermute | solution.py:640
  319.3 8.8 %collective-permute-start.15 = (bf16[1,1152]{1,0:T(2,128)(2,1)S(1)}, bf16[1,1152]{1,0:T(2,128)(2,1)S(1)}, u32[]{:S(2)}, u32[]{:S(2)}) collective-permute-start(bf16[1,1152]{1,0:T(2,128)(2,1)S(1)} %get-tuple-element.119), channel_id=1, source_target_pairs={{8,0},{12,4},{9,1},{13,5},{10,2},{14,6},{11,3},{15,7},{24,16},{28,... | collective-permute-start | bytes 6920 | tf_op jit(solution)/shard_map/ppermute | solution.py:640
  320.6 8.1 %collective-permute-start.14 = (bf16[1,1152]{1,0:T(2,128)(2,1)S(1)}, bf16[1,1152]{1,0:T(2,128)(2,1)S(1)}, u32[]{:S(2)}, u32[]{:S(2)}) collective-permute-start(bf16[1,1152]{1,0:T(2,128)(2,1)S(1)} %get-tuple-element.120), channel_id=1, source_target_pairs={{0,8},{4,12},{1,9},{5,13},{2,10},{6,14},{3,11},{7,15},{16,24},{20,... | collective-permute-start | bytes 6920 | tf_op jit(solution)/shard_map/ppermute | solution.py:640
  326.0 5.5 %collective-permute-start.13 = (bf16[1,1152]{1,0:T(2,128)(2,1)S(1)}, bf16[1,1152]{1,0:T(2,128)(2,1)S(1)}, u32[]{:S(2)}, u32[]{:S(2)}) collective-permute-start(bf16[1,1152]{1,0:T(2,128)(2,1)S(1)} %get-tuple-element.121), channel_id=1, source_target_pairs={{4,0},{8,4},{12,8},{5,1},{9,5},{13,9},{6,2},{10,6},{14,10},{7,3},{... | collective-permute-start | bytes 6920 | tf_op jit(solution)/shard_map/ppermute | solution.py:640
  328.1 9.0 %collective-permute-start.9 = (bf16[256,768]{1,0:T(8,128)(2,1)S(1)}, bf16[256,768]{1,0:T(8,128)(2,1)S(1)}, u32[]{:S(2)}, u32[]{:S(2)}) collective-permute-start(bf16[256,768]{1,0:T(8,128)(2,1)S(1)} %slice.160), channel_id=1, source_target_pairs={{0,2},{1,3},{2,0},{3,1},{4,6},{5,7},{6,4},{7,5},{8,10},{9,11},{10,... | collective-permute-start | bytes 1179656 | tf_op jit(solution)/shard_map/ppermute | solution.py:610
  328.7 18.0 %collective-permute-start.18 = (bf16[4,2,48,2304]{3,2,0,1:T(8,128)(2,1)S(1)}, bf16[4,2,48,2304]{3,2,0,1:T(8,128)(2,1)S(1)}, u32[]{:S(2)}, u32[]{:S(2)}) collective-permute-start(bf16[4,2,48,2304]{3,2,0,1:T(8,128)(2,1)S(1)} %bitcast.278), channel_id=1, source_target_pairs={{0,1},{1,0},{2,3},{3,2},{4,5},{5,4},{6,7},{7,6},{8,9},{9,8},{10,11... | collective-permute-start | bytes 5308424 | tf_op jit(solution)/shard_map/ppermute | solution.py:614
  341.8 29.0 %collective-permute-start.43 = (bf16[4,192,768]{2,1,0:T(8,128)(2,1)S(1)}, bf16[4,192,768]{2,1,0:T(8,128)(2,1)S(1)}, u32[]{:S(2)}, u32[]{:S(2)}) collective-permute-start(bf16[4,192,768]{2,1,0:T(8,128)(2,1)S(1)} %dynamic-slice_bitcast_fusion), channel_id=1, source_target_pairs={{0,2},{1,3},{2,0},{3,1},{4,6},{5,7},{6,4},{7,5},{8,10},{9,11},{10,... | collective-permute-start | bytes 3538952 | tf_op jit(solution)/shard_map/ppermute | solution.py:610
  346.0 50.0 %collective-permute-start.35 = (bf16[4,48,3072]{2,1,0:T(8,128)(2,1)S(1)}, bf16[4,48,3072]{2,1,0:T(8,128)(2,1)S(1)}, u32[]{:S(2)}, u32[]{:S(2)}) collective-permute-start(bf16[4,48,3072]{2,1,0:T(8,128)(2,1)S(1)} %dynamic-slice_bitcast_fusion.1), channel_id=1, source_target_pairs={{0,2},{1,3},{2,0},{3,1},{4,6},{5,7},{6,4},{7,5},{8,10},{9,11},{10,... | collective-permute-start | bytes 3538952 | tf_op jit(solution)/shard_map/ppermute | solution.py:610
  347.1 63.8 %collective-permute-start.19 = (bf16[4,48,2304]{2,1,0:T(8,128)(2,1)S(1)}, bf16[4,48,2304]{2,1,0:T(8,128)(2,1)S(1)}, u32[]{:S(2)}, u32[]{:S(2)}) collective-permute-start(bf16[4,48,2304]{2,1,0:T(8,128)(2,1)S(1)} %dynamic-slice_bitcast_fusion.2), channel_id=1, source_target_pairs={{0,2},{1,3},{2,0},{3,1},{4,6},{5,7},{6,4},{7,5},{8,10},{9,11},{10,... | collective-permute-start | bytes 2654216 | tf_op jit(solution)/shard_map/ppermute | solution.py:610
  371.2 43.4 %collective-permute-start.44 = (bf16[192,768]{1,0:T(8,128)(2,1)S(1)}, bf16[192,768]{1,0:T(8,128)(2,1)S(1)}, u32[]{:S(2)}, u32[]{:S(2)}) collective-permute-start(bf16[192,768]{1,0:T(8,128)(2,1)S(1)} %get-tuple-element.84), channel_id=1, source_target_pairs={{0,4},{4,8},{8,12},{1,5},{5,9},{9,13},{2,6},{6,10},{10,14},{3,7},{... | collective-permute-start | bytes 884744 | tf_op jit(solution)/shard_map/ppermute | solution.py:640
  375.4 40.4 %collective-permute-start.49 = (bf16[192,768]{1,0:T(8,128)(2,1)S(1)}, bf16[192,768]{1,0:T(8,128)(2,1)S(1)}, u32[]{:S(2)}, u32[]{:S(2)}) collective-permute-start(bf16[192,768]{1,0:T(8,128)(2,1)S(1)} %get-tuple-element.85), channel_id=1, source_target_pairs={{12,0},{13,1},{14,2},{15,3},{28,16},{29,17},{30,18},{31,19}} | collective-permute-start | bytes 884744 | tf_op jit(solution)/shard_map/ppermute | solution.py:640
  396.6 24.8 %collective-permute-start.36 = (bf16[48,3072]{1,0:T(8,128)(2,1)S(1)}, bf16[48,3072]{1,0:T(8,128)(2,1)S(1)}, u32[]{:S(2)}, u32[]{:S(2)}) collective-permute-start(bf16[48,3072]{1,0:T(8,128)(2,1)S(1)} %get-tuple-element.90), channel_id=1, source_target_pairs={{0,4},{4,8},{8,12},{1,5},{5,9},{9,13},{2,6},{6,10},{10,14},{3,7},{... | collective-permute-start | bytes 884744 | tf_op jit(solution)/shard_map/ppermute | solution.py:640
  400.8 21.9 %collective-permute-start.41 = (bf16[48,3072]{1,0:T(8,128)(2,1)S(1)}, bf16[48,3072]{1,0:T(8,128)(2,1)S(1)}, u32[]{:S(2)}, u32[]{:S(2)}) collective-permute-start(bf16[48,3072]{1,0:T(8,128)(2,1)S(1)} %get-tuple-element.91), channel_id=1, source_target_pairs={{12,0},{13,1},{14,2},{15,3},{28,16},{29,17},{30,18},{31,19}} | collective-permute-start | bytes 884744 | tf_op jit(solution)/shard_map/ppermute | solution.py:640
  410.9 15.3 %collective-permute-start.40 = (bf16[48,3072]{1,0:T(8,128)(2,1)S(1)}, bf16[48,3072]{1,0:T(8,128)(2,1)S(1)}, u32[]{:S(2)}, u32[]{:S(2)}) collective-permute-start(bf16[48,3072]{1,0:T(8,128)(2,1)S(1)} %get-tuple-element.92), channel_id=1, source_target_pairs={{0,12},{1,13},{2,14},{3,15},{16,28},{17,29},{18,30},{19,31}} | collective-permute-start | bytes 884744 | tf_op jit(solution)/shard_map/ppermute | solution.py:640
  414.6 21.5 %collective-permute-start.39 = (bf16[48,3072]{1,0:T(8,128)(2,1)S(1)}, bf16[48,3072]{1,0:T(8,128)(2,1)S(1)}, u32[]{:S(2)}, u32[]{:S(2)}) collective-permute-start(bf16[48,3072]{1,0:T(8,128)(2,1)S(1)} %get-tuple-element.93), channel_id=1, source_target_pairs={{8,0},{12,4},{9,1},{13,5},{10,2},{14,6},{11,3},{15,7},{24,16},{28,... | collective-permute-start | bytes 884744 | tf_op jit(solution)/shard_map/ppermute | solution.py:640
  415.9 21.5 %collective-permute-start.38 = (bf16[48,3072]{1,0:T(8,128)(2,1)S(1)}, bf16[48,3072]{1,0:T(8,128)(2,1)S(1)}, u32[]{:S(2)}, u32[]{:S(2)}) collective-permute-start(bf16[48,3072]{1,0:T(8,128)(2,1)S(1)} %get-tuple-element.94), channel_id=1, source_target_pairs={{0,8},{4,12},{1,9},{5,13},{2,10},{6,14},{3,11},{7,15},{16,24},{20,... | collective-permute-start | bytes 884744 | tf_op jit(solution)/shard_map/ppermute | solution.py:640
  421.4 17.3 %collective-permute-start.37 = (bf16[48,3072]{1,0:T(8,128)(2,1)S(1)}, bf16[48,3072]{1,0:T(8,128)(2,1)S(1)}, u32[]{:S(2)}, u32[]{:S(2)}) collective-permute-start(bf16[48,3072]{1,0:T(8,128)(2,1)S(1)} %get-tuple-element.95), channel_id=1, source_target_pairs={{4,0},{8,4},{12,8},{5,1},{9,5},{13,9},{6,2},{10,6},{14,10},{7,3},{... | collective-permute-start | bytes 884744 | tf_op jit(solution)/shard_map/ppermute | solution.py:640
  422.8 27.5 %collective-permute-start.48 = (bf16[192,768]{1,0:T(8,128)(2,1)S(1)}, bf16[192,768]{1,0:T(8,128)(2,1)S(1)}, u32[]{:S(2)}, u32[]{:S(2)}) collective-permute-start(bf16[192,768]{1,0:T(8,128)(2,1)S(1)} %get-tuple-element.86), channel_id=1, source_target_pairs={{0,12},{1,13},{2,14},{3,15},{16,28},{17,29},{18,30},{19,31}} | collective-permute-start | bytes 884744 | tf_op jit(solution)/shard_map/ppermute | solution.py:640
  426.2 25.4 %collective-permute-start.47 = (bf16[192,768]{1,0:T(8,128)(2,1)S(1)}, bf16[192,768]{1,0:T(8,128)(2,1)S(1)}, u32[]{:S(2)}, u32[]{:S(2)}) collective-permute-start(bf16[192,768]{1,0:T(8,128)(2,1)S(1)} %get-tuple-element.87), channel_id=1, source_target_pairs={{8,0},{12,4},{9,1},{13,5},{10,2},{14,6},{11,3},{15,7},{24,16},{28,... | collective-permute-start | bytes 884744 | tf_op jit(solution)/shard_map/ppermute | solution.py:640
  436.0 22.0 %collective-permute-start.46 = (bf16[192,768]{1,0:T(8,128)(2,1)S(1)}, bf16[192,768]{1,0:T(8,128)(2,1)S(1)}, u32[]{:S(2)}, u32[]{:S(2)}) collective-permute-start(bf16[192,768]{1,0:T(8,128)(2,1)S(1)} %get-tuple-element.88), channel_id=1, source_target_pairs={{0,8},{4,12},{1,9},{5,13},{2,10},{6,14},{3,11},{7,15},{16,24},{20,... | collective-permute-start | bytes 884744 | tf_op jit(solution)/shard_map/ppermute | solution.py:640
  437.3 22.0 %collective-permute-start.45 = (bf16[192,768]{1,0:T(8,128)(2,1)S(1)}, bf16[192,768]{1,0:T(8,128)(2,1)S(1)}, u32[]{:S(2)}, u32[]{:S(2)}) collective-permute-start(bf16[192,768]{1,0:T(8,128)(2,1)S(1)} %get-tuple-element.89), channel_id=1, source_target_pairs={{4,0},{8,4},{12,8},{5,1},{9,5},{13,9},{6,2},{10,6},{14,10},{7,3},{... | collective-permute-start | bytes 884744 | tf_op jit(solution)/shard_map/ppermute | solution.py:640
  438.7 26.1 %collective-permute-start.20 = (bf16[48,2304]{1,0:T(8,128)(2,1)S(1)}, bf16[48,2304]{1,0:T(8,128)(2,1)S(1)}, u32[]{:S(2)}, u32[]{:S(2)}) collective-permute-start(bf16[48,2304]{1,0:T(8,128)(2,1)S(1)} %get-tuple-element.100), channel_id=1, source_target_pairs={{0,4},{4,8},{8,12},{1,5},{5,9},{9,13},{2,6},{6,10},{10,14},{3,7},{... | collective-permute-start | bytes 663560 | tf_op jit(solution)/shard_map/ppermute | solution.py:640
  450.3 16.9 %collective-permute-start.25 = (bf16[48,2304]{1,0:T(8,128)(2,1)S(1)}, bf16[48,2304]{1,0:T(8,128)(2,1)S(1)}, u32[]{:S(2)}, u32[]{:S(2)}) collective-permute-start(bf16[48,2304]{1,0:T(8,128)(2,1)S(1)} %get-tuple-element.101), channel_id=1, source_target_pairs={{12,0},{13,1},{14,2},{15,3},{28,16},{29,17},{30,18},{31,19}} | collective-permute-start | bytes 663560 | tf_op jit(solution)/shard_map/ppermute | solution.py:640
  451.6 15.6 %collective-permute-start.24 = (bf16[48,2304]{1,0:T(8,128)(2,1)S(1)}, bf16[48,2304]{1,0:T(8,128)(2,1)S(1)}, u32[]{:S(2)}, u32[]{:S(2)}) collective-permute-start(bf16[48,2304]{1,0:T(8,128)(2,1)S(1)} %get-tuple-element.102), channel_id=1, source_target_pairs={{0,12},{1,13},{2,14},{3,15},{16,28},{17,29},{18,30},{19,31}} | collective-permute-start | bytes 663560 | tf_op jit(solution)/shard_map/ppermute | solution.py:640
  458.0 11.8 %collective-permute-start.23 = (bf16[48,2304]{1,0:T(8,128)(2,1)S(1)}, bf16[48,2304]{1,0:T(8,128)(2,1)S(1)}, u32[]{:S(2)}, u32[]{:S(2)}) collective-permute-start(bf16[48,2304]{1,0:T(8,128)(2,1)S(1)} %get-tuple-element.103), channel_id=1, source_target_pairs={{8,0},{12,4},{9,1},{13,5},{10,2},{14,6},{11,3},{15,7},{24,16},{28,... | collective-permute-start | bytes 663560 | tf_op jit(solution)/shard_map/ppermute | solution.py:640
  459.3 10.5 %collective-permute-start.22 = (bf16[48,2304]{1,0:T(8,128)(2,1)S(1)}, bf16[48,2304]{1,0:T(8,128)(2,1)S(1)}, u32[]{:S(2)}, u32[]{:S(2)}) collective-permute-start(bf16[48,2304]{1,0:T(8,128)(2,1)S(1)} %get-tuple-element.104), channel_id=1, source_target_pairs={{0,8},{4,12},{1,9},{5,13},{2,10},{6,14},{3,11},{7,15},{16,24},{20,... | collective-permute-start | bytes 663560 | tf_op jit(solution)/shard_map/ppermute | solution.py:640
  464.8 9.6 %collective-permute-start.21 = (bf16[48,2304]{1,0:T(8,128)(2,1)S(1)}, bf16[48,2304]{1,0:T(8,128)(2,1)S(1)}, u32[]{:S(2)}, u32[]{:S(2)}) collective-permute-start(bf16[48,2304]{1,0:T(8,128)(2,1)S(1)} %get-tuple-element.105), channel_id=1, source_target_pairs={{4,0},{8,4},{12,8},{5,1},{9,5},{13,9},{6,2},{10,6},{14,10},{7,3},{... | collective-permute-start | bytes 663560 | tf_op jit(solution)/shard_map/ppermute | solution.py:640
  (88 other events, 1143.0 us)

commit v2 on v0

--- a/solution.py
+++ b/solution.py
@@ -1,11 +1,572 @@
+import functools
+import math
 import jax
 import jax.numpy as jnp
 from jax import lax
+from jax.experimental import pallas as pl
+from jax.experimental.pallas import tpu as pltpu
 from jax.sharding import PartitionSpec as P
 
 D = 768
 HEADS = 12
 HDIM = 64
+PAIR = 2 * HDIM
+PAIRS = HEADS // 2
+OWN = 4
+CHUNK = 128
+BACK_CHUNK = 1024
+SAFE = 60.0
+NT = (((1,), (1,)), ((), ()))
+TN = (((0,), (0,)), ((), ()))
+NN = (((1,), (0,)), ((), ()))
+
+
+def dot(left, right, dims):
+    return lax.dot_general(left, right, dims, preferred_element_type=jnp.float32)
+
+
+def slot_meta(own_pos, other_pos, signed):
+    rank = jnp.sum((own_pos[None, :] < own_pos[:, None]).astype(jnp.int32), axis=1)
+    chosen = rank[None, :] == jnp.arange(OWN, dtype=jnp.int32)[:, None]
+    ranked = jnp.sum(jnp.where(chosen, jnp.arange(OWN, dtype=jnp.int32)[None, :], 0), axis=1)
+    ranked_pos = jnp.sum(jnp.where(chosen, own_pos[None, :], 0), axis=1)
+    return jnp.concatenate([own_pos, other_pos, ranked, ranked_pos, signed.astype(jnp.int32)[None]])
+
+
+def sort_rows(meta, own, other, target, span, first):
+    columns = slice(first, first + D)
+    for slot in range(OWN):
+        for base, source in ((0, own), (OWN, other)):
+            start = pl.multiple_of(meta[base + slot] * span, span)
+            target[pl.ds(start, span), :] = source[slot * span : (slot + 1) * span, columns]
+
+
+def reach(rank, slots):
+    return ((0, slots // 2 - 2), (1, slots // 2 - 1), (slots // 2, slots - 2), (slots // 2 + 1, slots - 1))[rank]
+
+
+def stacked_heads(rows):
+    second = lax.broadcasted_iota(jnp.int32, rows.shape, 1) >= HDIM
+    zero = jnp.zeros_like(rows)
+    return jnp.concatenate([jnp.where(second, zero, rows), jnp.where(second, rows, zero)], axis=0)
+
+
+def visible(values, start, least, span, position, fill):
+    if start + values.shape[0] <= least * span:
+        return values
+    key_at = lax.broadcasted_iota(jnp.int32, values.shape, 0) + start
+    lane = lax.broadcasted_iota(jnp.int32, values.shape, 1)
+    query_at = position * span + jnp.where(lane >= span, lane - span, lane)
+    return jnp.where(key_at <= query_at, values, fill)
+
+
+def unstack(pair, span):
+    row = lax.broadcasted_iota(jnp.int32, (PAIR, span), 0)
+    return jnp.where(row < HDIM, pair[:, :span], pair[:, span:]).T
+
+
+def chunks_of(count, chunk):
+    return [slice(start, min(start + chunk, count)) for start in range(0, count, chunk)]
+
+
+def eight(values):
+    return values.reshape(-1, 8, values.shape[-1])
+
+
+def pair_columns(at):
+    return pl.ds(pl.multiple_of(at * PAIR, PAIR), PAIR)
+
+
+def largest_norm(rows_ref):
+    feature = lax.broadcasted_iota(jnp.int32, (D, PAIR), 0) // HDIM
+    head = lax.broadcasted_iota(jnp.int32, (D, PAIR), 1)
+    chosen = jnp.where(feature == head, 1.0, 0.0).astype(jnp.bfloat16)
+    rows = rows_ref[...]
+    return jnp.max(dot(rows * rows, chosen, NN))
+
+
+def forward_kernel(meta, q_ref, kv_ref, kv2_ref, o_ref, lse_ref, keys, values, *, span):
+    slots = keys.shape[0] // span
+    sort_rows(meta, kv_ref, kv2_ref, keys, span, 0)
+    sort_rows(meta, kv_ref, kv2_ref, values, span, D)
+    bound = largest_norm(q_ref) * largest_norm(keys) * (1.1 / HDIM)
+    near = bound < SAFE * SAFE
+
+    def run(signed, safe):
+        def one_pair(pair, _):
+            columns = pair_columns(pair)
+            values_t = values[:, columns].T
+            for rank in reversed(range(OWN)):
+                least, most = reach(rank, slots)
+                count = (most + 1) * span
+                row_at = pl.multiple_of(meta[2 * OWN + rank] * span, span)
+                position = meta[3 * OWN + rank]
+                queries = stacked_heads(q_ref[pl.ds(row_at, span), columns] * 0.125)
+                largest = None
+                if not safe:
+                    most_seen = jnp.full((8, 2 * span), -1e30, jnp.float32)
+                    for part in chunks_of(count, CHUNK):
+                        scores = dot(keys[part, columns], queries, NT)
+                        scores = jnp.abs(scores) if signed else scores
+                        scores = visible(scores, part.start, least, span, position, -1e30)
+                        most_seen = jnp.maximum(most_seen, jnp.max(eight(scores), axis=0))
+                    largest = jnp.max(most_seen, axis=0, keepdims=True)
+                    if signed:
+                        square = largest * largest + 1.0
+                        largest = square * lax.rsqrt(square)
+                total = jnp.zeros((8, 2 * span), jnp.float32)
+                gathered = jnp.zeros((PAIR, 2 * span), jnp.float32)
+                for part in chunks_of(count, CHUNK):
+                    scores = dot(keys[part, columns], queries, NT)
+                    argument = scores
+                    if signed:
+                        square = scores * scores + 1.0
+                        inverse = lax.rsqrt(square)
+                        argument = square * inverse
+                    if not safe:
+                        argument = argument - largest
+                    weights = jnp.exp(visible(argument, part.start, least, span, position, -1e30))
+                    total += jnp.sum(eight(weights), axis=0)
+                    if signed:
+                        weights = weights * (scores * inverse)
+                    gathered += dot(values_t[:, part], weights.astype(jnp.bfloat16), NN)
+                total = jnp.sum(total, axis=0, keepdims=True)
+                lse = jnp.log(total)
+                lse_ref[pair, rank : rank + 1, :] = lse if safe else lse + largest
+                gathered = gathered * (1.0 / total)
+                o_ref[pl.ds(row_at, span), columns] = unstack(gathered, span).astype(jnp.bfloat16)
+            return 0
+
+        lax.fori_loop(0, PAIRS, one_pair, 0)
+
+    for signed in (True, False):
+        for safe in (True, False):
+            chosen = (meta[4 * OWN] == int(signed)) & (near == safe)
+            pl.when(chosen)(functools.partial(run, signed, safe))
+
+
+SMEM_SPEC = pl.BlockSpec(memory_space=pltpu.SMEM)
+VMEM_SPEC = pl.BlockSpec(memory_space=pltpu.VMEM)
+
+
+def sorted_attend(meta, queries, kv, kv_other):
+    rows = kv.shape[0]
+    span = rows // OWN
+    return pl.pallas_call(
+        functools.partial(forward_kernel, span=span),
+        in_specs=[SMEM_SPEC] + [VMEM_SPEC] * 3,
+        out_specs=[VMEM_SPEC] * 2,
+        scratch_shapes=[pltpu.VMEM((2 * rows, D), jnp.bfloat16)] * 2,
+        out_shape=[
+            jax.ShapeDtypeStruct((rows, D), jnp.bfloat16),
+            jax.ShapeDtypeStruct((PAIRS, OWN, 2 * span), jnp.float32),
+        ],
+        compiler_params=pltpu.CompilerParams(vmem_limit_bytes=12 * 1024 * 1024),
+        cost_estimate=pl.CostEstimate(flops=4_000_000_000, bytes_accessed=0, transcendentals=0),
+        name="attend",
+    )(meta, queries, kv, kv_other)
+
+
+def backward_kernel(
+    meta, q_ref, kv_ref, kv2_ref, o_ref, do_ref, lse_ref,
+    dq_ref, own_ref, other_ref, keys, values, grad_k, grad_v, *, span,
+):
+    slots = keys.shape[0] // span
+    sort_rows(meta, kv_ref, kv2_ref, keys, span, 0)
+    sort_rows(meta, kv_ref, kv2_ref, values, span, D)
+
+    def run(signed):
+        def one_pair(pair, _):
+            columns = pair_columns(pair)
+            keys_t = keys[:, columns].T
+            for rank in reversed(range(OWN)):
+                least, most = reach(rank, slots)
+                count = (most + 1) * span
+                row_at = pl.multiple_of(meta[2 * OWN + rank] * span, span)
+                position = meta[3 * OWN + rank]
+                queries = stacked_heads(q_ref[pl.ds(row_at, span), columns] * 0.125)
+                grad_rows = do_ref[pl.ds(row_at, span), columns]
+                grads = stacked_heads(grad_rows)
+                product = grad_rows.astype(jnp.float32) * o_ref[pl.ds(row_at, span), columns].astype(jnp.float32)
+                delta = jnp.sum(stacked_heads(product).T, axis=0, keepdims=True)
+                lse = lse_ref[pair, rank : rank + 1, :]
+                gathered = jnp.zeros((PAIR, 2 * span), jnp.float32)
+                for part in chunks_of(count, BACK_CHUNK):
+                    scores = dot(keys[part, columns], queries, NT)
+                    along = dot(values[part, columns], grads, NT)
+                    argument = scores
+                    if signed:
+                        square = scores * scores + 1.0
+                        inverse = lax.rsqrt(square)
+                        argument = square * inverse
+                    prob = jnp.exp(visible(argument - lse, part.start, least, span, position, -1e30))
+                    if signed:
+                        sign_pattern = scores * inverse
+                        weights = prob * sign_pattern
+                        bend = inverse * inverse * inverse
+                        dscore = prob * ((sign_pattern * along - delta) * sign_pattern + along * bend)
+                    else:
+                        weights = prob
+                        dscore = prob * (along - delta)
+                    weights = weights.astype(jnp.bfloat16)
+                    dscore = dscore.astype(jnp.bfloat16)
+                    added_v = dot(weights, grads, NN)
+                    added_k = dot(dscore, queries, NN)
+                    if rank == OWN - 1:
+                        grad_v[part, :] = added_v
+                        grad_k[part, :] = added_k
+                    else:
+                        grad_v[part, :] += added_v
+                        grad_k[part, :] += added_k
+                    gathered += dot(keys_t[:, part], dscore, NN)
+                dq_ref[pl.ds(row_at, span), columns] = (unstack(gathered, span) * 0.125).astype(jnp.bfloat16)
+            for slot in range(OWN):
+                there = slice(slot * span, (slot + 1) * span)
+                own_at = pl.multiple_of(meta[slot] * span, span)
+                other_at = pl.multiple_of(meta[OWN + slot] * span, span)
+                for part, total in enumerate((grad_k, grad_v)):
+                    own_ref[part, there, columns] = total[pl.ds(own_at, span), :].astype(jnp.bfloat16)
+                    other_ref[part, there, columns] = total[pl.ds(other_at, span), :].astype(jnp.bfloat16)
+            return 0
+
+        lax.fori_loop(0, PAIRS, one_pair, 0)
+
+    for signed in (True, False):
+        pl.when(meta[4 * OWN] == int(signed))(functools.partial(run, signed))
+
+
+def sorted_attend_back(meta, queries, kv, kv_other, attended, grad_att, lse):
+    rows = kv.shape[0]
+    span = rows // OWN
+    return pl.pallas_call(
+        functools.partial(backward_kernel, span=span),
+        in_specs=[SMEM_SPEC] + [VMEM_SPEC] * 6,
+        out_specs=[VMEM_SPEC] * 3,
+        scratch_shapes=[pltpu.VMEM((2 * rows, D), jnp.bfloat16)] * 2
+        + [pltpu.VMEM((2 * rows, PAIR), jnp.float32)] * 2,
+        out_shape=[
+            jax.ShapeDtypeStruct((rows, D), jnp.bfloat16),
+            jax.ShapeDtypeStruct((2, rows, D), jnp.bfloat16),
+            jax.ShapeDtypeStruct((2, rows, D), jnp.bfloat16),
+        ],
+        compiler_params=pltpu.CompilerParams(vmem_limit_bytes=18 * 1024 * 1024),
+        cost_estimate=pl.CostEstimate(flops=8_000_000_000, bytes_accessed=0, transcendentals=0),
+        name="attend_back",
+    )(meta, queries, kv, kv_other, attended, grad_att, lse)
+
+
+TURN_TANH = 0.7978845608028654
+CUBE = 0.044715
+CHUNKS = 1
+
+
+def normalised(rows):
+    center = rows - jnp.mean(rows, axis=-1, keepdims=True)
+    inverse = lax.rsqrt(jnp.mean(center * center, axis=-1, keepdims=True) + 1e-05)
+    return center * inverse, inverse
+
+
+def norm_back(unit, inverse, gain_row, grad):
+    scaled = grad * gain_row
+    along = jnp.mean(scaled * unit, axis=-1, keepdims=True)
+    return inverse * (scaled - jnp.mean(scaled, axis=-1, keepdims=True) - unit * along)
+
+
+def row_chunks(rows, chunks=CHUNKS):
+    return [slice(at * rows // chunks, (at + 1) * rows // chunks) for at in range(chunks)]
+
+
+def column_sum(values):
+    return jnp.sum(values, axis=0, keepdims=True)
+
+
+def gelu_parts(hidden):
+    square = hidden * hidden
+    curve = jnp.tanh(hidden * (TURN_TANH + TURN_TANH * CUBE * square))
+    half = 0.5 + 0.5 * curve
+    inner = hidden * (TURN_TANH + 3.0 * TURN_TANH * CUBE * square)
+    return hidden * half, half + 0.5 * (1.0 - curve * curve) * inner
+
+
+def gelu_only(hidden):
+    square = hidden * hidden
+    curve = jnp.tanh(hidden * (TURN_TANH + TURN_TANH * CUBE * square))
+    return hidden * (0.5 + 0.5 * curve)
+
+
+def cost(flops, nbytes):
+    return pl.CostEstimate(flops=int(flops) // 8, bytes_accessed=0, transcendentals=0)
+
+
+def call(kernel, name, megabytes, flops, outs, scratch, *operands, smem=0):
+    shapes = [jax.ShapeDtypeStruct(shape, dtype) for shape, dtype in outs]
+    nbytes = sum(value.size * value.dtype.itemsize for value in (*operands, *shapes))
+    return pl.pallas_call(
+        kernel,
+        in_specs=[SMEM_SPEC] * smem + [VMEM_SPEC] * (len(operands) - smem),
+        out_specs=[VMEM_SPEC] * len(shapes),
+        out_shape=shapes,
+        scratch_shapes=scratch,
+        compiler_params=pltpu.CompilerParams(vmem_limit_bytes=megabytes * 1024 * 1024),
+        cost_estimate=cost(flops, nbytes),
+        name=name,
+    )(*operands)
+
+
+def bias_part(biases, at):
+    return biases[0:1, at * D : (at + 1) * D]
+
+
+def tile(at):
+    return slice(at * D, (at + 1) * D)
+
+
+def whole(*shape):
+    return pl.BlockSpec(shape, lambda *_: (0,) * len(shape))
+
+
+def front_kernel(x_ref, gains, biases, w_ref, normed_ref, q_ref, kv_ref):
+    for part in row_chunks(x_ref.shape[0]):
+        unit, _ = normalised(x_ref[part, :].astype(jnp.float32))
+        normed = (unit * gains[0:1, :] + bias_part(biases, 0)).astype(jnp.bfloat16)
+        normed_ref[part, :] = normed
+        kv_ref[part, :D] = dot(normed, w_ref[0, :, tile(1)], NN).astype(jnp.bfloat16)
+        kv_ref[part, D:] = (dot(normed, w_ref[0, :, tile(2)], NN) + bias_part(biases, 3)).astype(jnp.bfloat16)
+        q_ref[part, :] = (dot(normed, w_ref[0, :, tile(0)], NN) + bias_part(biases, 2)).astype(jnp.bfloat16)
+
+
+def front(entry, gains, biases, w_qkv):
+    rows = entry.shape[0]
+    narrow = jnp.bfloat16
+    outs = [((rows, D), narrow), ((rows, D), narrow), ((rows, 2 * D), narrow)]
+    return call(front_kernel, "front", 8, 6 * rows * D * D, outs, [], entry, gains, biases, w_qkv)
+
+
+def middle_rows(x_ref, o_ref, w_out, biases, part):
+    return x_ref[part, :].astype(jnp.float32) + dot(o_ref[part, :], w_out[0], NN) + bias_part(biases, 4)
+
+
+def rest_kernel(x_ref, o_ref, gains, biases, w_out, w_up, w_down, result_ref):
+    for part in row_chunks(x_ref.shape[0]):
+        middle = middle_rows(x_ref, o_ref, w_out, biases, part)
+        unit, _ = normalised(middle)
+        normed = (unit * gains[1:2, :] + bias_part(biases, 1)).astype(jnp.bfloat16)
+        total = middle + bias_part(biases, 5)
+        for at in range(w_up.shape[2] // D):
+            hidden = dot(normed, w_up[0, :, tile(at)], NN) + bias_part(biases, 6 + at)
+            total += dot(gelu_only(hidden).astype(jnp.bfloat16), w_down[0, tile(at), :], NN)
+        result_ref[part, :] = total.astype(jnp.bfloat16)
+
+
+def rest(entry, attended, gains, biases, w_out, w_up, w_down):
+    rows = entry.shape[0]
+    flops = 2 * rows * (D * D + 2 * w_up.size)
+    return call(
+        rest_kernel, "rest", 8, flops, [((rows, D), jnp.bfloat16)], [],
+        entry, attended, gains, biases, w_out, w_up, w_down,
+    )[0]
+
+
+def turn_kernel(
+    x_ref, o_ref, d_ref, gains, biases, w_out, w_up, out_t, up_t, down_t,
+    middle_ref, normed_ref, active_ref, slope_ref, grad_ref, grad_att_ref,
+):
+    for part in row_chunks(x_ref.shape[0]):
+        middle = middle_rows(x_ref, o_ref, w_out, biases, part)
+        middle_ref[part, :] = middle
+        unit, inverse = normalised(middle)
+        normed = (unit * gains[1:2, :] + bias_part(biases, 1)).astype(jnp.bfloat16)
+        normed_ref[part, :] = normed
+        total = jnp.zeros_like(middle)
+        for at in range(w_up.shape[2] // D):
+            hidden = dot(normed, w_up[0, :, tile(at)], NN) + bias_part(biases, 6 + at)
+            active, slope = gelu_parts(hidden)
+            active_ref[part, tile(at)] = active.astype(jnp.bfloat16)
+            slope_ref[part, tile(at)] = slope.astype(jnp.bfloat16)
+            grad_hidden = dot(d_ref[part, :], down_t[:, tile(at)], NN) * slope
+            total += dot(grad_hidden.astype(jnp.bfloat16), up_t[tile(at), :], NN)
+        unit, inverse = normalised(middle_ref[part, :])
+        grad = d_ref[part, :].astype(jnp.float32) + norm_back(unit, inverse, gains[1:2, :], total)
+        grad_ref[part, :] = grad
+        grad_att_ref[part, :] = dot(grad.astype(jnp.bfloat16), out_t[...], NN).astype(jnp.bfloat16)
+
+
+def turn(entry, attended, result_gradient, gains, biases, w_out, w_up, out_t, up_t, down_t):
+    rows = entry.shape[0]
+    wide, narrow = jnp.float32, jnp.bfloat16
+    inner = w_up.shape[2]
+    outs = [
+        ((rows, D), wide), ((rows, D), narrow), ((rows, inner), narrow),
+        ((rows, inner), narrow), ((rows, D), wide), ((rows, D), narrow),
+    ]
+    return call(
+        turn_kernel, "turn", 12, 2 * rows * (2 * D * D + 3 * w_up.size), outs, [],
+        entry, attended, result_gradient, gains, biases, w_out, w_up, out_t, up_t, down_t,
+    )
+
+
+def down_back_kernel(
+    d_ref, slope_ref, middle_ref, gains, out_t, up_t, down_t,
+    hidden_ref, grad_ref, grad_b_ref, grad_att_ref, sums_ref, up_ref,
+):
+    sums = [jnp.zeros((1, D), jnp.float32)] * 4
+    steps = up_t.shape[0] // D
+    up_sums = [jnp.zeros((1, D), jnp.float32)] * steps
+    for part in row_chunks(d_ref.shape[0]):
+        given = d_ref[part, :]
+        through = jnp.zeros(given.shape, jnp.float32)
+        for at in range(steps):
+            grad_hidden = dot(given, down_t[:, tile(at)], NN) * slope_ref[part, tile(at)].astype(jnp.float32)
+            up_sums[at] = up_sums[at] + column_sum(grad_hidden)
+            grad_hidden = grad_hidden.astype(jnp.bfloat16)
+            hidden_ref[part, tile(at)] = grad_hidden
+            through += dot(grad_hidden, up_t[tile(at), :], NN)
+        unit, inverse = normalised(middle_ref[part, :])
+        given = given.astype(jnp.float32)
+        grad = given + norm_back(unit, inverse, gains[1:2, :], through)
+        grad_ref[part, :] = grad
+        grad_b = grad.astype(jnp.bfloat16)
+        grad_b_ref[part, :] = grad_b
+        grad_att_ref[part, :] = dot(grad_b, out_t[...], NN).astype(jnp.bfloat16)
+        for at, term in enumerate((through * unit, through, grad, given)):
+            sums[at] = sums[at] + column_sum(term)
+    sums_ref[...] = jnp.concatenate(sums, axis=0)
+    up_ref[...] = jnp.concatenate(up_sums, axis=0)
+
+
+def down_back(result_gradient, slope, middle, gains, out_t, up_t, down_t):
+    rows = result_gradient.shape[0]
+    wide, narrow = jnp.float32, jnp.bfloat16
+    inner = up_t.shape[0]
+    outs = [
+        ((rows, inner), narrow), ((rows, D), wide), ((rows, D), narrow),
+        ((rows, D), narrow), ((4, D), wide), ((inner // D, D), wide),
+    ]
+    return call(
+        down_back_kernel, "down_back", 10, 2 * rows * (D * D + 2 * up_t.size), outs, [],
+        result_gradient, slope, middle, gains, out_t, up_t, down_t,
+    )
+
+
+def qkv_tiles(part, q_ref, own_ref, there_ref):
+    tiles = [q_ref[part, :]]
+    for at in range(2):
+        total = own_ref[at, part, :].astype(jnp.float32) + there_ref[at, part, :].astype(jnp.float32)
+        tiles.append(total.astype(jnp.bfloat16))
+    return tiles
+
+
+def front_back_kernel(q_ref, own_ref, there_ref, x_ref, grad_ref, gains, qkv_t, out_ref, sums_ref):
+    sums = [jnp.zeros((1, D), jnp.float32)] * 4
+    for part in row_chunks(x_ref.shape[0]):
+        tiles = qkv_tiles(part, q_ref, own_ref, there_ref)
+        through = sum(dot(value, qkv_t[tile(at), :], NN) for at, value in enumerate(tiles))
+        unit, inverse = normalised(x_ref[part, :].astype(jnp.float32))
+        out = grad_ref[part, :] + norm_back(unit, inverse, gains[0:1, :], through)
+        out_ref[part, :] = out.astype(out_ref.dtype)
+        terms = (through * unit, through, tiles[0].astype(jnp.float32), tiles[2].astype(jnp.float32))
+        for at, term in enumerate(terms):
+            sums[at] = sums[at] + column_sum(term)
+    sums_ref[...] = jnp.concatenate(sums, axis=0)
+
+
+def front_back(grad_q, own, there, entry, grad_middle, gains, qkv_t, dtype):
+    rows = entry.shape[0]
+    outs = [((rows, D), dtype), ((4, D), jnp.float32)]
+    return call(
+        front_back_kernel, "front_back", 8, 6 * rows * D * D, outs, [],
+        grad_q, own, there, entry, grad_middle, gains, qkv_t,
+    )
+
+
+def write_blocks(place, tile, order, kept_ref, sent_ref):
+    rows = kept_ref.shape[2]
+
+    def write(core):
+        for at, (z_at, y_at, core_at) in enumerate(order):
+            target = kept_ref if core_at == core else sent_ref
+            target[y_at, z_at] = tile[at * rows : (at + 1) * rows]
+
+    for core in range(2):
+        pl.when(place[0] == core)(functools.partial(write, core))
+
+
+def weight_grad_kernel(place, left_ref, right_ref, kept_ref, sent_ref, *, order):
+    tile = dot(left_ref[...], right_ref[...], NN).astype(jnp.bfloat16)
+    write_blocks(place, tile, order, kept_ref, sent_ref)
+
+
+def qkv_weight_grad_kernel(place, left_ref, q_ref, own_ref, there_ref, kept_ref, sent_ref, right, *, order):
+    step = pl.program_id(0)
+
+    @pl.when(step == 0)
+    def _():
+        right[...] = q_ref[...]
+
+    @pl.when(step > 0)
+    def _():
+        total = own_ref[0].astype(jnp.float32) + there_ref[0].astype(jnp.float32)
+        right[...] = total.astype(jnp.bfloat16)
+
+    weight_grad_kernel(place, left_ref, right, kept_ref, sent_ref, order=order)
+
+
+def all_blocks(z_count):
+    return [(z_at, y_at, core) for z_at in range(z_count) for y_at in range(2) for core in range(2)]
+
+
+def qkv_weight_grad(place, left, grad_q, own, there, z_count):
+    rows = left.shape[1]
+    block = D // (4 * z_count)
+    part = pl.BlockSpec((1, rows, D), lambda i, _: (jnp.maximum(i - 1, 0), 0, 0))
+    out_spec = pl.BlockSpec((2, z_count, block, D), lambda i, _: (0, 0, 0, i))
+    shape = jax.ShapeDtypeStruct((2, z_count, block, 3 * D), jnp.bfloat16)
+    return pl.pallas_call(
+        functools.partial(qkv_weight_grad_kernel, order=all_blocks(z_count)),
+        grid_spec=pltpu.PrefetchScalarGridSpec(
+            num_scalar_prefetch=1,
+            grid=(3,),
+            in_specs=[whole(D, rows), whole(rows, D), part, part],
+            out_specs=[out_spec, out_spec],
+            scratch_shapes=[pltpu.VMEM((rows, D), jnp.bfloat16)],
+        ),
+        out_shape=[shape, shape],
+        compiler_params=pltpu.CompilerParams(vmem_limit_bytes=14 * 1024 * 1024),
+        cost_estimate=cost(6 * rows * D * D, 20 * rows * D + 6 * D * D),
+        name="qkv_weight_grad",
+    )(place, left, grad_q, own, there)
+
+
+def weight_grad(place, left, right, z_count):
+    height, rows = left.shape
+    width = right.shape[1]
+    block = height // (4 * z_count)
+    if height > D:
+        grid = z_count
+        order = [(0, y_at, core) for y_at in range(2) for core in range(2)]
+        left_spec = pl.BlockSpec((height // grid, rows), lambda i, _: (i, 0))
+        right_spec = whole(rows, width)
+        out_spec = pl.BlockSpec((2, 1, block, width), lambda i, _: (0, i, 0, 0))
+    else:
+        grid = width // D
+        order = all_blocks(z_count)
+        left_spec = whole(height, rows)
+        right_spec = pl.BlockSpec((rows, D), lambda i, _: (0, i))
+        out_spec = pl.BlockSpec((2, z_count, block, D), lambda i, _: (0, 0, 0, i))
+    shape = jax.ShapeDtypeStruct((2, z_count, block, width), jnp.bfloat16)
+    return pl.pallas_call(
+        functools.partial(weight_grad_kernel, order=order),
+        grid_spec=pltpu.PrefetchScalarGridSpec(
+            num_scalar_prefetch=1,
+            grid=(grid,),
+            in_specs=[left_spec, right_spec],
+            out_specs=[out_spec, out_spec],
+        ),
+        out_shape=[shape, shape],
+        compiler_params=pltpu.CompilerParams(vmem_limit_bytes=14 * 1024 * 1024),
+        cost_estimate=cost(2 * rows * height * width, 2 * (rows * height + rows * width + height * width)),
+        name="weight_grad",
+    )(place, left, right)
 
 
 def shifted(value, axis, steps):
@@ -171,7 +732,7 @@
     return (middle, normed_two, hidden, active, result)
 
 
-def body(inputs, slot_order, cotangent, gains, biases, w_qkv, w_out, w_up, w_down):
+def general_body(inputs, slot_order, cotangent, gains, biases, w_qkv, w_out, w_up, w_down):
     micro_count = inputs.shape[0]
     row_count = inputs.shape[2]
     section_at = lax.axis_index("section")
@@ -363,6 +924,207 @@
     )
 
 
+def swap_halves(value):
+    count = lax.axis_size("ctx")
+    return lax.ppermute(value, "ctx", [(at, (at + count // 2) % count) for at in range(count)])
+
+
+def swap_cores(value):
+    return lax.ppermute(value, "ctx", [(at, at ^ 1) for at in range(lax.axis_size("ctx"))])
+
+
+def swap_z(value, step):
+    return lax.ppermute(value, "dp", [(at, at ^ step) for at in range(lax.axis_size("dp"))])
+
+
+def fold_kernel(place, kept_ref, arrived_ref, keep_ref, send_ref):
+    for target, chosen in ((send_ref, 1 - place[0]), (keep_ref, place[0])):
+        for at in range(target.shape[0]):
+            total = kept_ref[at, chosen].astype(jnp.float32) + arrived_ref[at, chosen].astype(jnp.float32)
+            target[at] = total.astype(target.dtype)
+
+
+def fold(kept, arrived, place, outer):
+    rows, width = kept.shape[-2:]
+    lead = math.prod(kept.shape[:outer])
+    inner = math.prod(kept.shape[outer + 1 : -1])
+    shape = (lead, 2, inner, width)
+    outs = [((lead, inner, width), kept.dtype)] * 2
+    keep, send = call(
+        fold_kernel, "fold", 4, 0, outs, [], place, kept.reshape(shape), arrived.reshape(shape), smem=1
+    )
+    left = kept.shape[:outer] + kept.shape[outer + 1 :]
+    return keep.reshape(left), send.reshape(left)
+
+
+def wide_sum(kept, arrived):
+    return kept.astype(jnp.float32) + arrived.astype(jnp.float32)
+
+
+def fast_body(inputs, slot_order, cotangent, gains, biases, w_qkv, w_out, w_up, w_down):
+    rows = inputs.shape[2]
+    count = lax.axis_size("ctx")
+    z_count = lax.axis_size("dp")
+    half = count // 2
+    ctx_at = lax.axis_index("ctx")
+    mine = ctx_at // half
+    y_at, core_at = ctx_at // 2, ctx_at % 2
+    signed = lax.axis_index("section") == 0
+    place = core_at[None].astype(jnp.int32)
+    y_place = y_at[None].astype(jnp.int32)
+    z_at = lax.axis_index("dp")
+    gain_pair = gains[0]
+    wide, narrow, barrier = jnp.float32, jnp.bfloat16, lax.optimization_barrier
+
+    def gathered(value):
+        kept = lax.dynamic_index_in_dim(value, mine, 0, keepdims=False)
+        sent = lax.dynamic_index_in_dim(value, 1 - mine, 0, keepdims=False)
+        return jnp.concatenate([kept, swap_halves(sent)], axis=0)
+
+    def returned(kept, arrived):
+        arrived = arrived.astype(kept.dtype)
+        first = jnp.where(mine == 0, kept, arrived)
+        second = jnp.where(mine == 0, arrived, kept)
+        return jnp.stack([first, second])
+
+    order = lax.dynamic_index_in_dim(slot_order[:, 0], mine, 0, keepdims=False)
+    pairs = order.reshape(count, 2)
+
+    def slots_of(device):
+        return jnp.concatenate([pairs[device], pairs[(device + half) % count]])
+
+    meta = slot_meta(slots_of(ctx_at), slots_of(ctx_at ^ 1), signed)
+
+    def through_attention(entry):
+        normed, queries, kv = front(entry, gain_pair, biases, w_qkv)
+        there = swap_cores(kv)
+        attended, lse = sorted_attend(meta, queries, kv, there)
+        return normed, queries, kv, there, attended, lse
+
+    inputs, meta = barrier((inputs, meta))
+    first = gathered(inputs[:, 0])
+    qkv_t, out_t = w_qkv[0].T, w_out[0].T
+    first, qkv_t, out_t = barrier((first, qkv_t, out_t))
+    attended = through_attention(first)[4]
+    sent = rest(first, attended, gain_pair, biases, w_out, w_up, w_down)
+    sent, later = barrier((sent, (cotangent, w_up, w_down)))
+    arrived = shifted(sent, "section", 1)
+    given = gathered(later[0][:, 0])
+    up_t, down_t = [weight[0].T for weight in later[1:]]
+    arrived, given, up_t, down_t = barrier((arrived, given, up_t, down_t))
+    entry = jnp.where(signed, first, arrived)
+
+    normed, queries, kv, kv_there, attended, lse = through_attention(entry)
+    middle, normed_two, active, slope, grad_middle, grad_att = turn(
+        entry, attended, given, gain_pair, biases, w_out, w_up, out_t, up_t, down_t
+    )
+
+    def attention_back(grad_att):
+        grad_q, own, sent = sorted_attend_back(meta, queries, kv, kv_there, attended, grad_att, lse)
+        return grad_q, own, swap_cores(sent)
+
+    grad_qkv = attention_back(grad_att)
+    handed, _ = front_back(*grad_qkv, entry, grad_middle, gain_pair, qkv_t, narrow)
+    lefts = (active, normed, attended, normed_two)
+    handed, lefts = barrier((handed, lefts))
+    back = shifted(handed, "section", -1)
+    active = lefts[0]
+    lefts = [value.T for value in lefts]
+    result = middle + dot(active, w_down[0], NN) + biases[0, 5 * D : 6 * D]
+    result = result.astype(narrow)
+    acts_there = swap_halves(result[rows:])
+    back, acts_there, lefts = barrier((back, acts_there, lefts))
+    active_t, normed_t, attended_t, normed_two_t = lefts
+    back = jnp.where(signed, back, given)
+
+    z_steps = [1 << at for at in range(z_count.bit_length() - 1)]
+    split = [2] * len(z_steps)
+    by_z = [((z_at >> at) & 1)[None].astype(jnp.int32) for at in range(len(z_steps))]
+
+    def bits(value, before):
+        return value.reshape(value.shape[:before] + tuple(split) + value.shape[before + 1 :])
+
+    grad_hidden, grad_middle, grad_middle_b, grad_att, sums_two, up_sum = down_back(
+        back, slope, middle, gain_pair, out_t, up_t, down_t
+    )
+    back, grad_hidden = barrier((back, grad_hidden))
+    down_kept, down_sent = weight_grad(place, active_t, back, z_count)
+    grad_hidden, down_sent = barrier((grad_hidden, down_sent))
+    down_there = swap_cores(down_sent)
+    up_kept, up_sent = weight_grad(place, normed_two_t, grad_hidden, z_count)
+    grad_middle_b, up_sent = barrier((grad_middle_b, up_sent))
+    up_there = swap_cores(up_sent)
+    down_kept, down_sent = fold(down_kept, down_there, y_place, 0)
+    grad_middle_b, down_sent = barrier((grad_middle_b, down_sent))
+    down_there = swap_halves(down_sent)
+    out_kept, out_sent = weight_grad(place, attended_t, grad_middle_b, z_count)
+    out_there = swap_cores(out_sent)
+    up_kept, up_sent = fold(bits(up_kept, 1), bits(up_there, 1), by_z[0], len(split))
+    grad_att, up_sent, out_there = barrier((grad_att, up_sent, out_there))
+    up_there = swap_z(up_sent, z_steps[0])
+    grad_q, own, sent = sorted_attend_back(meta, queries, kv, kv_there, attended, grad_att, lse)
+    sent, own, down_there, up_there = barrier((sent, own, down_there, up_there))
+    there = swap_cores(sent)
+    down_kept, down_sent = fold(bits(down_kept, 0), bits(down_there, 0), by_z[0], len(split) - 1)
+    up_kept, up_sent = fold(up_kept, up_there, y_place, 0)
+    there, down_sent, up_sent = barrier((there, down_sent, up_sent))
+    down_there, up_there = swap_z(down_sent, z_steps[0]), swap_halves(up_sent)
+    qkv_kept, qkv_sent = qkv_weight_grad(place, normed_t, grad_q, own, there, z_count)
+    qkv_sent, grad_q, own, there = barrier((qkv_sent, grad_q, own, there))
+    qkv_there = swap_cores(qkv_sent)
+    input_gradient, sums_one = front_back(grad_q, own, there, entry, grad_middle, gain_pair, qkv_t, wide)
+    out_kept, out_sent = fold(out_kept, out_there, y_place, 0)
+    small = jnp.concatenate([sums_one, sums_two, up_sum], axis=0)
+    small = small + swap_cores(small)
+    qkv_kept, qkv_sent = fold(qkv_kept, qkv_there, y_place, 0)
+    qkv_sent, out_sent, small = barrier((qkv_sent, out_sent, small))
+    small_there, qkv_there, out_there = swap_halves(small), swap_halves(qkv_sent), swap_halves(out_sent)
+    down_kept, down_sent = fold(down_kept, down_there, by_z[1], 0)
+    down_there = swap_z(down_sent, z_steps[1])
+    up_kept, up_sent = fold(up_kept, up_there, by_z[1], 0)
+    up_there = swap_z(up_sent, z_steps[1])
+    qkv_kept, qkv_sent = fold(bits(qkv_kept, 0), bits(qkv_there, 0), by_z[0], len(split) - 1)
+    out_kept, out_sent = fold(bits(out_kept, 0), bits(out_there, 0), by_z[0], len(split) - 1)
+    small = small + small_there
+    rounded = input_gradient.astype(narrow)
+    qkv_sent, out_sent, small, rounded = barrier((qkv_sent, out_sent, small, rounded))
+    small_there, qkv_there, out_there = [swap_z(value, z_steps[0]) for value in (small, qkv_sent, out_sent)]
+    grads_there = swap_halves(rounded[rows:])
+    qkv_kept, qkv_sent = fold(qkv_kept, qkv_there, by_z[1], 0)
+    out_kept, out_sent = fold(out_kept, out_there, by_z[1], 0)
+    small = small + small_there
+    qkv_sent, out_sent, small = barrier((qkv_sent, out_sent, small))
+    small_there, qkv_there, out_there = [swap_z(value, z_steps[1]) for value in (small, qkv_sent, out_sent)]
+    wdown = wide_sum(down_kept, down_there)
+    wup = wide_sum(up_kept, up_there)
+    wqkv = wide_sum(qkv_kept, qkv_there)
+    wout = wide_sum(out_kept, out_there)
+    small = small + small_there
+    grads_kept = jnp.where(signed, input_gradient[:rows], rounded[:rows].astype(wide))
+    blocks = count * z_count
+    block_at = lax.axis_index("dp") * count + ctx_at
+    gain_piece = lax.dynamic_slice_in_dim(small[0:5:4], block_at * (D // blocks), D // blocks, 1)
+    bias_rows = [small[1], small[5], small[2], small[3], small[6], small[7], small[8:].reshape(-1)]
+    bias_row = jnp.concatenate(bias_rows)
+    width = bias_row.shape[0] // blocks
+    bias_piece = lax.dynamic_slice_in_dim(bias_row, block_at * width, width, 0)
+    return (
+        returned(result[:rows], acts_there)[None, :, None],
+        returned(grads_kept, grads_there)[None, :, None],
+        gain_piece[None],
+        bias_piece[None],
+        wqkv[None],
+        wout[None],
+        wup[None],
+        wdown[None],
+    )
+
+
+def body_for(mesh):
+    sizes = dict(mesh.shape)
+    return fast_body if (sizes["ctx"], sizes["dp"]) == (4, 4) else general_body
+
+
 def solution(mesh):
     in_specs = (
         P(None, "dp", "ctx", None),
@@ -385,4 +1147,6 @@
         P("section", ("dp", "ctx"), None),
         P("section", ("dp", "ctx"), None),
     )
-    return jax.shard_map(body, mesh=mesh, in_specs=in_specs, out_specs=out_specs, check_vma=False)
+    return jax.shard_map(
+        body_for(mesh), mesh=mesh, in_specs=in_specs, out_specs=out_specs, check_vma=False
+    )

time: 1640 us -> 318 us (0.19)
  matrix products: 636 us -> 2.61 us
  waiting for transfers between devices: 501 us -> 69.2 us
  local copies, waits for them, and re-layouts: 249 us -> 64.3 us
  Pallas kernels: 0 us -> 133 us
  other arithmetic: 126 us -> 11 us
  blocking collectives: 59.9 us -> 0 us
    dot_general x128 -> x1, matrix products: 636 us -> 2.61 us  [dot(): lax.dot_general(left, right, dims, preferred_element_type=jnp.float32)]
    reduce_scatter x12 -> x0, waiting for transfers between devices: 388 us -> none  [the longest x1 117 us: body(): lax.psum_scatter(partial_sums[4], ('dp', 'ctx'), scatter_dimension=0, til...]
    pallas_call x0 -> x27, Pallas kernels: none -> 133 us  [the longest x19 45.2 us: call(): pl.pallas_call(kernel, in_specs=[SMEM_SPEC] * smem + [VMEM_SPEC] * (len(o...]
    reduce_sum x60 -> x2, other arithmetic: 90 us -> 0.33 us  [the longest x1 0.18 us: slot_meta(): jnp.sum((own_pos[None, :] < own_pos[:, None]).astype(jnp.int32), axis=1)]
    all_gather x16 -> x0, waiting for transfers between devices: 83.8 us -> none  [the longest x4 67.3 us: layer_reverse_pass(): lax.all_gather(projected[:, D:2 * D], 'ctx', axis=0, tiled=True)]
    dynamic_slice x72 -> x2, local copies, waits for them, and re-layouts: 66.3 us -> 0.68 us  [the longest x1 0.66 us: fast_body(): bias_piece = lax.dynamic_slice_in_dim(bias_row, block_at * width, width, 0)]
    ppermute x0 -> x28, waiting for transfers between devices: none -> 65.3 us  [the longest x9 29 us: swap_halves(): lax.ppermute(value, 'ctx', [(at, (at + count // 2) % count) for at in ran...]
    dynamic_update_slice x28 -> x0, local copies, waits for them, and re-layouts: 60.8 us -> none  [the longest x24 57.5 us: backward_summed(): lax.scan(step_back, start_q, (key_split, value_split, pos_split))]
  transfers between devices with their start and end apart: 37 -> 30, of which waited for: 17 -> 12; matrix products, arithmetic and copies ran while one was open for 58% -> 15% of each run, Pallas kernels for 0% -> 12%
where the time goes in v2:
time: 318 us; the launch traced here: 314 us
  Pallas kernels  133 us (42%)
  waiting for transfers between devices  69.2 us (22%)
  local copies, waits for them, and re-layouts  64.3 us (20%)
  starting transfers between devices  32.4 us (10%)
  other arithmetic  11 us (3%)
    pallas_call x19, Pallas kernels, call(): pl.pallas_call(kernel, in_specs=[SMEM_SPEC] * smem + [VMEM_SPEC] * (len(o...  45.2 us
    pallas_call x2, Pallas kernels, sorted_attend_back(): pl.pallas_call(functools.partial(backward_kernel, span=span), in_specs=[S...  39.8 us
    pallas_call x2, Pallas kernels, sorted_attend(): pl.pallas_call(functools.partial(forward_kernel, span=span), in_specs=[SM...  34 us
    unnamed x170, local copies, waits for them, and re-layouts  33.8 us
    ppermute x9, waiting for transfers between devices, swap_halves(): lax.ppermute(value, 'ctx', [(at, (at + count // 2) % count) for at in ran...  29 us
    ppermute x10, waiting for transfers between devices, swap_z(): lax.ppermute(value, 'dp', [(at, at ^ step) for at in range(lax.axis_size(...  25.7 us
    ppermute x10, starting transfers between devices, swap_z(): lax.ppermute(value, 'dp', [(at, at ^ step) for at in range(lax.axis_size(...  15.5 us
    optimization_barrier x2, local copies, waits for them, and re-layouts, fast_body(): sent, later = barrier((sent, (cotangent, w_up, w_down)))  13.3 us
  transfers between devices with their start and end apart: 30, of which 12 were waited for; matrix products, arithmetic and copies ran while one was open for 15% of the time, Pallas kernels for 12%

profile of v2, /device:TPU:0, one launch (start us, length us, event | category | flops | bytes accessed | tf_op | source)
XLA Modules:
  0.0 314.3 jit_solution(16234938512920137910)
XLA Ops:
  1.9 2.0 dynamic-slice_bitcast_fusion.3
  4.0 3.0 collective-permute-start
  7.0 5.8 %copy.37 = bf16[1,768,2304]{1,2,0:T(8,128)(2,1)} copy(bf16[1,768,2304]{2,1,0:T(8,128)(2,1)} %w_ref.3) | data formatting | bytes 7077888 | tf_op args[5]
  12.7 2.6 copy.38
  17.6 2.4 front.2
  20.1 3.4 %collective-permute-done.1.kv2_ref = bf16[512,1536]{1,0:T(8,128)(2,1)S(1)} collective-permute-done((bf16[512,1536]{1,0:T(8,128)(2,1)S(1)}, bf16[512,1536]{1,0:T(8,128)(2,1)S(1)}, u32[]{:S(2)}, u32[]{:S(2)}) %collective-permute-start.1) | collective-permute-done | bytes 1572896 | tf_op jit(solution)/shard_map/ppermute | solution.py:933
  23.5 12.1 %attend.2 = (bf16[512,768]{1,0:T(8,128)(2,1)S(1)}, f32[6,4,256]{2,1,0:T(4,128)}) custom-call(s32[17]{0:T(128)S(1)} %concatenate.20.meta, bf16[512,768]{1,0:T(8,128)(2,1)S(1)} %get-tuple-element.128.q_ref, bf16[512,1536]{1,0:T(8,128)(2,1)S(1)} %get-tuple-element.129.kv_ref, bf16[512,1536]{1,0:T(8,128)(2,1)S(1)} %collective-permute-done.1.kv2_ref), custom_call_target="tpu_custom_call" | custom-call | flops 4000000000 | tf_op jit(solution)/shard_map/attend/pallas_call | solution.py:155
  35.6 7.3 %rest.1 = bf16[512,768]{1,0:T(8,128)(2,1)} custom-call(bf16[512,768]{1,0:T(8,128)(2,1)S(1)} %pad_maximum_fusion.x_ref, bf16[512,768]{1,0:T(8,128)(2,1)S(1)} %get-tuple-element.130.o_ref, f32[2,768]{1,0:T(2,128)S(1)} %bitcast.159, f32[1,7680]{1,0:T(1,128)S(1)} %copy-done.46, bf16[1,768,768]{2,1,0:T(8,128)(2,1)S(1)} %copy-done.11, ...), custom_call_target="tpu_custom_call" | custom-call | flops 679477248 | tf_op jit(solution)/shard_map/rest/pallas_call | solution.py:304
  43.0 2.3 collective-permute-start.2
  46.2 1.7 collective-permute-start.3
  47.9 6.6 %copy.39 = bf16[1,768,3072]{1,2,0:T(8,128)(2,1)} copy(bf16[1,768,3072]{2,1,0:T(8,128)(2,1)} %w_up.3) | data formatting | bytes 9437184 | tf_op jit(solution)/shard_map/optimization_barrier | solution.py:1010
  54.5 6.7 %copy.40 = bf16[1,3072,768]{1,2,0:T(8,128)(2,1)} copy(bf16[1,3072,768]{2,1,0:T(8,128)(2,1)} %w_down.1) | data formatting | bytes 9437184 | tf_op jit(solution)/shard_map/optimization_barrier | solution.py:1010
  63.3 2.4 front.3
  66.6 3.4 %collective-permute-done.4.kv2_ref = bf16[512,1536]{1,0:T(8,128)(2,1)S(1)} collective-permute-done((bf16[512,1536]{1,0:T(8,128)(2,1)S(1)}, bf16[512,1536]{1,0:T(8,128)(2,1)S(1)}, u32[]{:S(2)}, u32[]{:S(2)}) %collective-permute-start.4) | collective-permute-done | bytes 1572896 | tf_op jit(solution)/shard_map/ppermute | solution.py:933
  70.0 21.9 %attend.3 = (bf16[512,768]{1,0:T(8,128)(2,1)S(1)}, f32[6,4,256]{2,1,0:T(4,128)S(1)}) custom-call(s32[17]{0:T(128)S(1)} %concatenate.20.meta, bf16[512,768]{1,0:T(8,128)(2,1)S(1)} %get-tuple-element.136.q_ref, bf16[512,1536]{1,0:T(8,128)(2,1)S(1)} %get-tuple-element.137.kv_ref, bf16[512,1536]{1,0:T(8,128)(2,1)S(1)} %collective-permute-done.4.kv2_ref), custom_call_target="tpu_custom_call" | custom-call | flops 4000000000 | tf_op jit(solution)/shard_map/attend/pallas_call | solution.py:155
  92.1 11.6 %turn.1 = (f32[512,768]{1,0:T(8,128)S(1)}, bf16[512,768]{1,0:T(8,128)(2,1)S(1)}, bf16[512,3072]{1,0:T(8,128)(2,1)S(1)}, bf16[512,3072]{1,0:T(8,128)(2,1)S(1)}, f...) custom-call(bf16[512,768]{1,0:T(8,128)(2,1)S(1)} %broadcast_select_fusion.1.x_ref, ...), custom_call_target="tpu_custom_call" | custom-call | flops 1056964608 | tf_op jit(solution)/shard_map/turn/pallas_call | solution.py:304
  103.7 1.6 copy-done.22
  105.4 20.0 %attend_back.2 = (bf16[512,768]{1,0:T(8,128)(2,1)S(1)}, bf16[2,512,768]{2,1,0:T(8,128)(2,1)S(1)}, bf16[2,512,768]{2,1,0:T(8,128)(2,1)S(1)}) custom-call(s32[17]{0:T(128)S(1)} %concatenate.20.meta, bf16[512,768]{1,0:T(8,128)(2,1)S(1)} %get-tuple-element.136.q_ref, bf16[512,1536]{1,0:T(8,128)(2,1)S(1)} %get-tuple-element.137.kv_ref, ...), custom_call_target="tpu_custom_call" | custom-call | flops 8000000000 | tf_op jit(solution)/shard_map/attend_back/pallas_call | solution.py:241
  125.7 3.3 %collective-permute-done.5.there_ref = bf16[2,512,768]{2,1,0:T(8,128)(2,1)S(1)} collective-permute-done((bf16[2,512,768]{2,1,0:T(8,128)(2,1)S(1)}, bf16[2,512,768]{2,1,0:T(8,128)(2,1)S(1)}, u32[]{:S(2)}, u32[]{:S(2)}) %collective-permute-start.5) | collective-permute-done | bytes 1572896 | tf_op jit(solution)/shard_map/ppermute | solution.py:933
  129.0 3.6 %front_back.2 = (bf16[512,768]{1,0:T(8,128)(2,1)}, f32[4,768]{1,0:T(4,128)}) custom-call(bf16[512,768]{1,0:T(8,128)(2,1)S(1)} %get-tuple-element.146.q_ref, bf16[2,512,768]{2,1,0:T(8,128)(2,1)S(1)} %get-tuple-element.147.own_ref, bf16[2,512,768]{2,1,0:T(8,128)(2,1)S(1)} %collective-permute-done.5.there_ref, ...), custom_call_target="tpu_custom_call" | custom-call | flops 226492416 | tf_op jit(solution)/shard_map/front_back/pallas_call | solution.py:304
  134.0 2.6 add_convert_fusion
  138.7 4.8 %copy.41 = bf16[512,3072]{0,1:T(8,128)(2,1)} copy(bf16[512,3072]{1,0:T(8,128)(2,1)} %copy-done.19) | data formatting | bytes 6291456 | tf_op jit(solution)/shard_map/optimization_barrier | solution.py:1029
  143.6 2.3 copy.42
  145.9 2.3 copy.43
  148.2 2.3 copy.44
  150.5 3.9 %collective-permute-done.6 = bf16[512,768]{1,0:T(8,128)(2,1)} collective-permute-done((bf16[512,768]{1,0:T(8,128)(2,1)}, bf16[512,768]{1,0:T(8,128)(2,1)}, u32[]{:S(2)}, u32[]{:S(2)}) %collective-permute-start.6) | collective-permute-done | bytes 786464 | tf_op jit(solution)/shard_map/ppermute | solution.py:575
  155.6 2.3 copy-done.2
  158.0 2.3 copy-done.3
  160.3 1.9 copy-done.23
  163.6 6.8 %down_back.1 = (bf16[512,3072]{1,0:T(8,128)(2,1)S(1)}, f32[512,768]{1,0:T(8,128)S(1)}, bf16[512,768]{1,0:T(8,128)(2,1)S(1)}, bf16[512,768]{1,0:T(8,128)(2,1)S(1)...) custom-call(bf16[512,768]{1,0:T(8,128)(2,1)S(1)} %broadcast_select_fusion.d_ref.right_ref, ...), custom_call_target="tpu_custom_call" | custom-call | flops 679477248 | tf_op jit(solution)/shard_map/down_back/pallas_call | solution.py:304
  171.4 3.9 %weight_grad.3 = (bf16[2,4,192,768]{3,2,1,0:T(8,128)(2,1)S(1)}, bf16[2,4,192,768]{3,2,1,0:T(8,128)(2,1)S(1)}) custom-call(s32[1]{0:T(128)} %bitcast.27.place, bf16[3072,512]{1,0:T(8,128)(2,1)S(1)} %bitcast.134, bf16[512,768]{1,0:T(8,128)(2,1)S(1)} %broadcast_select_fusion.d_ref.right_ref), custom_call_target="tpu_custom_call" | custom-call | flops 301989888 | tf_op jit(solution)/shard_map/weight_grad/pallas_call | solution.py:557
  175.4 4.9 %weight_grad.4 = (bf16[2,4,48,3072]{3,2,1,0:T(8,128)(2,1)S(1)}, bf16[2,4,48,3072]{3,2,1,0:T(8,128)(2,1)}) custom-call(s32[1]{0:T(128)} %bitcast.27.place, bf16[768,512]{1,0:T(8,128)(2,1)S(1)} %bitcast.139, bf16[512,3072]{1,0:T(8,128)(2,1)S(1)} %get-tuple-element.171.right_ref), custom_call_target="tpu_custom_call" | custom-call | flops 301989888 | tf_op jit(solution)/shard_map/weight_grad/pallas_call | solution.py:557
  183.8 1.7 weight_grad.5
  187.3 1.7 copy-done.27
  189.0 2.4 fold.12
  191.4 1.6 collective-permute-start.12
  194.9 19.8 %attend_back.3 = (bf16[512,768]{1,0:T(8,128)(2,1)S(1)}, bf16[2,512,768]{2,1,0:T(8,128)(2,1)S(1)}, bf16[2,512,768]{2,1,0:T(8,128)(2,1)S(1)}) custom-call(s32[17]{0:T(128)S(1)} %concatenate.20.meta, bf16[512,768]{1,0:T(8,128)(2,1)S(1)} %copy-done.61, bf16[512,1536]{1,0:T(8,128)(2,1)S(1)} %copy-done.56, bf16[512,1536]{1,0:T(8,128)(2,1)S(1)} %copy-done.58, ...), custom_call_target="tpu_custom_call" | custom-call | flops 8000000000 | tf_op jit(solution)/shard_map/attend_back/pallas_call | solution.py:241
  214.9 4.1 %collective-permute-done.12 = bf16[2,2,48,3072]{3,2,1,0:T(8,128)(2,1)S(1)} collective-permute-done((bf16[2,2,48,3072]{3,2,1,0:T(8,128)(2,1)S(1)}, bf16[2,2,48,3072]{3,2,1,0:T(8,128)(2,1)S(1)}, u32[]{:S(2)}, u32[]{:S(2)}) %collective-permute-start.12) | collective-permute-done | bytes 1179680 | tf_op jit(solution)/shard_map/ppermute | solution.py:937
  222.5 3.4 %qkv_weight_grad.1 = (bf16[2,4,48,2304]{3,2,1,0:T(8,128)(2,1)S(1)}, bf16[2,4,48,2304]{3,2,1,0:T(8,128)(2,1)S(1)}) custom-call(s32[1]{0:T(128)} %bitcast.27.place, bf16[768,512]{1,0:T(8,128)(2,1)S(1)} %bitcast.137, bf16[512,768]{1,0:T(8,128)(2,1)S(1)} %get-tuple-element.200.q_ref, bf16[2,512,768]{2,1,0:T(8,128)(2,1)S(1)} %get-tuple-element.201.own_ref, ...), custom_call_target="tpu_custom_call" | custom-call | flops 226492416 | tf_op jit(solution)/shard_map/qkv_weight_grad/pallas_call | solution.py:524
  226.2 2.7 front_back.3
  235.1 1.6 collective-permute-start.28
  236.7 10.4 %collective-permute-done.26 = bf16[2,48,3072]{2,1,0:T(8,128)(2,1)S(1)} collective-permute-done((bf16[2,48,3072]{2,1,0:T(8,128)(2,1)}, bf16[2,48,3072]{2,1,0:T(8,128)(2,1)S(1)}, u32[]{:S(2)}, u32[]{:S(2)}) %collective-permute-start.26) | collective-permute-done | bytes 589856 | tf_op jit(solution)/shard_map/ppermute | solution.py:929
  247.3 2.6 collective-permute-start.27
  255.8 17.2 %collective-permute-done.18 = f32[12,768]{1,0:T(8,128)S(1)} collective-permute-done((f32[12,768]{1,0:T(8,128)S(1)}, f32[12,768]{1,0:T(8,128)S(1)}, u32[]{:S(2)}, u32[]{:S(2)}) %collective-permute-start.18) | collective-permute-done | bytes 36896 | tf_op jit(solution)/shard_map/ppermute | solution.py:929
  282.4 11.2 %collective-permute-done.22 = f32[12,768]{1,0:T(8,128)S(1)} collective-permute-done((f32[12,768]{1,0:T(8,128)S(1)}, f32[12,768]{1,0:T(8,128)S(1)}, u32[]{:S(2)}, u32[]{:S(2)}) %collective-permute-start.22) | collective-permute-done | bytes 36896 | tf_op jit(solution)/shard_map/ppermute | solution.py:937
  293.9 2.6 collective-permute-start.23
  298.1 2.6 collective-permute-start.25
  302.2 10.4 %collective-permute-done.25 = bf16[48,768]{1,0:T(8,128)(2,1)S(1)} collective-permute-done((bf16[48,768]{1,0:T(8,128)(2,1)S(1)}, bf16[48,768]{1,0:T(8,128)(2,1)S(1)}, u32[]{:S(2)}, u32[]{:S(2)}) %collective-permute-start.25) | collective-permute-done | bytes 73760 | tf_op jit(solution)/shard_map/ppermute | solution.py:937
  (260 shorter events, 52.1 us)
Async XLA Ops:
  4.0 12.4 %collective-permute-start = (bf16[256,768]{1,0:T(8,128)(2,1)}, bf16[256,768]{1,0:T(8,128)(2,1)}, u32[]{:S(2)}, u32[]{:S(2)}) collective-permute-start(bf16[256,768]{1,0:T(8,128)(2,1)} %get-tuple-element.281), channel_id=1, source_target_pairs={{0,2},{1,3},{2,0},{3,1},{4,6},{5,7},{6,4},{7,5},{8,10},{9,11},{10,... | collective-permute-start | bytes 1179656 | tf_op jit(solution)/shard_map/ppermute | solution.py:929
  20.0 3.5 %collective-permute-start.1 = (bf16[512,1536]{1,0:T(8,128)(2,1)S(1)}, bf16[512,1536]{1,0:T(8,128)(2,1)S(1)}, u32[]{:S(2)}, u32[]{:S(2)}) collective-permute-start(bf16[512,1536]{1,0:T(8,128)(2,1)S(1)} %get-tuple-element.129.kv_ref), channel_id=1, source_target_pairs={{0,1},{1,0},{2,3},{3,2},{4,5},{5,4},{6,7},{7,6},{8,9},{9,8},{10,11... | collective-permute-start | bytes 4718600 | tf_op jit(solution)/shard_map/ppermute | solution.py:933
  43.0 19.5 %collective-permute-start.2 = (bf16[512,768]{1,0:T(8,128)(2,1)}, bf16[512,768]{1,0:T(8,128)(2,1)}, u32[]{:S(2)}, u32[]{:S(2)}) collective-permute-start(bf16[512,768]{1,0:T(8,128)(2,1)} %rest.1), channel_id=1, source_target_pairs={{0,16},{1,17},{2,18},{3,19},{4,20},{5,21},{6,22},{7,23},{8,24},{9,... | collective-permute-start | bytes 2359304 | tf_op jit(solution)/shard_map/ppermute | solution.py:575
  46.2 15.1 %collective-permute-start.3 = (bf16[256,768]{1,0:T(8,128)(2,1)}, bf16[256,768]{1,0:T(8,128)(2,1)}, u32[]{:S(2)}, u32[]{:S(2)}) collective-permute-start(bf16[256,768]{1,0:T(8,128)(2,1)} %get-tuple-element.279), channel_id=1, source_target_pairs={{0,2},{1,3},{2,0},{3,1},{4,6},{5,7},{6,4},{7,5},{8,10},{9,11},{10,... | collective-permute-start | bytes 1179656 | tf_op jit(solution)/shard_map/ppermute | solution.py:929
  62.5 29.5 %copy-start.15 = (bf16[512,768]{1,0:T(8,128)(2,1)}, bf16[512,768]{1,0:T(8,128)(2,1)S(1)}, u32[]{:S(2)}) copy-start(bf16[512,768]{1,0:T(8,128)(2,1)S(1)} %pad_maximum_fusion.1.d_ref) | copy-start | bytes 2359300
  63.3 65.7 %copy-start.6 = (bf16[512,768]{1,0:T(8,128)(2,1)}, bf16[512,768]{1,0:T(8,128)(2,1)S(1)}, u32[]{:S(2)}) copy-start(bf16[512,768]{1,0:T(8,128)(2,1)S(1)} %broadcast_select_fusion.1.x_ref) | copy-start | bytes 2359300
  63.3 28.7 %slice-start = ((s8[4718592]{0:T(1024)(128)(4,1)}), s8[4194304]{0:T(1024)(128)(4,1)S(1)}, s32[]{:S(2)}) async-start(s8[4718592]{0:T(1024)(128)(4,1)} %bitcast.116), calls=%async_computation | async-start | bytes 8388608
  63.3 28.7 %slice-start.2 = ((s8[4718592]{0:T(1024)(128)(4,1)}), s8[4194304]{0:T(1024)(128)(4,1)S(1)}, s32[]{:S(2)}) async-start(s8[4718592]{0:T(1024)(128)(4,1)} %bitcast.120), calls=%async_computation.2 | async-start | bytes 8388608
  63.3 28.7 %slice-start.6 = ((s8[4718592]{0:T(1024)(128)(4,1)}), s8[4194304]{0:T(1024)(128)(4,1)S(1)}, s32[]{:S(2)}) async-start(s8[4718592]{0:T(1024)(128)(4,1)} %bitcast.126), calls=%async_computation.6 | async-start | bytes 8388608
  66.6 38.8 %copy-start.55 = (bf16[512,1536]{1,0:T(8,128)(2,1)}, bf16[512,1536]{1,0:T(8,128)(2,1)S(1)}, u32[]{:S(2)}) copy-start(bf16[512,1536]{1,0:T(8,128)(2,1)S(1)} %get-tuple-element.137.kv_ref) | copy-start | bytes 4718596
  66.6 38.8 %copy-start.60 = (bf16[512,768]{1,0:T(8,128)(2,1)}, bf16[512,768]{1,0:T(8,128)(2,1)S(1)}, u32[]{:S(2)}) copy-start(bf16[512,768]{1,0:T(8,128)(2,1)S(1)} %get-tuple-element.136.q_ref) | copy-start | bytes 2359300
  66.6 3.4 %collective-permute-start.4 = (bf16[512,1536]{1,0:T(8,128)(2,1)S(1)}, bf16[512,1536]{1,0:T(8,128)(2,1)S(1)}, u32[]{:S(2)}, u32[]{:S(2)}) collective-permute-start(bf16[512,1536]{1,0:T(8,128)(2,1)S(1)} %get-tuple-element.137.kv_ref), channel_id=1, source_target_pairs={{0,1},{1,0},{2,3},{3,2},{4,5},{5,4},{6,7},{7,6},{8,9},{9,8},{10,11... | collective-permute-start | bytes 4718600 | tf_op jit(solution)/shard_map/ppermute | solution.py:933
  70.0 35.4 %copy-start.57 = (bf16[512,1536]{1,0:T(8,128)(2,1)}, bf16[512,1536]{1,0:T(8,128)(2,1)S(1)}, u32[]{:S(2)}) copy-start(bf16[512,1536]{1,0:T(8,128)(2,1)S(1)} %collective-permute-done.4.kv2_ref) | copy-start | bytes 4718596
  70.0 22.0 %slice-start.3 = ((s8[4718592]{0:T(1024)(128)(4,1)}), s8[524288]{0:T(1024)(128)(4,1)S(1)}, s32[]{:S(2)}) async-start(s8[4718592]{0:T(1024)(128)(4,1)} %bitcast.120), calls=%async_computation.3 | async-start | bytes 1048576
  70.0 22.0 %slice-start.7 = ((s8[4718592]{0:T(1024)(128)(4,1)}), s8[524288]{0:T(1024)(128)(4,1)S(1)}, s32[]{:S(2)}) async-start(s8[4718592]{0:T(1024)(128)(4,1)} %bitcast.126), calls=%async_computation.7 | async-start | bytes 1048576
  70.0 22.0 %copy-start.12 = (bf16[1,768,768]{2,1,0:T(8,128)(2,1)S(1)}, bf16[1,768,768]{2,1,0:T(8,128)(2,1)}, u32[]{:S(2)}) copy-start(bf16[1,768,768]{2,1,0:T(8,128)(2,1)} %w_out.3) | copy-start | bytes 3538948
  70.0 22.0 %copy-start.13 = (bf16[1,768,768]{1,2,0:T(8,128)(2,1)S(1)}, bf16[1,768,768]{1,2,0:T(8,128)(2,1)}, u32[]{:S(2)}) copy-start(bf16[1,768,768]{1,2,0:T(8,128)(2,1)} %copy.38) | copy-start | bytes 3538948
  92.1 41.8 %slice-start.10 = ((s8[4718592]{0:T(1024)(128)(4,1)}), s8[524288]{0:T(1024)(128)(4,1)S(1)}, s32[]{:S(2)}) async-start(s8[4718592]{0:T(1024)(128)(4,1)} %bitcast.132), calls=%async_computation.10 | async-start | bytes 1048576
  105.4 28.5 %copy-start.19 = (bf16[512,3072]{1,0:T(8,128)(2,1)}, bf16[512,3072]{1,0:T(8,128)(2,1)S(1)}, u32[]{:S(2)}) copy-start(bf16[512,3072]{1,0:T(8,128)(2,1)S(1)} %get-tuple-element.155) | copy-start | bytes 9437188
  105.4 28.5 %copy-start.30 = (f32[512,768]{1,0:T(8,128)}, f32[512,768]{1,0:T(8,128)S(1)}, u32[]{:S(2)}) copy-start(f32[512,768]{1,0:T(8,128)S(1)} %get-tuple-element.143.middle_ref) | copy-start | bytes 4718596
  105.4 23.5 %copy-start.5 = (bf16[1,768,2304]{1,2,0:T(8,128)(2,1)S(1)}, bf16[1,768,2304]{1,2,0:T(8,128)(2,1)}, u32[]{:S(2)}) copy-start(bf16[1,768,2304]{1,2,0:T(8,128)(2,1)} %copy.37) | copy-start | bytes 10616836
  105.4 28.5 %slice-start.11 = ((s8[4718592]{0:T(1024)(128)(4,1)}), s8[4194304]{0:T(1024)(128)(4,1)S(1)}, s32[]{:S(2)}) async-start(s8[4718592]{0:T(1024)(128)(4,1)} %bitcast.132), calls=%async_computation.11 | async-start | bytes 8388608
  125.5 3.5 %collective-permute-start.5 = (bf16[2,512,768]{2,1,0:T(8,128)(2,1)S(1)}, bf16[2,512,768]{2,1,0:T(8,128)(2,1)S(1)}, u32[]{:S(2)}, u32[]{:S(2)}) collective-permute-start(bf16[2,512,768]{2,1,0:T(8,128)(2,1)S(1)} %get-tuple-element.148), channel_id=1, source_target_pairs={{0,1},{1,0},{2,3},{3,2},{4,5},{5,4},{6,7},{7,6},{8,9},{9,8},{10,11... | collective-permute-start | bytes 4718600 | tf_op jit(solution)/shard_map/ppermute | solution.py:933
  132.6 21.8 %collective-permute-start.6 = (bf16[512,768]{1,0:T(8,128)(2,1)}, bf16[512,768]{1,0:T(8,128)(2,1)}, u32[]{:S(2)}, u32[]{:S(2)}) collective-permute-start(bf16[512,768]{1,0:T(8,128)(2,1)} %get-tuple-element.156), channel_id=1, source_target_pairs={{16,0},{17,1},{18,2},{19,3},{20,4},{21,5},{22,6},{23,7},{24,8},{25... | collective-permute-start | bytes 2359304 | tf_op jit(solution)/shard_map/ppermute | solution.py:575
  138.2 12.3 %collective-permute-start.7 = (bf16[256,768]{1,0:T(8,128)(2,1)}, bf16[256,768]{1,0:T(8,128)(2,1)}, u32[]{:S(2)}, u32[]{:S(2)}) collective-permute-start(bf16[256,768]{1,0:T(8,128)(2,1)} %slice.57), channel_id=1, source_target_pairs={{0,2},{1,3},{2,0},{3,1},{4,6},{5,7},{6,4},{7,5},{8,10},{9,11},{10,... | collective-permute-start | bytes 1179656 | tf_op jit(solution)/shard_map/ppermute | solution.py:929
  175.3 5.4 %collective-permute-start.9 = (bf16[2,4,192,768]{3,2,1,0:T(8,128)(2,1)S(1)}, bf16[2,4,192,768]{3,2,1,0:T(8,128)(2,1)S(1)}, u32[]{:S(2)}, u32[]{:S(2)}) collective-permute-start(bf16[2,4,192,768]{3,2,1,0:T(8,128)(2,1)S(1)} %get-tuple-element.180), channel_id=1, source_target_pairs={{0,1},{1,0},{2,3},{3,2},{4,5},{5,4},{6,7},{7,6},{8,9},{9,8},{10,11... | collective-permute-start | bytes 7077896 | tf_op jit(solution)/shard_map/ppermute | solution.py:933
  180.3 7.0 %collective-permute-start.8 = (bf16[2,4,48,3072]{3,2,1,0:T(8,128)(2,1)}, bf16[2,4,48,3072]{3,2,1,0:T(8,128)(2,1)}, u32[]{:S(2)}, u32[]{:S(2)}) collective-permute-start(bf16[2,4,48,3072]{3,2,1,0:T(8,128)(2,1)} %get-tuple-element.175), channel_id=1, source_target_pairs={{0,1},{1,0},{2,3},{3,2},{4,5},{5,4},{6,7},{7,6},{8,9},{9,8},{10,11... | collective-permute-start | bytes 7077896 | tf_op jit(solution)/shard_map/ppermute | solution.py:933
  186.4 5.0 %collective-permute-start.10 = (bf16[2,4,48,768]{3,2,1,0:T(8,128)(2,1)}, bf16[2,4,48,768]{3,2,1,0:T(8,128)(2,1)}, u32[]{:S(2)}, u32[]{:S(2)}) collective-permute-start(bf16[2,4,48,768]{3,2,1,0:T(8,128)(2,1)} %get-tuple-element.183), channel_id=1, source_target_pairs={{0,1},{1,0},{2,3},{3,2},{4,5},{5,4},{6,7},{7,6},{8,9},{9,8},{10,11... | collective-permute-start | bytes 1769480 | tf_op jit(solution)/shard_map/ppermute | solution.py:933
  186.8 28.1 %collective-permute-start.11 = (bf16[4,192,768]{2,1,0:T(8,128)(2,1)}, bf16[4,192,768]{2,1,0:T(8,128)(2,1)S(1)}, u32[]{:S(2)}, u32[]{:S(2)}) collective-permute-start(bf16[4,192,768]{2,1,0:T(8,128)(2,1)} %bitcast.169), channel_id=1, source_target_pairs={{0,2},{1,3},{2,0},{3,1},{4,6},{5,7},{6,4},{7,5},{8,10},{9,11},{10,... | collective-permute-start | bytes 3538952 | tf_op jit(solution)/shard_map/ppermute | solution.py:929
  191.4 27.7 %copy-start.33 = (bf16[1,768,768]{2,1,0:T(8,128)(2,1)S(1)}, bf16[1,768,768]{2,1,0:T(8,128)(2,1)}, u32[]{:S(2)}) copy-start(bf16[1,768,768]{2,1,0:T(8,128)(2,1)} %copy-done.32) | copy-start | bytes 3538948
  191.4 27.7 %collective-permute-start.12 = (bf16[2,2,48,3072]{3,2,1,0:T(8,128)(2,1)S(1)}, bf16[2,2,48,3072]{3,2,1,0:T(8,128)(2,1)S(1)}, u32[]{:S(2)}, u32[]{:S(2)}) collective-permute-start(bf16[2,2,48,3072]{3,2,1,0:T(8,128)(2,1)S(1)} %bitcast.170), channel_id=1, source_target_pairs={{0,4},{4,0},{8,12},{12,8},{1,5},{5,1},{9,13},{13,9},{2,6},{6,2},{1... | collective-permute-start | bytes 3538952 | tf_op jit(solution)/shard_map/ppermute | solution.py:937
  219.1 3.4 %collective-permute-start.13 = (bf16[2,512,768]{2,1,0:T(8,128)(2,1)S(1)}, bf16[2,512,768]{2,1,0:T(8,128)(2,1)S(1)}, u32[]{:S(2)}, u32[]{:S(2)}) collective-permute-start(bf16[2,512,768]{2,1,0:T(8,128)(2,1)S(1)} %get-tuple-element.191), channel_id=1, source_target_pairs={{0,1},{1,0},{2,3},{3,2},{4,5},{5,4},{6,7},{7,6},{8,9},{9,8},{10,11... | collective-permute-start | bytes 4718600 | tf_op jit(solution)/shard_map/ppermute | solution.py:933
  226.0 6.4 %collective-permute-start.14 = (bf16[2,4,48,2304]{3,2,1,0:T(8,128)(2,1)S(1)}, bf16[2,4,48,2304]{3,2,1,0:T(8,128)(2,1)S(1)}, u32[]{:S(2)}, u32[]{:S(2)}) collective-permute-start(bf16[2,4,48,2304]{3,2,1,0:T(8,128)(2,1)S(1)} %get-tuple-element.206), channel_id=1, source_target_pairs={{0,1},{1,0},{2,3},{3,2},{4,5},{5,4},{6,7},{7,6},{8,9},{9,8},{10,11... | collective-permute-start | bytes 5308424 | tf_op jit(solution)/shard_map/ppermute | solution.py:933
  229.0 3.3 %collective-permute-start.15 = (f32[12,768]{1,0:T(8,128)S(1)}, f32[12,768]{1,0:T(8,128)S(1)}, u32[]{:S(2)}, u32[]{:S(2)}) collective-permute-start(f32[12,768]{1,0:T(8,128)S(1)} %pad_maximum_fusion.2), channel_id=1, source_target_pairs={{0,1},{1,0},{2,3},{3,2},{4,5},{5,4},{6,7},{7,6},{8,9},{9,8},{10,11... | collective-permute-start | bytes 110600 | tf_op jit(solution)/shard_map/ppermute | solution.py:933
  230.7 16.4 %collective-permute-start.26 = (bf16[2,48,3072]{2,1,0:T(8,128)(2,1)}, bf16[2,48,3072]{2,1,0:T(8,128)(2,1)S(1)}, u32[]{:S(2)}, u32[]{:S(2)}) collective-permute-start(bf16[2,48,3072]{2,1,0:T(8,128)(2,1)} %bitcast.40), channel_id=1, source_target_pairs={{0,2},{1,3},{2,0},{3,1},{4,6},{5,7},{6,4},{7,5},{8,10},{9,11},{10,... | collective-permute-start | bytes 1769480 | tf_op jit(solution)/shard_map/ppermute | solution.py:929
  234.6 38.5 %collective-permute-start.16 = (bf16[4,48,2304]{2,1,0:T(8,128)(2,1)}, bf16[4,48,2304]{2,1,0:T(8,128)(2,1)S(1)}, u32[]{:S(2)}, u32[]{:S(2)}) collective-permute-start(bf16[4,48,2304]{2,1,0:T(8,128)(2,1)} %bitcast.44), channel_id=1, source_target_pairs={{0,2},{1,3},{2,0},{3,1},{4,6},{5,7},{6,4},{7,5},{8,10},{9,11},{10,... | collective-permute-start | bytes 2654216 | tf_op jit(solution)/shard_map/ppermute | solution.py:929
  235.1 19.1 %collective-permute-start.28 = (bf16[2,192,768]{2,1,0:T(8,128)(2,1)}, bf16[2,192,768]{2,1,0:T(8,128)(2,1)S(1)}, u32[]{:S(2)}, u32[]{:S(2)}) collective-permute-start(bf16[2,192,768]{2,1,0:T(8,128)(2,1)} %get-tuple-element.239), channel_id=1, source_target_pairs={{0,4},{4,0},{8,12},{12,8},{1,5},{5,1},{9,13},{13,9},{2,6},{6,2},{1... | collective-permute-start | bytes 1769480 | tf_op jit(solution)/shard_map/ppermute | solution.py:937
  247.3 29.7 %collective-permute-start.27 = (bf16[48,3072]{1,0:T(8,128)(2,1)S(1)}, bf16[48,3072]{1,0:T(8,128)(2,1)S(1)}, u32[]{:S(2)}, u32[]{:S(2)}) collective-permute-start(bf16[48,3072]{1,0:T(8,128)(2,1)S(1)} %bitcast.172), channel_id=1, source_target_pairs={{0,8},{4,12},{8,0},{12,4},{1,9},{5,13},{9,1},{13,5},{2,10},{6,14},... | collective-permute-start | bytes 884744 | tf_op jit(solution)/shard_map/ppermute | solution.py:937
  249.9 23.1 %collective-permute-start.17 = (bf16[4,48,768]{2,1,0:T(8,128)(2,1)}, bf16[4,48,768]{2,1,0:T(8,128)(2,1)S(1)}, u32[]{:S(2)}, u32[]{:S(2)}) collective-permute-start(bf16[4,48,768]{2,1,0:T(8,128)(2,1)} %bitcast.171), channel_id=1, source_target_pairs={{0,2},{1,3},{2,0},{3,1},{4,6},{5,7},{6,4},{7,5},{8,10},{9,11},{10,... | collective-permute-start | bytes 884744 | tf_op jit(solution)/shard_map/ppermute | solution.py:929
  252.6 20.4 %collective-permute-start.18 = (f32[12,768]{1,0:T(8,128)S(1)}, f32[12,768]{1,0:T(8,128)S(1)}, u32[]{:S(2)}, u32[]{:S(2)}) collective-permute-start(f32[12,768]{1,0:T(8,128)S(1)} %fusion.16), channel_id=1, source_target_pairs={{0,2},{1,3},{2,0},{3,1},{4,6},{5,7},{6,4},{7,5},{8,10},{9,11},{10,... | collective-permute-start | bytes 110600 | tf_op jit(solution)/shard_map/ppermute | solution.py:929
  255.4 26.1 %collective-permute-start.29 = (bf16[192,768]{1,0:T(8,128)(2,1)S(1)}, bf16[192,768]{1,0:T(8,128)(2,1)S(1)}, u32[]{:S(2)}, u32[]{:S(2)}) collective-permute-start(bf16[192,768]{1,0:T(8,128)(2,1)S(1)} %bitcast.173), channel_id=1, source_target_pairs={{0,8},{4,12},{8,0},{12,4},{1,9},{5,13},{9,1},{13,5},{2,10},{6,14},... | collective-permute-start | bytes 884744 | tf_op jit(solution)/shard_map/ppermute | solution.py:937
  275.4 18.2 %collective-permute-start.19 = (bf16[256,768]{1,0:T(8,128)(2,1)S(1)}, bf16[256,768]{1,0:T(8,128)(2,1)S(1)}, u32[]{:S(2)}, u32[]{:S(2)}) collective-permute-start(bf16[256,768]{1,0:T(8,128)(2,1)S(1)} %slice.47), channel_id=1, source_target_pairs={{0,2},{1,3},{2,0},{3,1},{4,6},{5,7},{6,4},{7,5},{8,10},{9,11},{10,... | collective-permute-start | bytes 1179656 | tf_op jit(solution)/shard_map/ppermute | solution.py:929
  277.9 15.9 %collective-permute-start.20 = (bf16[2,48,2304]{2,1,0:T(8,128)(2,1)S(1)}, bf16[2,48,2304]{2,1,0:T(8,128)(2,1)S(1)}, u32[]{:S(2)}, u32[]{:S(2)}) collective-permute-start(bf16[2,48,2304]{2,1,0:T(8,128)(2,1)S(1)} %get-tuple-element.223), channel_id=1, source_target_pairs={{0,4},{4,0},{8,12},{12,8},{1,5},{5,1},{9,13},{13,9},{2,6},{6,2},{1... | collective-permute-start | bytes 1327112 | tf_op jit(solution)/shard_map/ppermute | solution.py:937
  279.5 14.1 %collective-permute-start.21 = (bf16[2,48,768]{2,1,0:T(8,128)(2,1)S(1)}, bf16[2,48,768]{2,1,0:T(8,128)(2,1)S(1)}, u32[]{:S(2)}, u32[]{:S(2)}) collective-permute-start(bf16[2,48,768]{2,1,0:T(8,128)(2,1)S(1)} %get-tuple-element.226), channel_id=1, source_target_pairs={{0,4},{4,0},{8,12},{12,8},{1,5},{5,1},{9,13},{13,9},{2,6},{6,2},{1... | collective-permute-start | bytes 442376 | tf_op jit(solution)/shard_map/ppermute | solution.py:937
  279.9 13.6 %collective-permute-start.22 = (f32[12,768]{1,0:T(8,128)S(1)}, f32[12,768]{1,0:T(8,128)S(1)}, u32[]{:S(2)}, u32[]{:S(2)}) collective-permute-start(f32[12,768]{1,0:T(8,128)S(1)} %add.103), channel_id=1, source_target_pairs={{0,4},{4,0},{8,12},{12,8},{1,5},{5,1},{9,13},{13,9},{2,6},{6,2},{1... | collective-permute-start | bytes 110600 | tf_op jit(solution)/shard_map/ppermute | solution.py:937
  293.9 6.8 %collective-permute-start.23 = (f32[12,768]{1,0:T(8,128)S(1)}, f32[12,768]{1,0:T(8,128)S(1)}, u32[]{:S(2)}, u32[]{:S(2)}) collective-permute-start(f32[12,768]{1,0:T(8,128)S(1)} %add.104), channel_id=1, source_target_pairs={{0,8},{4,12},{8,0},{12,4},{1,9},{5,13},{9,1},{13,5},{2,10},{6,14},... | collective-permute-start | bytes 110600 | tf_op jit(solution)/shard_map/ppermute | solution.py:937
  297.8 15.5 %collective-permute-start.24 = (bf16[48,2304]{1,0:T(8,128)(2,1)S(1)}, bf16[48,2304]{1,0:T(8,128)(2,1)S(1)}, u32[]{:S(2)}, u32[]{:S(2)}) collective-permute-start(bf16[48,2304]{1,0:T(8,128)(2,1)S(1)} %bitcast.174), channel_id=1, source_target_pairs={{0,8},{4,12},{8,0},{12,4},{1,9},{5,13},{9,1},{13,5},{2,10},{6,14},... | collective-permute-start | bytes 663560 | tf_op jit(solution)/shard_map/ppermute | solution.py:937
  298.1 14.5 %collective-permute-start.25 = (bf16[48,768]{1,0:T(8,128)(2,1)S(1)}, bf16[48,768]{1,0:T(8,128)(2,1)S(1)}, u32[]{:S(2)}, u32[]{:S(2)}) collective-permute-start(bf16[48,768]{1,0:T(8,128)(2,1)S(1)} %bitcast.175), channel_id=1, source_target_pairs={{0,8},{4,12},{8,0},{12,4},{1,9},{5,13},{9,1},{13,5},{2,10},{6,14},... | collective-permute-start | bytes 221192 | tf_op jit(solution)/shard_map/ppermute | solution.py:937
  (63 other events, 367.2 us)

commit v3 on v2

--- a/solution.py
+++ b/solution.py
@@ -16,6 +16,7 @@
 CHUNK = 128
 BACK_CHUNK = 1024
 SAFE = 60.0
+IDLE = 2
 NT = (((1,), (1,)), ((), ()))
 TN = (((0,), (0,)), ((), ()))
 NN = (((1,), (0,)), ((), ()))
@@ -145,6 +146,10 @@
             pl.when(chosen)(functools.partial(run, signed, safe))
 
 
+def in_vmem(*values):
+    return [pltpu.with_memory_space_constraint(value, pltpu.VMEM) for value in values]
+
+
 SMEM_SPEC = pl.BlockSpec(memory_space=pltpu.SMEM)
 VMEM_SPEC = pl.BlockSpec(memory_space=pltpu.VMEM)
 
@@ -161,10 +166,10 @@
             jax.ShapeDtypeStruct((rows, D), jnp.bfloat16),
             jax.ShapeDtypeStruct((PAIRS, OWN, 2 * span), jnp.float32),
         ],
-        compiler_params=pltpu.CompilerParams(vmem_limit_bytes=12 * 1024 * 1024),
+        compiler_params=pltpu.CompilerParams(vmem_limit_bytes=10 * 1024 * 1024),
         cost_estimate=pl.CostEstimate(flops=4_000_000_000, bytes_accessed=0, transcendentals=0),
         name="attend",
-    )(meta, queries, kv, kv_other)
+    )(meta, *in_vmem(queries, kv, kv_other))
 
 
 def backward_kernel(
@@ -234,6 +239,11 @@
     for signed in (True, False):
         pl.when(meta[4 * OWN] == int(signed))(functools.partial(run, signed))
 
+    @pl.when(meta[4 * OWN] == IDLE)
+    def _():
+        for out_ref in (dq_ref, own_ref, other_ref):
+            out_ref[...] = jnp.zeros_like(out_ref)
+
 
 def sorted_attend_back(meta, queries, kv, kv_other, attended, grad_att, lse):
     rows = kv.shape[0]
@@ -249,10 +259,10 @@
             jax.ShapeDtypeStruct((2, rows, D), jnp.bfloat16),
             jax.ShapeDtypeStruct((2, rows, D), jnp.bfloat16),
         ],
-        compiler_params=pltpu.CompilerParams(vmem_limit_bytes=18 * 1024 * 1024),
+        compiler_params=pltpu.CompilerParams(vmem_limit_bytes=10 * 1024 * 1024),
         cost_estimate=pl.CostEstimate(flops=8_000_000_000, bytes_accessed=0, transcendentals=0),
         name="attend_back",
-    )(meta, queries, kv, kv_other, attended, grad_att, lse)
+    )(meta, *in_vmem(queries, kv, kv_other, attended, grad_att), lse)
 
 
 TURN_TANH = 0.7978845608028654
@@ -294,21 +304,27 @@
     return hidden * (0.5 + 0.5 * curve)
 
 
-def cost(flops, nbytes):
+def cost(flops):
     return pl.CostEstimate(flops=int(flops) // 8, bytes_accessed=0, transcendentals=0)
 
 
+def in_hbm(value):
+    return pltpu.with_memory_space_constraint(value, pltpu.HBM)
+
+
+def placed(shape, dtype, space=None):
+    return jax.ShapeDtypeStruct(shape, dtype) if space is None else space(shape, dtype)
+
+
 def call(kernel, name, megabytes, flops, outs, scratch, *operands, smem=0):
-    shapes = [jax.ShapeDtypeStruct(shape, dtype) for shape, dtype in outs]
-    nbytes = sum(value.size * value.dtype.itemsize for value in (*operands, *shapes))
     return pl.pallas_call(
         kernel,
         in_specs=[SMEM_SPEC] * smem + [VMEM_SPEC] * (len(operands) - smem),
-        out_specs=[VMEM_SPEC] * len(shapes),
-        out_shape=shapes,
+        out_specs=[VMEM_SPEC] * len(outs),
+        out_shape=[placed(*out) for out in outs],
         scratch_shapes=scratch,
         compiler_params=pltpu.CompilerParams(vmem_limit_bytes=megabytes * 1024 * 1024),
-        cost_estimate=cost(flops, nbytes),
+        cost_estimate=cost(flops),
         name=name,
     )(*operands)
 
@@ -323,6 +339,54 @@
 
 def whole(*shape):
     return pl.BlockSpec(shape, lambda *_: (0,) * len(shape))
+
+
+def flip_kernel(in_ref, out_ref):
+    out_ref[...] = in_ref[...].T
+
+
+def copy_kernel(in_ref, out_ref):
+    out_ref[...] = in_ref[...]
+
+
+def fetched(value):
+    height, width = value.shape
+    block = pl.BlockSpec((height // 4, width), lambda i: (i, 0))
+    return pl.pallas_call(
+        copy_kernel,
+        grid=(4,),
+        in_specs=[block],
+        out_specs=block,
+        out_shape=placed(value.shape, value.dtype, pltpu.VMEM),
+        compiler_params=pltpu.CompilerParams(vmem_limit_bytes=7 * 1024 * 1024),
+        cost_estimate=cost(0),
+        name="fetched",
+    )(in_hbm(value))
+
+
+def flip(value, space=None):
+    height, width = value.shape[-2:]
+    lead = (None,) * (value.ndim - 2)
+    zeros = (0,) * (value.ndim - 2)
+    if height > D:
+        grid = height // D
+        in_spec = pl.BlockSpec(lead + (D, width), lambda i: zeros + (i, 0))
+        out_spec = pl.BlockSpec((width, D), lambda i: (0, i))
+    else:
+        step = min(width, D)
+        grid = width // step
+        in_spec = pl.BlockSpec(lead + (height, step), lambda i: zeros + (0, i))
+        out_spec = pl.BlockSpec((step, height), lambda i: (i, 0))
+    return pl.pallas_call(
+        flip_kernel,
+        grid=(grid,),
+        in_specs=[in_spec],
+        out_specs=out_spec,
+        out_shape=placed((width, height), value.dtype, space),
+        compiler_params=pltpu.CompilerParams(vmem_limit_bytes=7 * 1024 * 1024),
+        cost_estimate=cost(0),
+        name="flip",
+    )(value)
 
 
 def front_kernel(x_ref, gains, biases, w_ref, normed_ref, q_ref, kv_ref):
@@ -362,7 +426,7 @@
     rows = entry.shape[0]
     flops = 2 * rows * (D * D + 2 * w_up.size)
     return call(
-        rest_kernel, "rest", 8, flops, [((rows, D), jnp.bfloat16)], [],
+        rest_kernel, "rest", 7, flops, [((rows, D), jnp.bfloat16)], [],
         entry, attended, gains, biases, w_out, w_up, w_down,
     )[0]
 
@@ -370,44 +434,66 @@
 def turn_kernel(
     x_ref, o_ref, d_ref, gains, biases, w_out, w_up, out_t, up_t, down_t,
     middle_ref, normed_ref, active_ref, slope_ref, grad_ref, grad_att_ref,
+    middle, normed, actives, slopes, done,
 ):
-    for part in row_chunks(x_ref.shape[0]):
-        middle = middle_rows(x_ref, o_ref, w_out, biases, part)
-        middle_ref[part, :] = middle
-        unit, inverse = normalised(middle)
-        normed = (unit * gains[1:2, :] + bias_part(biases, 1)).astype(jnp.bfloat16)
-        normed_ref[part, :] = normed
-        total = jnp.zeros_like(middle)
-        for at in range(w_up.shape[2] // D):
-            hidden = dot(normed, w_up[0, :, tile(at)], NN) + bias_part(biases, 6 + at)
-            active, slope = gelu_parts(hidden)
-            active_ref[part, tile(at)] = active.astype(jnp.bfloat16)
-            slope_ref[part, tile(at)] = slope.astype(jnp.bfloat16)
-            grad_hidden = dot(d_ref[part, :], down_t[:, tile(at)], NN) * slope
-            total += dot(grad_hidden.astype(jnp.bfloat16), up_t[tile(at), :], NN)
-        unit, inverse = normalised(middle_ref[part, :])
-        grad = d_ref[part, :].astype(jnp.float32) + norm_back(unit, inverse, gains[1:2, :], total)
-        grad_ref[part, :] = grad
-        grad_att_ref[part, :] = dot(grad.astype(jnp.bfloat16), out_t[...], NN).astype(jnp.bfloat16)
+    copies = []
+
+    def leave(source, target):
+        copies.append(pltpu.make_async_copy(source, target, done.at[len(copies)]))
+        copies[-1].start()
+
+    rows = x_ref[...].astype(jnp.float32) + dot(o_ref[...], w_out[0], NN) + bias_part(biases, 4)
+    middle[...] = rows
+    leave(middle, middle_ref)
+    unit, _ = normalised(rows)
+    normed[...] = (unit * gains[1:2, :] + bias_part(biases, 1)).astype(jnp.bfloat16)
+    leave(normed, normed_ref)
+    total = jnp.zeros_like(rows)
+    for at in range(w_up.shape[2] // D):
+        hidden = dot(normed[...], w_up[0, :, tile(at)], NN) + bias_part(biases, 6 + at)
+        active, slope = gelu_parts(hidden)
+        actives[at] = active.astype(jnp.bfloat16)
+        slopes[at] = slope.astype(jnp.bfloat16)
+        leave(actives.at[at], active_ref.at[:, tile(at)])
+        leave(slopes.at[at], slope_ref.at[:, tile(at)])
+        grad_hidden = dot(d_ref[...], down_t[:, tile(at)], NN) * slope
+        total += dot(grad_hidden.astype(jnp.bfloat16), up_t[tile(at), :], NN)
+    unit, inverse = normalised(middle[...])
+    grad = d_ref[...].astype(jnp.float32) + norm_back(unit, inverse, gains[1:2, :], total)
+    grad = grad.astype(jnp.bfloat16)
+    grad_ref[...] = grad
+    grad_att_ref[...] = dot(grad, out_t[...], NN).astype(jnp.bfloat16)
+    for copy in copies:
+        copy.wait()
 
 
 def turn(entry, attended, result_gradient, gains, biases, w_out, w_up, out_t, up_t, down_t):
     rows = entry.shape[0]
     wide, narrow = jnp.float32, jnp.bfloat16
     inner = w_up.shape[2]
-    outs = [
-        ((rows, D), wide), ((rows, D), narrow), ((rows, inner), narrow),
-        ((rows, inner), narrow), ((rows, D), wide), ((rows, D), narrow),
-    ]
-    return call(
-        turn_kernel, "turn", 12, 2 * rows * (2 * D * D + 3 * w_up.size), outs, [],
-        entry, attended, result_gradient, gains, biases, w_out, w_up, out_t, up_t, down_t,
-    )
+    steps = inner // D
+    far = [((rows, D), wide), ((rows, D), narrow), ((rows, inner), narrow), ((rows, inner), narrow)]
+    return pl.pallas_call(
+        turn_kernel,
+        in_specs=[VMEM_SPEC] * 10,
+        out_specs=[pl.BlockSpec(memory_space=pltpu.HBM)] * len(far) + [VMEM_SPEC] * 2,
+        out_shape=[placed(*out, pltpu.HBM) for out in far] + [placed((rows, D), narrow)] * 2,
+        scratch_shapes=[
+            pltpu.VMEM((rows, D), wide),
+            pltpu.VMEM((rows, D), narrow),
+            pltpu.VMEM((steps, rows, D), narrow),
+            pltpu.VMEM((steps, rows, D), narrow),
+            pltpu.SemaphoreType.DMA((2 + 2 * steps,)),
+        ],
+        compiler_params=pltpu.CompilerParams(vmem_limit_bytes=18 * 1024 * 1024),
+        cost_estimate=cost(2 * rows * (2 * D * D + 3 * w_up.size)),
+        name="turn",
+    )(entry, attended, result_gradient, gains, biases, w_out, w_up, out_t, up_t, down_t)
 
 
 def down_back_kernel(
     d_ref, slope_ref, middle_ref, gains, out_t, up_t, down_t,
-    hidden_ref, grad_ref, grad_b_ref, grad_att_ref, sums_ref, up_ref,
+    hidden_ref, grad_ref, grad_att_ref, sums_ref, up_ref,
 ):
     sums = [jnp.zeros((1, D), jnp.float32)] * 4
     steps = up_t.shape[0] // D
@@ -424,9 +510,8 @@
         unit, inverse = normalised(middle_ref[part, :])
         given = given.astype(jnp.float32)
         grad = given + norm_back(unit, inverse, gains[1:2, :], through)
-        grad_ref[part, :] = grad
         grad_b = grad.astype(jnp.bfloat16)
-        grad_b_ref[part, :] = grad_b
+        grad_ref[part, :] = grad_b
         grad_att_ref[part, :] = dot(grad_b, out_t[...], NN).astype(jnp.bfloat16)
         for at, term in enumerate((through * unit, through, grad, given)):
             sums[at] = sums[at] + column_sum(term)
@@ -439,11 +524,11 @@
     wide, narrow = jnp.float32, jnp.bfloat16
     inner = up_t.shape[0]
     outs = [
-        ((rows, inner), narrow), ((rows, D), wide), ((rows, D), narrow),
-        ((rows, D), narrow), ((4, D), wide), ((inner // D, D), wide),
+        ((rows, inner), narrow), ((rows, D), narrow), ((rows, D), narrow),
+        ((4, D), wide), ((inner // D, D), wide),
     ]
     return call(
-        down_back_kernel, "down_back", 10, 2 * rows * (D * D + 2 * up_t.size), outs, [],
+        down_back_kernel, "down_back", 8, 2 * rows * (D * D + 2 * up_t.size), outs, [],
         result_gradient, slope, middle, gains, out_t, up_t, down_t,
     )
 
@@ -462,7 +547,7 @@
         tiles = qkv_tiles(part, q_ref, own_ref, there_ref)
         through = sum(dot(value, qkv_t[tile(at), :], NN) for at, value in enumerate(tiles))
         unit, inverse = normalised(x_ref[part, :].astype(jnp.float32))
-        out = grad_ref[part, :] + norm_back(unit, inverse, gains[0:1, :], through)
+        out = grad_ref[part, :].astype(jnp.float32) + norm_back(unit, inverse, gains[0:1, :], through)
         out_ref[part, :] = out.astype(out_ref.dtype)
         terms = (through * unit, through, tiles[0].astype(jnp.float32), tiles[2].astype(jnp.float32))
         for at, term in enumerate(terms):
@@ -472,7 +557,7 @@
 
 def front_back(grad_q, own, there, entry, grad_middle, gains, qkv_t, dtype):
     rows = entry.shape[0]
-    outs = [((rows, D), dtype), ((4, D), jnp.float32)]
+    outs = [((rows, D), dtype, pltpu.VMEM), ((4, D), jnp.float32)]
     return call(
         front_back_kernel, "front_back", 8, 6 * rows * D * D, outs, [],
         grad_q, own, there, entry, grad_middle, gains, qkv_t,
@@ -496,77 +581,187 @@
     write_blocks(place, tile, order, kept_ref, sent_ref)
 
 
-def qkv_weight_grad_kernel(place, left_ref, q_ref, own_ref, there_ref, kept_ref, sent_ref, right, *, order):
-    step = pl.program_id(0)
-
-    @pl.when(step == 0)
-    def _():
-        right[...] = q_ref[...]
-
-    @pl.when(step > 0)
-    def _():
-        total = own_ref[0].astype(jnp.float32) + there_ref[0].astype(jnp.float32)
-        right[...] = total.astype(jnp.bfloat16)
-
-    weight_grad_kernel(place, left_ref, right, kept_ref, sent_ref, order=order)
+def outer_grad_kernel(place, o_ref, normed_ref, d_ref, q_ref, kept_ref, sent_ref, *, order):
+    for step, (left, right) in enumerate(((o_ref, d_ref), (normed_ref, q_ref))):
+        pl.when(pl.program_id(0) == step)(
+            functools.partial(weight_grad_kernel, place, left, right, kept_ref, sent_ref, order=order)
+        )
+
+
+def inner_grad_kernel(place, normed_ref, own_ref, there_ref, kept_ref, sent_ref, *, order):
+    right = (own_ref[0].astype(jnp.float32) + there_ref[0].astype(jnp.float32)).astype(jnp.bfloat16)
+    tile = dot(normed_ref[...], right, NN).astype(jnp.bfloat16)
+    write_blocks(place, tile, order, kept_ref, sent_ref)
 
 
 def all_blocks(z_count):
     return [(z_at, y_at, core) for z_at in range(z_count) for y_at in range(2) for core in range(2)]
 
 
-def qkv_weight_grad(place, left, grad_q, own, there, z_count):
-    rows = left.shape[1]
+def blocks_call(
+    kernel, name, grid, order, in_specs, out_spec, block, width, z_count, flops, place, *operands, space=None
+):
+    shape = placed((2, z_count, block, width), jnp.bfloat16, space)
+    return pl.pallas_call(
+        functools.partial(kernel, order=order),
+        grid_spec=pltpu.PrefetchScalarGridSpec(
+            num_scalar_prefetch=1, grid=(grid,), in_specs=in_specs, out_specs=[out_spec, out_spec]
+        ),
+        out_shape=[shape, shape],
+        compiler_params=pltpu.CompilerParams(vmem_limit_bytes=9 * 1024 * 1024),
+        cost_estimate=cost(flops),
+        name=name,
+    )(place, *operands)
+
+
+def column_blocks(block, z_count):
+    return pl.BlockSpec((2, z_count, block, D), lambda i, _: (0, 0, 0, i))
+
+
+def down_grad(place, active_t, back, z_count):
+    height, rows = active_t.shape
+    block = height // (4 * z_count)
+    specs = [pl.BlockSpec((height // z_count, rows), lambda i, _: (i, 0)), whole(rows, D)]
+    out_spec = pl.BlockSpec((2, 1, block, D), lambda i, _: (0, i, 0, 0))
+    order = [(0, y_at, core) for y_at in range(2) for core in range(2)]
+    return blocks_call(
+        weight_grad_kernel, "down_grad", z_count, order, specs, out_spec, block, D, z_count,
+        2 * rows * height * D, place, active_t, back, space=pltpu.HBM,
+    )
+
+
+def up_grad(place, normed_t, grad_hidden, z_count):
+    rows, width = grad_hidden.shape
     block = D // (4 * z_count)
-    part = pl.BlockSpec((1, rows, D), lambda i, _: (jnp.maximum(i - 1, 0), 0, 0))
-    out_spec = pl.BlockSpec((2, z_count, block, D), lambda i, _: (0, 0, 0, i))
-    shape = jax.ShapeDtypeStruct((2, z_count, block, 3 * D), jnp.bfloat16)
-    return pl.pallas_call(
-        functools.partial(qkv_weight_grad_kernel, order=all_blocks(z_count)),
+    specs = [whole(D, rows), pl.BlockSpec((rows, D), lambda i, _: (0, i))]
+    return blocks_call(
+        weight_grad_kernel, "up_grad", width // D, all_blocks(z_count), specs, column_blocks(block, z_count),
+        block, width, z_count, 2 * rows * width * D, place, normed_t, grad_hidden, space=pltpu.HBM,
+    )
+
+
+def outer_grad(place, attended_t, normed_t, grad_middle, grad_q, z_count):
+    rows = grad_q.shape[0]
+    block = D // (4 * z_count)
+    specs = [whole(D, rows)] * 2 + [whole(rows, D)] * 2
+    return blocks_call(
+        outer_grad_kernel, "outer_grad", 2, all_blocks(z_count), specs, column_blocks(block, z_count),
+        block, 2 * D, z_count, 4 * rows * D * D, place, attended_t, normed_t, grad_middle, grad_q,
+    )
+
+
+def inner_grad(place, normed_t, own, there, z_count):
+    rows = own.shape[1]
+    block = D // (4 * z_count)
+    part = pl.BlockSpec((1, rows, D), lambda i, _: (i, 0, 0))
+    return blocks_call(
+        inner_grad_kernel, "inner_grad", 2, all_blocks(z_count), [whole(D, rows), part, part],
+        column_blocks(block, z_count), block, 2 * D, z_count, 4 * rows * D * D, place, normed_t, own, there,
+    )
+
+
+def added(kept, arrived, dtype=jnp.bfloat16):
+    return (kept.astype(jnp.float32) + arrived.astype(jnp.float32)).astype(dtype)
+
+
+def fold_kernel(place, kept_ref, arrived_ref, keep_ref, send_ref):
+    for target, chosen in ((send_ref, 1 - place[0]), (keep_ref, place[0])):
+        for at in range(target.shape[0]):
+            target[at] = added(kept_ref[at, chosen], arrived_ref[at, chosen])
+
+
+def fold(kept, arrived, place, outer):
+    width = kept.shape[-1]
+    lead = math.prod(kept.shape[:outer])
+    inner = math.prod(kept.shape[outer + 1 : -1])
+    shape = (lead, 2, inner, width)
+    outs = [((lead, inner, width), kept.dtype)] * 2
+    keep, send = call(
+        fold_kernel, "fold", 4, 0, outs, [], place, kept.reshape(shape), arrived.reshape(shape), smem=1
+    )
+    left = kept.shape[:outer] + kept.shape[outer + 1 :]
+    return keep.reshape(left), send.reshape(left)
+
+
+def fold_halves_kernel(place, kept_ref, arrived_ref, y_keep, y_send, z_keep, z_send):
+    y_at, z_at = place[0], place[1]
+    half = y_keep.shape[1]
+    first, second = slice(0, half), slice(half, 2 * half)
+    for target, chosen in ((y_send, 1 - y_at), (y_keep, y_at)):
+        for z_block in range(target.shape[0]):
+            target[z_block] = added(kept_ref[chosen, z_block, first], arrived_ref[chosen, z_block, first])
+    for target, chosen in ((z_send, 1 - z_at), (z_keep, z_at)):
+        for y_block in range(2):
+            for high in range(target.shape[1]):
+                at = 2 * high + chosen
+                target[y_block, high] = added(kept_ref[y_block, at, second], arrived_ref[y_block, at, second])
+
+
+def fold_halves(kept, arrived, place):
+    _, z_count, block, width = kept.shape
+    y_shape, z_shape = (z_count, block // 2, width), (2, z_count // 2, block // 2, width)
+    outs = [(shape, kept.dtype) for shape in (y_shape, y_shape, z_shape, z_shape)]
+    return call(fold_halves_kernel, "fold_halves", 6, 0, outs, [], place, kept, arrived, smem=1)
+
+
+def fold_columns_kernel(place, kept_a, arrived_a, kept_b, arrived_b, keep_ref, send_ref):
+    width = kept_a.shape[-1]
+    for target, chosen in ((send_ref, 1 - place[0]), (keep_ref, place[0])):
+        for at in range(target.shape[0]):
+            target[at, :, :width] = added(kept_a[chosen, at], arrived_a[chosen, at])
+            target[at, :, width:] = added(kept_b[chosen, at], arrived_b[chosen, at])
+
+
+def fold_columns(first, second, place):
+    _, z_count, block, width = first[0].shape
+    outs = [((z_count, block, 2 * width), jnp.bfloat16)] * 2
+    return call(fold_columns_kernel, "fold_columns", 6, 0, outs, [], place, *first, *second, smem=1)
+
+
+def fold_rows_kernel(place, kept_a, arrived_a, kept_b, arrived_b, keep_ref, send_ref):
+    rows = kept_a.shape[1]
+    for target, chosen in ((send_ref, 1 - place[0]), (keep_ref, place[0])):
+        target[:rows] = added(kept_a[chosen], arrived_a[chosen])
+        target[rows:] = added(kept_b[chosen], arrived_b[chosen])
+
+
+def fold_rows(first, second, place):
+    _, block, width = first[0].shape
+    outs = [((2 * block, width), jnp.bfloat16)] * 2
+    return call(fold_rows_kernel, "fold_rows", 4, 0, outs, [], place, *first, *second, smem=1)
+
+
+def stream_fold_kernel(place, kept_keep, kept_send, arrived_keep, arrived_send, keep_ref, send_ref):
+    send_ref[...] = added(kept_send[...], arrived_send[...])
+    keep_ref[...] = added(kept_keep[...], arrived_keep[...])
+
+
+def stream_fold(kept, arrived, place, outer):
+    width = kept.shape[-1]
+    lead = math.prod(kept.shape[:outer])
+    inner = math.prod(kept.shape[outer + 1 : -1])
+    parts = 1 if lead > 1 else 4
+    shape = (lead, 2, inner, width)
+    block = (None, None, inner // parts, width)
+    keep_spec = pl.BlockSpec(block, lambda i, place: (i // parts, place[0], i % parts, 0))
+    send_spec = pl.BlockSpec(block, lambda i, place: (i // parts, 1 - place[0], i % parts, 0))
+    out_spec = pl.BlockSpec(block[1:], lambda i, place: (i // parts, i % parts, 0))
+    left = kept.shape[:outer] + kept.shape[outer + 1 :]
+    kept, arrived = [in_hbm(value.reshape(shape)) for value in (kept, arrived)]
+    keep, send = pl.pallas_call(
+        stream_fold_kernel,
         grid_spec=pltpu.PrefetchScalarGridSpec(
             num_scalar_prefetch=1,
-            grid=(3,),
-            in_specs=[whole(D, rows), whole(rows, D), part, part],
-            out_specs=[out_spec, out_spec],
-            scratch_shapes=[pltpu.VMEM((rows, D), jnp.bfloat16)],
-        ),
-        out_shape=[shape, shape],
-        compiler_params=pltpu.CompilerParams(vmem_limit_bytes=14 * 1024 * 1024),
-        cost_estimate=cost(6 * rows * D * D, 20 * rows * D + 6 * D * D),
-        name="qkv_weight_grad",
-    )(place, left, grad_q, own, there)
-
-
-def weight_grad(place, left, right, z_count):
-    height, rows = left.shape
-    width = right.shape[1]
-    block = height // (4 * z_count)
-    if height > D:
-        grid = z_count
-        order = [(0, y_at, core) for y_at in range(2) for core in range(2)]
-        left_spec = pl.BlockSpec((height // grid, rows), lambda i, _: (i, 0))
-        right_spec = whole(rows, width)
-        out_spec = pl.BlockSpec((2, 1, block, width), lambda i, _: (0, i, 0, 0))
-    else:
-        grid = width // D
-        order = all_blocks(z_count)
-        left_spec = whole(height, rows)
-        right_spec = pl.BlockSpec((rows, D), lambda i, _: (0, i))
-        out_spec = pl.BlockSpec((2, z_count, block, D), lambda i, _: (0, 0, 0, i))
-    shape = jax.ShapeDtypeStruct((2, z_count, block, width), jnp.bfloat16)
-    return pl.pallas_call(
-        functools.partial(weight_grad_kernel, order=order),
-        grid_spec=pltpu.PrefetchScalarGridSpec(
-            num_scalar_prefetch=1,
-            grid=(grid,),
-            in_specs=[left_spec, right_spec],
+            grid=(lead * parts,),
+            in_specs=[keep_spec, send_spec] * 2,
             out_specs=[out_spec, out_spec],
         ),
-        out_shape=[shape, shape],
-        compiler_params=pltpu.CompilerParams(vmem_limit_bytes=14 * 1024 * 1024),
-        cost_estimate=cost(2 * rows * height * width, 2 * (rows * height + rows * width + height * width)),
-        name="weight_grad",
-    )(place, left, right)
+        out_shape=[jax.ShapeDtypeStruct((lead, inner, width), jnp.bfloat16)] * 2,
+        compiler_params=pltpu.CompilerParams(vmem_limit_bytes=6 * 1024 * 1024),
+        cost_estimate=cost(0),
+        name="stream_fold",
+    )(place, kept, kept, arrived, arrived)
+    return keep.reshape(left), send.reshape(left)
 
 
 def shifted(value, axis, steps):
@@ -937,26 +1132,6 @@
     return lax.ppermute(value, "dp", [(at, at ^ step) for at in range(lax.axis_size("dp"))])
 
 
-def fold_kernel(place, kept_ref, arrived_ref, keep_ref, send_ref):
-    for target, chosen in ((send_ref, 1 - place[0]), (keep_ref, place[0])):
-        for at in range(target.shape[0]):
-            total = kept_ref[at, chosen].astype(jnp.float32) + arrived_ref[at, chosen].astype(jnp.float32)
-            target[at] = total.astype(target.dtype)
-
-
-def fold(kept, arrived, place, outer):
-    rows, width = kept.shape[-2:]
-    lead = math.prod(kept.shape[:outer])
-    inner = math.prod(kept.shape[outer + 1 : -1])
-    shape = (lead, 2, inner, width)
-    outs = [((lead, inner, width), kept.dtype)] * 2
-    keep, send = call(
-        fold_kernel, "fold", 4, 0, outs, [], place, kept.reshape(shape), arrived.reshape(shape), smem=1
-    )
-    left = kept.shape[:outer] + kept.shape[outer + 1 :]
-    return keep.reshape(left), send.reshape(left)
-
-
 def wide_sum(kept, arrived):
     return kept.astype(jnp.float32) + arrived.astype(jnp.float32)
 
@@ -995,46 +1170,50 @@
 
     meta = slot_meta(slots_of(ctx_at), slots_of(ctx_at ^ 1), signed)
 
-    def through_attention(entry):
+    def through_attention(entry, keep):
         normed, queries, kv = front(entry, gain_pair, biases, w_qkv)
         there = swap_cores(kv)
+        normed_t = None
+        if keep:
+            normed_t = flip(normed, pltpu.HBM)
+            there, normed_t = barrier((there, normed_t))
         attended, lse = sorted_attend(meta, queries, kv, there)
-        return normed, queries, kv, there, attended, lse
+        return normed_t, queries, kv, there, attended, lse
 
     inputs, meta = barrier((inputs, meta))
     first = gathered(inputs[:, 0])
-    qkv_t, out_t = w_qkv[0].T, w_out[0].T
+    qkv_t, out_t = flip(w_qkv, pltpu.HBM), flip(w_out, pltpu.HBM)
     first, qkv_t, out_t = barrier((first, qkv_t, out_t))
-    attended = through_attention(first)[4]
+    attended = through_attention(first, False)[4]
     sent = rest(first, attended, gain_pair, biases, w_out, w_up, w_down)
     sent, later = barrier((sent, (cotangent, w_up, w_down)))
     arrived = shifted(sent, "section", 1)
     given = gathered(later[0][:, 0])
-    up_t, down_t = [weight[0].T for weight in later[1:]]
+    up_t, down_t = [flip(weight, pltpu.HBM) for weight in later[1:]]
     arrived, given, up_t, down_t = barrier((arrived, given, up_t, down_t))
     entry = jnp.where(signed, first, arrived)
 
-    normed, queries, kv, kv_there, attended, lse = through_attention(entry)
+    normed_t, queries, kv, kv_there, attended, lse = through_attention(entry, True)
     middle, normed_two, active, slope, grad_middle, grad_att = turn(
         entry, attended, given, gain_pair, biases, w_out, w_up, out_t, up_t, down_t
     )
 
-    def attention_back(grad_att):
-        grad_q, own, sent = sorted_attend_back(meta, queries, kv, kv_there, attended, grad_att, lse)
-        return grad_q, own, swap_cores(sent)
-
-    grad_qkv = attention_back(grad_att)
-    handed, _ = front_back(*grad_qkv, entry, grad_middle, gain_pair, qkv_t, narrow)
-    lefts = (active, normed, attended, normed_two)
-    handed, lefts = barrier((handed, lefts))
+    waiting = meta.at[-1].set(jnp.where(signed, IDLE, 0))
+    grad_q, own, sent = sorted_attend_back(waiting, queries, kv, kv_there, attended, grad_att, lse)
+    own, sent, attended, normed_two = barrier((own, sent, attended, normed_two))
+    there = swap_cores(sent)
+    attended_t, normed_two_t = flip(attended, pltpu.HBM), flip(normed_two, pltpu.HBM)
+    there, attended_t, normed_two_t = barrier((there, attended_t, normed_two_t))
+    handed, _ = front_back(grad_q, own, there, entry, grad_middle, gain_pair, qkv_t, narrow)
+    handed, active, middle, weights = barrier((handed, active, middle, (w_up, w_down)))
     back = shifted(handed, "section", -1)
-    active = lefts[0]
-    lefts = [value.T for value in lefts]
     result = middle + dot(active, w_down[0], NN) + biases[0, 5 * D : 6 * D]
     result = result.astype(narrow)
     acts_there = swap_halves(result[rows:])
-    back, acts_there, lefts = barrier((back, acts_there, lefts))
-    active_t, normed_t, attended_t, normed_two_t = lefts
+    middle, acts_there, active = barrier((middle, acts_there, active))
+    up_t, down_t = [flip(in_hbm(weight), pltpu.VMEM) for weight in weights]
+    active_t = flip(active, pltpu.VMEM)
+    back, up_t, down_t, active_t = barrier((back, up_t, down_t, active_t))
     back = jnp.where(signed, back, given)
 
     z_steps = [1 << at for at in range(z_count.bit_length() - 1)]
@@ -1044,68 +1223,67 @@
     def bits(value, before):
         return value.reshape(value.shape[:before] + tuple(split) + value.shape[before + 1 :])
 
-    grad_hidden, grad_middle, grad_middle_b, grad_att, sums_two, up_sum = down_back(
+    grad_hidden, grad_middle, grad_att, sums_two, up_sum = down_back(
         back, slope, middle, gain_pair, out_t, up_t, down_t
     )
     back, grad_hidden = barrier((back, grad_hidden))
-    down_kept, down_sent = weight_grad(place, active_t, back, z_count)
+    down_kept, down_sent = down_grad(place, active_t, back, z_count)
     grad_hidden, down_sent = barrier((grad_hidden, down_sent))
     down_there = swap_cores(down_sent)
-    up_kept, up_sent = weight_grad(place, normed_two_t, grad_hidden, z_count)
-    grad_middle_b, up_sent = barrier((grad_middle_b, up_sent))
+    up_kept, up_sent = up_grad(place, normed_two_t, grad_hidden, z_count)
+    down_there, up_sent = barrier((down_there, up_sent))
     up_there = swap_cores(up_sent)
-    down_kept, down_sent = fold(down_kept, down_there, y_place, 0)
-    grad_middle_b, down_sent = barrier((grad_middle_b, down_sent))
-    down_there = swap_halves(down_sent)
-    out_kept, out_sent = weight_grad(place, attended_t, grad_middle_b, z_count)
-    out_there = swap_cores(out_sent)
-    up_kept, up_sent = fold(bits(up_kept, 1), bits(up_there, 1), by_z[0], len(split))
-    grad_att, up_sent, out_there = barrier((grad_att, up_sent, out_there))
-    up_there = swap_z(up_sent, z_steps[0])
+    down_kept, down_sent = stream_fold(down_kept, down_there, y_place, 0)
+    up_there, down_sent = barrier((up_there, down_sent))
+    up_kept, up_sent = stream_fold(bits(up_kept, 1), bits(up_there, 1), by_z[0], len(split))
+    grad_att, down_sent, up_sent = barrier((grad_att, down_sent, up_sent))
+    down_there, up_there = swap_halves(down_sent), swap_z(up_sent, z_steps[0])
     grad_q, own, sent = sorted_attend_back(meta, queries, kv, kv_there, attended, grad_att, lse)
-    sent, own, down_there, up_there = barrier((sent, own, down_there, up_there))
+
+    grad_q, own, sent, down_there, up_there = barrier((grad_q, own, sent, down_there, up_there))
     there = swap_cores(sent)
+    outer_kept, outer_sent = outer_grad(place, attended_t, normed_t, grad_middle, grad_q, z_count)
+    there, outer_sent = barrier((there, outer_sent))
+    outer_there = swap_cores(outer_sent)
+    inner_kept, inner_sent = inner_grad(place, normed_t, own, there, z_count)
+    inner_sent, down_there, up_there = barrier((inner_sent, down_there, up_there))
+    inner_there = swap_cores(inner_sent)
     down_kept, down_sent = fold(bits(down_kept, 0), bits(down_there, 0), by_z[0], len(split) - 1)
-    up_kept, up_sent = fold(up_kept, up_there, y_place, 0)
-    there, down_sent, up_sent = barrier((there, down_sent, up_sent))
-    down_there, up_there = swap_z(down_sent, z_steps[0]), swap_halves(up_sent)
-    qkv_kept, qkv_sent = qkv_weight_grad(place, normed_t, grad_q, own, there, z_count)
-    qkv_sent, grad_q, own, there = barrier((qkv_sent, grad_q, own, there))
-    qkv_there = swap_cores(qkv_sent)
+    up_kept, up_sent = fold(up_kept, up_there, by_z[1], 1)
+    outer_there, inner_there, down_sent, up_sent = barrier((outer_there, inner_there, down_sent, up_sent))
+    rest_kept, rest_sent = fold_columns((outer_kept, outer_there), (inner_kept, inner_there), y_place)
+    rest_sent, down_sent, up_sent, grad_q, own, there = barrier((rest_sent, down_sent, up_sent, grad_q, own, there))
+    rest_there, down_there, up_there = swap_halves(rest_sent), swap_z(down_sent, z_steps[0]), swap_z(up_sent, z_steps[1])
     input_gradient, sums_one = front_back(grad_q, own, there, entry, grad_middle, gain_pair, qkv_t, wide)
-    out_kept, out_sent = fold(out_kept, out_there, y_place, 0)
     small = jnp.concatenate([sums_one, sums_two, up_sum], axis=0)
     small = small + swap_cores(small)
-    qkv_kept, qkv_sent = fold(qkv_kept, qkv_there, y_place, 0)
-    qkv_sent, out_sent, small = barrier((qkv_sent, out_sent, small))
-    small_there, qkv_there, out_there = swap_halves(small), swap_halves(qkv_sent), swap_halves(out_sent)
+    rounded = input_gradient.astype(narrow)
+    small, rounded = barrier((small, rounded))
+    small = small + swap_z(small, z_steps[0])
+    rest_there, down_there, up_there, small = barrier((rest_there, down_there, up_there, small))
+
+    rest_kept, rest_sent = fold(bits(rest_kept, 0), bits(rest_there, 0), by_z[0], len(split) - 1)
+    rest_there = swap_z(rest_sent, z_steps[0])
     down_kept, down_sent = fold(down_kept, down_there, by_z[1], 0)
-    down_there = swap_z(down_sent, z_steps[1])
-    up_kept, up_sent = fold(up_kept, up_there, by_z[1], 0)
-    up_there = swap_z(up_sent, z_steps[1])
-    qkv_kept, qkv_sent = fold(bits(qkv_kept, 0), bits(qkv_there, 0), by_z[0], len(split) - 1)
-    out_kept, out_sent = fold(bits(out_kept, 0), bits(out_there, 0), by_z[0], len(split) - 1)
+    up_kept, up_sent = fold(up_kept, up_there, y_place, 0)
+    down_there, up_there = swap_z(down_sent, z_steps[1]), swap_halves(up_sent)
+    small_there = swap_z(small, z_steps[1])
+    rest_there, up_there, small_there, rounded = barrier((rest_there, up_there, small_there, rounded))
+    rest_kept, rest_sent = fold(rest_kept, rest_there, by_z[1], 0)
     small = small + small_there
-    rounded = input_gradient.astype(narrow)
-    qkv_sent, out_sent, small, rounded = barrier((qkv_sent, out_sent, small, rounded))
-    small_there, qkv_there, out_there = [swap_z(value, z_steps[0]) for value in (small, qkv_sent, out_sent)]
+    rest_sent, small, rounded, result, acts_there = barrier((rest_sent, small, rounded, result, acts_there))
+    rest_there = swap_z(rest_sent, z_steps[1])
+    small = small + swap_halves(small)
     grads_there = swap_halves(rounded[rows:])
-    qkv_kept, qkv_sent = fold(qkv_kept, qkv_there, by_z[1], 0)
-    out_kept, out_sent = fold(out_kept, out_there, by_z[1], 0)
-    small = small + small_there
-    qkv_sent, out_sent, small = barrier((qkv_sent, out_sent, small))
-    small_there, qkv_there, out_there = [swap_z(value, z_steps[1]) for value in (small, qkv_sent, out_sent)]
     wdown = wide_sum(down_kept, down_there)
     wup = wide_sum(up_kept, up_there)
-    wqkv = wide_sum(qkv_kept, qkv_there)
-    wout = wide_sum(out_kept, out_there)
-    small = small + small_there
     grads_kept = jnp.where(signed, input_gradient[:rows], rounded[:rows].astype(wide))
+    wout = wide_sum(rest_kept[:, :D], rest_there[:, :D])
+    wqkv = wide_sum(rest_kept[:, D:], rest_there[:, D:])
     blocks = count * z_count
     block_at = lax.axis_index("dp") * count + ctx_at
     gain_piece = lax.dynamic_slice_in_dim(small[0:5:4], block_at * (D // blocks), D // blocks, 1)
-    bias_rows = [small[1], small[5], small[2], small[3], small[6], small[7], small[8:].reshape(-1)]
-    bias_row = jnp.concatenate(bias_rows)
+    bias_row = jnp.concatenate([small[1:2], small[5:6], small[2:4], small[6:]], axis=0).reshape(-1)
     width = bias_row.shape[0] // blocks
     bias_piece = lax.dynamic_slice_in_dim(bias_row, block_at * width, width, 0)
     return (

time: 318 us -> 297 us (0.934)
  local copies, waits for them, and re-layouts: 64.3 us -> 20.2 us
  Pallas kernels: 133 us -> 146 us
  waiting for transfers between devices: 69.2 us -> 78 us
    pallas_call x4 -> x17, Pallas kernels: 14 us -> 57.9 us  [the longest x10 23.8 us: flip(): pl.pallas_call(flip_kernel, grid=(grid,), in_specs=[in_spec], out_specs=o...]
    optimization_barrier x6 -> x0, local copies, waits for them, and re-layouts: 25.1 us -> none  [the longest x2 13.3 us: fast_body(): sent, later = barrier((sent, (cotangent, w_up, w_down)))]
    ppermute x9 -> x8, waiting for transfers between devices: 29 us -> 10.9 us  [swap_halves(): lax.ppermute(value, 'ctx', [(at, (at + count // 2) % count) for at in ran...]
    unnamed x170 -> x155, local copies, waits for them, and re-layouts: 33.8 us -> 16.6 us
    pallas_call x19 -> x13, Pallas kernels: 45.2 us -> 29.1 us  [call(): pl.pallas_call(kernel, in_specs=[SMEM_SPEC] * smem + [VMEM_SPEC] * (len(o...]
    pallas_call x2, Pallas kernels: 39.8 us -> 23.9 us  [sorted_attend_back(): pl.pallas_call(functools.partial(backward_kernel, span=span), in_specs=[S...]
    ppermute x10 -> x8, waiting for transfers between devices: 25.7 us -> 41.2 us  [swap_z(): lax.ppermute(value, 'dp', [(at, at ^ step) for at in range(lax.axis_size(...]
    ppermute x2, waiting for transfers between devices: 3.89 us -> 18.9 us  [shifted(): lax.ppermute(value, axis, [(source, source + steps) for source in range(i...]
  transfers between devices with their start and end apart: 30 -> 27, of which waited for: 12 -> 16; matrix products, arithmetic and copies ran while one was open for 15% -> 5% of each run, Pallas kernels for 12% -> 20%
where the time goes in v3:
time: 297 us; the launch traced here: 294 us
  Pallas kernels  146 us (49%)
  waiting for transfers between devices  78 us (26%)
  starting transfers between devices  31 us (10%)
  local copies, waits for them, and re-layouts  20.2 us (7%)
  other arithmetic  14 us (5%)
    ppermute x8, waiting for transfers between devices, swap_z(): lax.ppermute(value, 'dp', [(at, at ^ step) for at in range(lax.axis_size(...  41.2 us
    pallas_call x2, Pallas kernels, sorted_attend(): pl.pallas_call(functools.partial(forward_kernel, span=span), in_specs=[SM...  35.6 us
    pallas_call x13, Pallas kernels, call(): pl.pallas_call(kernel, in_specs=[SMEM_SPEC] * smem + [VMEM_SPEC] * (len(o...  29.1 us
    pallas_call x2, Pallas kernels, sorted_attend_back(): pl.pallas_call(functools.partial(backward_kernel, span=span), in_specs=[S...  23.9 us
    pallas_call x10, Pallas kernels, flip(): pl.pallas_call(flip_kernel, grid=(grid,), in_specs=[in_spec], out_specs=o...  23.8 us
    ppermute x2, waiting for transfers between devices, shifted(): lax.ppermute(value, axis, [(source, source + steps) for source in range(i...  18.9 us
    unnamed x155, local copies, waits for them, and re-layouts  16.6 us
    pallas_call x4, Pallas kernels, blocks_call(): pl.pallas_call(functools.partial(kernel, order=order), grid_spec=pltpu.Pr...  15.6 us
  transfers between devices with their start and end apart: 27, of which 16 were waited for; matrix products, arithmetic and copies ran while one was open for 5% of the time, Pallas kernels for 20%

profile of v3, /device:TPU:0, one launch (start us, length us, event | category | flops | bytes accessed | tf_op | source)
XLA Modules:
  0.0 294.1 jit_solution(5073513359041539277)
XLA Ops:
  3.1 3.0 %collective-permute-start = (bf16[256,768]{1,0:T(8,128)(2,1)S(1)}, bf16[256,768]{1,0:T(8,128)(2,1)S(1)}, u32[]{:S(2)}, u32[]{:S(2)}) collective-permute-start(bf16[256,768]{1,0:T(8,128)(2,1)S(1)} %get-tuple-element.321), channel_id=1, source_target_pairs={{0,2},{1,3},{2,0},{3,1},{4,6},{5,7},{6,4},{7,5},{8,10},{9,11},{10,... | collective-permute-start | bytes 1179656 | tf_op jit(solution)/shard_map/ppermute | solution.py:1124
  6.1 2.0 copy-done.2
  8.2 3.0 %flip.10.qkv_t = bf16[2304,768]{1,0:T(8,128)(2,1)} custom-call(bf16[1,768,2304]{2,1,0:T(8,128)(2,1)S(1)} %copy-done.2), custom_call_target="tpu_custom_call" | custom-call | tf_op jit(solution)/shard_map/flip/pallas_call | solution.py:380
  12.6 2.6 collective-permute-done
  15.4 2.4 front.2
  17.9 3.4 %collective-permute-done.1.kv2_ref = bf16[512,1536]{1,0:T(8,128)(2,1)S(1)} collective-permute-done((bf16[512,1536]{1,0:T(8,128)(2,1)S(1)}, bf16[512,1536]{1,0:T(8,128)(2,1)S(1)}, u32[]{:S(2)}, u32[]{:S(2)}) %collective-permute-start.1) | collective-permute-done | bytes 1572896 | tf_op jit(solution)/shard_map/ppermute | solution.py:1128
  21.3 12.2 %attend.2 = (bf16[512,768]{1,0:T(8,128)(2,1)S(1)}, f32[6,4,256]{2,1,0:T(4,128)}) custom-call(s32[17]{0:T(128)S(1)} %concatenate.22.meta, bf16[512,768]{1,0:T(8,128)(2,1)S(1)} %get-tuple-element.157.q_ref, bf16[512,1536]{1,0:T(8,128)(2,1)S(1)} %get-tuple-element.158.kv_ref, bf16[512,1536]{1,0:T(8,128)(2,1)S(1)} %collective-permute-done.1.kv2_ref), custom_call_target="tpu_custom_call" | custom-call | flops 4000000000 | tf_op jit(solution)/shard_map/attend/pallas_call | solution.py:160
  33.5 6.6 %rest.1 = bf16[512,768]{1,0:T(8,128)(2,1)S(1)} custom-call(bf16[512,768]{1,0:T(8,128)(2,1)S(1)} %pad_maximum_fusion.x_ref, bf16[512,768]{1,0:T(8,128)(2,1)S(1)} %get-tuple-element.159.o_ref, f32[2,768]{1,0:T(2,128)S(1)} %bitcast.105, f32[1,7680]{1,0:T(1,128)S(1)} %copy-done.48, bf16[1,768,768]{2,1,0:T(8,128)(2,1)S(1)} %copy-done.9, ...), custom_call_target="tpu_custom_call" | custom-call | flops 679477248 | tf_op jit(solution)/shard_map/rest/pallas_call | solution.py:320
  41.5 1.8 collective-permute-start.3
  43.3 3.4 %flip.12.up_t = bf16[3072,768]{1,0:T(8,128)(2,1)} custom-call(bf16[1,768,3072]{2,1,0:T(8,128)(2,1)S(1)} %bitcast.84), custom_call_target="tpu_custom_call" | custom-call | tf_op jit(solution)/shard_map/flip/pallas_call | solution.py:380
  46.7 3.3 %flip.13.down_t = bf16[768,3072]{1,0:T(8,128)(2,1)} custom-call(bf16[1,3072,768]{2,1,0:T(8,128)(2,1)S(1)} %bitcast.88), custom_call_target="tpu_custom_call" | custom-call | tf_op jit(solution)/shard_map/flip/pallas_call | solution.py:380
  50.0 2.7 collective-permute-done.3
  52.8 5.9 %collective-permute-done.2 = bf16[512,768]{1,0:T(8,128)(2,1)S(1)} collective-permute-done((bf16[512,768]{1,0:T(8,128)(2,1)S(1)}, bf16[512,768]{1,0:T(8,128)(2,1)S(1)}, u32[]{:S(2)}, u32[]{:S(2)}) %collective-permute-start.2) | collective-permute-done | bytes 786464 | tf_op jit(solution)/shard_map/ppermute | solution.py:770
  58.8 3.1 %front.3 = (bf16[512,768]{1,0:T(8,128)(2,1)S(1)}, bf16[512,768]{1,0:T(8,128)(2,1)S(1)}, bf16[512,1536]{1,0:T(8,128)(2,1)}) custom-call(bf16[512,768]{1,0:T(8,128)(2,1)S(1)} %broadcast_select_fusion.1.x_ref, f32[2,768]{1,0:T(2,128)S(1)} %bitcast.106, f32[1,7680]{1,0:T(1,128)S(1)} %copy-done.48, bf16[1,768,2304]{2,1,0:T(8,128)(2,1)S(1)} %copy-done.3), custom_call_target="tpu_custom_call" | custom-call | flops 226492416 | tf_op jit(solution)/shard_map/front/pallas_call | solution.py:320
  64.0 2.6 collective-permute-done.4.kv2_ref
  66.6 23.4 %attend.3 = (bf16[512,768]{1,0:T(8,128)(2,1)S(1)}, f32[6,4,256]{2,1,0:T(4,128)S(1)}) custom-call(s32[17]{0:T(128)S(1)} %concatenate.22.meta, bf16[512,768]{1,0:T(8,128)(2,1)S(1)} %copy-done.56, bf16[512,1536]{1,0:T(8,128)(2,1)} %get-tuple-element.166.kv_ref, bf16[512,1536]{1,0:T(8,128)(2,1)} %collective-permute-done.4.kv2_ref), custom_call_target="tpu_custom_call" | custom-call | flops 4000000000 | tf_op jit(solution)/shard_map/attend/pallas_call | solution.py:160
  90.2 11.9 %turn.1 = (f32[512,768]{1,0:T(8,128)}, bf16[512,768]{1,0:T(8,128)(2,1)}, bf16[512,3072]{1,0:T(8,128)(2,1)}, bf16[512,3072]{1,0:T(8,128)(2,1)}, bf16[512,768]{1,0...) custom-call(bf16[512,768]{1,0:T(8,128)(2,1)S(1)} %broadcast_select_fusion.1.x_ref, ...), custom_call_target="tpu_custom_call" | custom-call | flops 1056964608 | tf_op jit(solution)/shard_map/turn/pallas_call | solution.py:476
  102.1 2.7 attend_back.2
  108.3 3.7 %front_back.2 = (bf16[512,768]{1,0:T(8,128)(2,1)}, f32[4,768]{1,0:T(4,128)}) custom-call(bf16[512,768]{1,0:T(8,128)(2,1)S(1)} %get-tuple-element.184.q_ref, bf16[2,512,768]{2,1,0:T(8,128)(2,1)S(1)} %get-tuple-element.185.own_ref, bf16[2,512,768]{2,1,0:T(8,128)(2,1)S(1)} %collective-permute-done.5.there_ref, bf16[512,768]{1,0:T(8,128)(2,1)S(1)} %copy-done.6, ...), custom_call_target="tpu_custom_call" | custom-call | flops 226492416 | tf_op jit(solution)/shard_map/front_back/pallas_call | solution.py:320
  112.0 1.7 collective-permute-start.6
  113.8 2.6 add_convert_fusion
  118.0 1.7 collective-permute-start.7
  119.8 3.7 %flip.17.up_t = bf16[3072,768]{1,0:T(8,128)(2,1)S(1)} custom-call(bf16[1,768,3072]{2,1,0:T(8,128)(2,1)} %in_ref.6), custom_call_target="tpu_custom_call" | custom-call | tf_op jit(solution)/shard_map/flip/pallas_call | solution.py:380
  123.5 4.1 %flip.18.down_t = bf16[768,3072]{1,0:T(8,128)(2,1)S(1)} custom-call(bf16[1,3072,768]{2,1,0:T(8,128)(2,1)} %in_ref.7), custom_call_target="tpu_custom_call" | custom-call | tf_op jit(solution)/shard_map/flip/pallas_call | solution.py:380
  127.7 1.9 collective-permute-done.7
  130.8 12.9 %collective-permute-done.6 = bf16[512,768]{1,0:T(8,128)(2,1)} collective-permute-done((bf16[512,768]{1,0:T(8,128)(2,1)}, bf16[512,768]{1,0:T(8,128)(2,1)}, u32[]{:S(2)}, u32[]{:S(2)}) %collective-permute-start.6) | collective-permute-done | bytes 786464 | tf_op jit(solution)/shard_map/ppermute | solution.py:770
  145.1 6.9 %down_back.1 = (bf16[512,3072]{1,0:T(8,128)(2,1)S(1)}, bf16[512,768]{1,0:T(8,128)(2,1)S(1)}, bf16[512,768]{1,0:T(8,128)(2,1)S(1)}, f32[4,768]{1,0:T(4,128)S(1)}, f32[4,768]{1,0:T(4,128)S(1)}) custom-call(bf16[512,768]{1,0:T(8,128)(2,1)S(1)} %broadcast_select_fusion.d_ref.right_ref, bf16[512,3072]{1,0:T(8,128)(2,1)S(1)} %copy-done.24, ...), custom_call_target="tpu_custom_call" | custom-call | flops 679477248 | tf_op jit(solution)/shard_map/down_back/pallas_call | solution.py:320
  152.8 4.8 %down_grad.1 = (bf16[2,4,192,768]{3,2,1,0:T(8,128)(2,1)}, bf16[2,4,192,768]{3,2,1,0:T(8,128)(2,1)}) custom-call(s32[1]{0:T(128)} %bitcast.3.place, bf16[3072,512]{1,0:T(8,128)(2,1)S(1)} %flip.19.left_ref, bf16[512,768]{1,0:T(8,128)(2,1)S(1)} %broadcast_select_fusion.d_ref.right_ref), custom_call_target="tpu_custom_call" | custom-call | flops 301989888 | tf_op jit(solution)/shard_map/down_grad/pallas_call | solution.py:605
  157.8 5.0 %up_grad.1 = (bf16[2,4,48,3072]{3,2,1,0:T(8,128)(2,1)}, bf16[2,4,48,3072]{3,2,1,0:T(8,128)(2,1)}) custom-call(s32[1]{0:T(128)} %bitcast.3.place, bf16[768,512]{1,0:T(8,128)(2,1)S(1)} %copy-done.23, bf16[512,3072]{1,0:T(8,128)(2,1)S(1)} %get-tuple-element.212.right_ref), custom_call_target="tpu_custom_call" | custom-call | flops 301989888 | tf_op jit(solution)/shard_map/up_grad/pallas_call | solution.py:605
  163.3 3.2 %stream_fold.2 = (bf16[1,768,768]{2,1,0:T(8,128)(2,1)S(1)}, bf16[1,768,768]{2,1,0:T(8,128)(2,1)S(1)}) custom-call(s32[1]{0:T(128)} %bitcast.2.place, bf16[1,2,768,768]{3,2,1,0:T(8,128)(2,1)} %bitcast.120, bf16[1,2,768,768]{3,2,1,0:T(8,128)(2,1)} %bitcast.121, bf16[1,2,768,768]{3,2,1,0:T(8,128)(2,1)} %bitcast.17.arrived_keep.arrived_send, ...), custom_call_target="tpu_custom_call" | custom-call | tf_op jit(solution)/shard_map/stream_fold/pallas_call | solution.py:751
  167.8 3.4 %stream_fold.3 = (bf16[4,48,3072]{2,1,0:T(8,128)(2,1)S(1)}, bf16[4,48,3072]{2,1,0:T(8,128)(2,1)S(1)}) custom-call(s32[1]{0:T(128)} %bitcast.1.place, bf16[4,2,48,3072]{3,2,1,0:T(8,128)(2,1)} %bitcast.118, bf16[4,2,48,3072]{3,2,1,0:T(8,128)(2,1)} %bitcast.119, bf16[4,2,48,3072]{3,2,1,0:T(8,128)(2,1)} %bitcast.20.arrived_keep.arrived_send, ...), custom_call_target="tpu_custom_call" | custom-call | tf_op jit(solution)/shard_map/stream_fold/pallas_call | solution.py:751
  172.2 1.8 collective-permute-start.10
  174.0 1.6 collective-permute-start.11
  175.6 21.2 %attend_back.3 = (bf16[512,768]{1,0:T(8,128)(2,1)S(1)}, bf16[2,512,768]{2,1,0:T(8,128)(2,1)S(1)}, bf16[2,512,768]{2,1,0:T(8,128)(2,1)S(1)}) custom-call(s32[17]{0:T(128)S(1)} %concatenate.22.meta, bf16[512,768]{1,0:T(8,128)(2,1)S(1)} %copy-done.57, bf16[512,1536]{1,0:T(8,128)(2,1)} %get-tuple-element.166.kv_ref, ...), custom_call_target="tpu_custom_call" | custom-call | flops 8000000000 | tf_op jit(solution)/shard_map/attend_back/pallas_call | solution.py:251
  196.8 3.7 %collective-permute-done.10 = bf16[4,192,768]{2,1,0:T(8,128)(2,1)S(1)} collective-permute-done((bf16[4,192,768]{2,1,0:T(8,128)(2,1)S(1)}, bf16[4,192,768]{2,1,0:T(8,128)(2,1)S(1)}, u32[]{:S(2)}, u32[]{:S(2)}) %collective-permute-start.10) | collective-permute-done | bytes 1179680 | tf_op jit(solution)/shard_map/ppermute | solution.py:1124
  203.0 2.8 outer_grad.1
  206.8 2.8 inner_grad.1
  216.7 2.3 fold_columns.1
  220.4 1.6 collective-permute-start.16
  222.0 2.6 collective-permute-start.17
  224.6 2.9 front_back.3
  229.4 20.1 %collective-permute-done.19 = f32[12,768]{1,0:T(8,128)S(1)} collective-permute-done((f32[12,768]{1,0:T(8,128)S(1)}, f32[12,768]{1,0:T(8,128)S(1)}, u32[]{:S(2)}, u32[]{:S(2)}) %collective-permute-start.19) | collective-permute-done | bytes 36896 | tf_op jit(solution)/shard_map/ppermute | solution.py:1132
  250.5 1.7 collective-permute-start.20
  252.3 2.0 collective-permute-start.26
  256.2 15.0 %collective-permute-done.26 = bf16[192,768]{1,0:T(8,128)(2,1)S(1)} collective-permute-done((bf16[192,768]{1,0:T(8,128)(2,1)S(1)}, bf16[192,768]{1,0:T(8,128)(2,1)S(1)}, u32[]{:S(2)}, u32[]{:S(2)}) %collective-permute-start.26) | collective-permute-done | bytes 294944 | tf_op jit(solution)/shard_map/ppermute | solution.py:1132
  273.4 3.1 %collective-permute-start.25 = (bf16[48,3072]{1,0:T(8,128)(2,1)S(1)}, bf16[48,3072]{1,0:T(8,128)(2,1)}, u32[]{:S(2)}, u32[]{:S(2)}) collective-permute-start(bf16[48,3072]{1,0:T(8,128)(2,1)S(1)} %bitcast.115), channel_id=1, source_target_pairs={{0,8},{4,12},{8,0},{12,4},{1,9},{5,13},{9,1},{13,5},{2,10},{6,14},... | collective-permute-start | bytes 884744 | tf_op jit(solution)/shard_map/ppermute | solution.py:1132
  282.9 5.3 %collective-permute-done.25 = bf16[48,3072]{1,0:T(8,128)(2,1)} collective-permute-done((bf16[48,3072]{1,0:T(8,128)(2,1)S(1)}, bf16[48,3072]{1,0:T(8,128)(2,1)}, u32[]{:S(2)}, u32[]{:S(2)}) %collective-permute-start.25) | collective-permute-done | bytes 294944 | tf_op jit(solution)/shard_map/ppermute | solution.py:1132
  288.2 1.7 add_bitcast_fusion
  (240 shorter events, 48.3 us)
Async XLA Ops:
  3.1 12.1 %collective-permute-start = (bf16[256,768]{1,0:T(8,128)(2,1)S(1)}, bf16[256,768]{1,0:T(8,128)(2,1)S(1)}, u32[]{:S(2)}, u32[]{:S(2)}) collective-permute-start(bf16[256,768]{1,0:T(8,128)(2,1)S(1)} %get-tuple-element.321), channel_id=1, source_target_pairs={{0,2},{1,3},{2,0},{3,1},{4,6},{5,7},{6,4},{7,5},{8,10},{9,11},{10,... | collective-permute-start | bytes 1179656 | tf_op jit(solution)/shard_map/ppermute | solution.py:1124
  15.3 18.1 %slice-start = ((s8[4718592]{0:T(1024)(128)(4,1)}), s8[4194304]{0:T(1024)(128)(4,1)S(1)}, s32[]{:S(2)}) async-start(s8[4718592]{0:T(1024)(128)(4,1)} %bitcast.83), calls=%async_computation | async-start | bytes 8388608
  15.4 18.1 %slice-start.4 = ((s8[4718592]{0:T(1024)(128)(4,1)}), s8[4194304]{0:T(1024)(128)(4,1)S(1)}, s32[]{:S(2)}) async-start(s8[4718592]{0:T(1024)(128)(4,1)} %bitcast.87), calls=%async_computation.4 | async-start | bytes 8388608
  17.8 3.5 %collective-permute-start.1 = (bf16[512,1536]{1,0:T(8,128)(2,1)S(1)}, bf16[512,1536]{1,0:T(8,128)(2,1)S(1)}, u32[]{:S(2)}, u32[]{:S(2)}) collective-permute-start(bf16[512,1536]{1,0:T(8,128)(2,1)S(1)} %get-tuple-element.158.kv_ref), channel_id=1, source_target_pairs={{0,1},{1,0},{2,3},{3,2},{4,5},{5,4},{6,7},{7,6},{8,9},{9,8},{10,11... | collective-permute-start | bytes 4718600 | tf_op jit(solution)/shard_map/ppermute | solution.py:1128
  40.1 18.7 %collective-permute-start.2 = (bf16[512,768]{1,0:T(8,128)(2,1)S(1)}, bf16[512,768]{1,0:T(8,128)(2,1)S(1)}, u32[]{:S(2)}, u32[]{:S(2)}) collective-permute-start(bf16[512,768]{1,0:T(8,128)(2,1)S(1)} %rest.1), channel_id=1, source_target_pairs={{0,16},{1,17},{2,18},{3,19},{4,20},{5,21},{6,22},{7,23},{8,24},{9,... | collective-permute-start | bytes 2359304 | tf_op jit(solution)/shard_map/ppermute | solution.py:770
  41.5 11.2 %collective-permute-start.3 = (bf16[256,768]{1,0:T(8,128)(2,1)S(1)}, bf16[256,768]{1,0:T(8,128)(2,1)S(1)}, u32[]{:S(2)}, u32[]{:S(2)}) collective-permute-start(bf16[256,768]{1,0:T(8,128)(2,1)S(1)} %get-tuple-element.319), channel_id=1, source_target_pairs={{0,2},{1,3},{2,0},{3,1},{4,6},{5,7},{6,4},{7,5},{8,10},{9,11},{10,... | collective-permute-start | bytes 1179656 | tf_op jit(solution)/shard_map/ppermute | solution.py:1124
  52.8 37.3 %copy-start.13 = (bf16[512,768]{1,0:T(8,128)(2,1)}, bf16[512,768]{1,0:T(8,128)(2,1)S(1)}, u32[]{:S(2)}) copy-start(bf16[512,768]{1,0:T(8,128)(2,1)S(1)} %pad_maximum_fusion.1.d_ref) | copy-start | bytes 2359300
  58.8 31.3 %copy-start.5 = (bf16[512,768]{1,0:T(8,128)(2,1)}, bf16[512,768]{1,0:T(8,128)(2,1)S(1)}, u32[]{:S(2)}) copy-start(bf16[512,768]{1,0:T(8,128)(2,1)S(1)} %broadcast_select_fusion.1.x_ref) | copy-start | bytes 2359300
  62.8 3.8 %collective-permute-start.4 = (bf16[512,1536]{1,0:T(8,128)(2,1)}, bf16[512,1536]{1,0:T(8,128)(2,1)}, u32[]{:S(2)}, u32[]{:S(2)}) collective-permute-start(bf16[512,1536]{1,0:T(8,128)(2,1)} %get-tuple-element.166.kv_ref), channel_id=1, source_target_pairs={{0,1},{1,0},{2,3},{3,2},{4,5},{5,4},{6,7},{7,6},{8,9},{9,8},{10,11... | collective-permute-start | bytes 4718600 | tf_op jit(solution)/shard_map/ppermute | solution.py:1128
  62.9 27.2 %slice-start.2 = ((s8[4718592]{0:T(1024)(128)(4,1)}), s8[4194304]{0:T(1024)(128)(4,1)S(1)}, s32[]{:S(2)}) async-start(s8[4718592]{0:T(1024)(128)(4,1)} %bitcast.85), calls=%async_computation.2 | async-start | bytes 8388608
  62.9 27.2 %slice-start.8 = ((s8[4718592]{0:T(1024)(128)(4,1)}), s8[4194304]{0:T(1024)(128)(4,1)S(1)}, s32[]{:S(2)}) async-start(s8[4718592]{0:T(1024)(128)(4,1)} %bitcast.91), calls=%async_computation.8 | async-start | bytes 8388608
  66.6 23.5 %slice-start.3 = ((s8[4718592]{0:T(1024)(128)(4,1)}), s8[524288]{0:T(1024)(128)(4,1)S(1)}, s32[]{:S(2)}) async-start(s8[4718592]{0:T(1024)(128)(4,1)} %bitcast.85), calls=%async_computation.3 | async-start | bytes 1048576
  66.6 23.5 %slice-start.9 = ((s8[4718592]{0:T(1024)(128)(4,1)}), s8[524288]{0:T(1024)(128)(4,1)S(1)}, s32[]{:S(2)}) async-start(s8[4718592]{0:T(1024)(128)(4,1)} %bitcast.91), calls=%async_computation.9 | async-start | bytes 1048576
  66.6 23.5 %copy-start.8 = (bf16[768,3072]{1,0:T(8,128)(2,1)S(1)}, bf16[768,3072]{1,0:T(8,128)(2,1)}, u32[]{:S(2)}) copy-start(bf16[768,3072]{1,0:T(8,128)(2,1)} %flip.13.down_t) | copy-start | bytes 14155780
  66.6 23.5 %copy-start.10 = (bf16[768,768]{1,0:T(8,128)(2,1)S(1)}, bf16[768,768]{1,0:T(8,128)(2,1)}, u32[]{:S(2)}) copy-start(bf16[768,768]{1,0:T(8,128)(2,1)} %flip.11.out_t) | copy-start | bytes 3538948
  66.6 23.5 %copy-start.49 = (f32[1,7680]{1,0:T(1,128)S(1)}, f32[1,7680]{1,0:T(1,128)}, u32[]{:S(2)}) copy-start(f32[1,7680]{1,0:T(1,128)} %biases.7) | copy-start | bytes 92164
  90.0 15.0 %copy-start.31 = (bf16[512,768]{1,0:T(8,128)(2,1)}, bf16[512,768]{1,0:T(8,128)(2,1)S(1)}, u32[]{:S(2)}) copy-start(bf16[512,768]{1,0:T(8,128)(2,1)S(1)} %get-tuple-element.180.o_ref.in_ref) | copy-start | bytes 2359300
  104.8 3.5 %collective-permute-start.5 = (bf16[2,512,768]{2,1,0:T(8,128)(2,1)S(1)}, bf16[2,512,768]{2,1,0:T(8,128)(2,1)S(1)}, u32[]{:S(2)}, u32[]{:S(2)}) collective-permute-start(bf16[2,512,768]{2,1,0:T(8,128)(2,1)S(1)} %get-tuple-element.179), channel_id=1, source_target_pairs={{0,1},{1,0},{2,3},{3,2},{4,5},{5,4},{6,7},{7,6},{8,9},{9,8},{10,11... | collective-permute-start | bytes 4718600 | tf_op jit(solution)/shard_map/ppermute | solution.py:1128
  112.0 31.8 %collective-permute-start.6 = (bf16[512,768]{1,0:T(8,128)(2,1)}, bf16[512,768]{1,0:T(8,128)(2,1)}, u32[]{:S(2)}, u32[]{:S(2)}) collective-permute-start(bf16[512,768]{1,0:T(8,128)(2,1)} %get-tuple-element.192), channel_id=1, source_target_pairs={{16,0},{17,1},{18,2},{19,3},{20,4},{21,5},{22,6},{23,7},{24,8},{25... | collective-permute-start | bytes 2359304 | tf_op jit(solution)/shard_map/ppermute | solution.py:770
  118.0 11.5 %collective-permute-start.7 = (bf16[256,768]{1,0:T(8,128)(2,1)}, bf16[256,768]{1,0:T(8,128)(2,1)}, u32[]{:S(2)}, u32[]{:S(2)}) collective-permute-start(bf16[256,768]{1,0:T(8,128)(2,1)} %slice.70), channel_id=1, source_target_pairs={{0,2},{1,3},{2,0},{3,1},{4,6},{5,7},{6,4},{7,5},{8,10},{9,11},{10,... | collective-permute-start | bytes 1179656 | tf_op jit(solution)/shard_map/ppermute | solution.py:1124
  127.6 16.1 %copy-start.14 = (bf16[512,768]{1,0:T(8,128)(2,1)S(1)}, bf16[512,768]{1,0:T(8,128)(2,1)}, u32[]{:S(2)}) copy-start(bf16[512,768]{1,0:T(8,128)(2,1)} %copy-done.13) | copy-start | bytes 2359300
  129.5 15.5 %copy-start.24 = (bf16[512,3072]{1,0:T(8,128)(2,1)S(1)}, bf16[512,3072]{1,0:T(8,128)(2,1)}, u32[]{:S(2)}) copy-start(bf16[512,3072]{1,0:T(8,128)(2,1)} %get-tuple-element.199.slope_ref) | copy-start | bytes 9437188
  129.5 15.5 %copy-start.34 = (f32[512,768]{1,0:T(8,128)S(1)}, f32[512,768]{1,0:T(8,128)}, u32[]{:S(2)}) copy-start(f32[512,768]{1,0:T(8,128)} %get-tuple-element.200.middle_ref) | copy-start | bytes 4718596
  130.8 14.2 %copy-start.11 = (bf16[768,768]{1,0:T(8,128)(2,1)S(1)}, bf16[768,768]{1,0:T(8,128)(2,1)}, u32[]{:S(2)}) copy-start(bf16[768,768]{1,0:T(8,128)(2,1)} %flip.11.out_t) | copy-start | bytes 3538948
  157.7 5.1 %collective-permute-start.8 = (bf16[2,4,192,768]{3,2,1,0:T(8,128)(2,1)}, bf16[2,4,192,768]{3,2,1,0:T(8,128)(2,1)}, u32[]{:S(2)}, u32[]{:S(2)}) collective-permute-start(bf16[2,4,192,768]{3,2,1,0:T(8,128)(2,1)} %get-tuple-element.210), channel_id=1, source_target_pairs={{0,1},{1,0},{2,3},{3,2},{4,5},{5,4},{6,7},{7,6},{8,9},{9,8},{10,11... | collective-permute-start | bytes 7077896 | tf_op jit(solution)/shard_map/ppermute | solution.py:1128
  162.8 5.0 %collective-permute-start.9 = (bf16[2,4,48,3072]{3,2,1,0:T(8,128)(2,1)}, bf16[2,4,48,3072]{3,2,1,0:T(8,128)(2,1)}, u32[]{:S(2)}, u32[]{:S(2)}) collective-permute-start(bf16[2,4,48,3072]{3,2,1,0:T(8,128)(2,1)} %get-tuple-element.214), channel_id=1, source_target_pairs={{0,1},{1,0},{2,3},{3,2},{4,5},{5,4},{6,7},{7,6},{8,9},{9,8},{10,11... | collective-permute-start | bytes 7077896 | tf_op jit(solution)/shard_map/ppermute | solution.py:1128
  172.2 30.8 %copy-start.12 = (bf16[768,512]{1,0:T(8,128)(2,1)S(1)}, bf16[768,512]{1,0:T(8,128)(2,1)}, u32[]{:S(2)}) copy-start(bf16[768,512]{1,0:T(8,128)(2,1)} %flip.14.normed_ref) | copy-start | bytes 2359300
  172.2 30.8 %copy-start.26 = (bf16[512,768]{1,0:T(8,128)(2,1)S(1)}, bf16[512,768]{1,0:T(8,128)(2,1)}, u32[]{:S(2)}) copy-start(bf16[512,768]{1,0:T(8,128)(2,1)} %copy-done.25) | copy-start | bytes 2359300
  172.2 30.8 %copy-start.30 = (bf16[768,512]{1,0:T(8,128)(2,1)S(1)}, bf16[768,512]{1,0:T(8,128)(2,1)}, u32[]{:S(2)}) copy-start(bf16[768,512]{1,0:T(8,128)(2,1)} %flip.15.o_ref) | copy-start | bytes 2359300
  172.2 28.3 %collective-permute-start.10 = (bf16[4,192,768]{2,1,0:T(8,128)(2,1)S(1)}, bf16[4,192,768]{2,1,0:T(8,128)(2,1)S(1)}, u32[]{:S(2)}, u32[]{:S(2)}) collective-permute-start(bf16[4,192,768]{2,1,0:T(8,128)(2,1)S(1)} %bitcast.113), channel_id=1, source_target_pairs={{0,2},{1,3},{2,0},{3,1},{4,6},{5,7},{6,4},{7,5},{8,10},{9,11},{10,... | collective-permute-start | bytes 3538952 | tf_op jit(solution)/shard_map/ppermute | solution.py:1124
  174.0 28.0 %collective-permute-start.11 = (bf16[2,2,48,3072]{3,2,1,0:T(8,128)(2,1)S(1)}, bf16[2,2,48,3072]{3,2,1,0:T(8,128)(2,1)S(1)}, u32[]{:S(2)}, u32[]{:S(2)}) collective-permute-start(bf16[2,2,48,3072]{3,2,1,0:T(8,128)(2,1)S(1)} %bitcast.114), channel_id=1, source_target_pairs={{0,4},{4,0},{8,12},{12,8},{1,5},{5,1},{9,13},{13,9},{2,6},{6,2},{1... | collective-permute-start | bytes 3538952 | tf_op jit(solution)/shard_map/ppermute | solution.py:1132
  203.0 3.9 %collective-permute-start.12 = (bf16[2,512,768]{2,1,0:T(8,128)(2,1)S(1)}, bf16[2,512,768]{2,1,0:T(8,128)(2,1)S(1)}, u32[]{:S(2)}, u32[]{:S(2)}) collective-permute-start(bf16[2,512,768]{2,1,0:T(8,128)(2,1)S(1)} %get-tuple-element.230), channel_id=1, source_target_pairs={{0,1},{1,0},{2,3},{3,2},{4,5},{5,4},{6,7},{7,6},{8,9},{9,8},{10,11... | collective-permute-start | bytes 4718600 | tf_op jit(solution)/shard_map/ppermute | solution.py:1128
  210.7 5.9 %collective-permute-start.14 = (bf16[2,4,48,1536]{3,2,1,0:T(8,128)(2,1)}, bf16[2,4,48,1536]{3,2,1,0:T(8,128)(2,1)}, u32[]{:S(2)}, u32[]{:S(2)}) collective-permute-start(bf16[2,4,48,1536]{3,2,1,0:T(8,128)(2,1)} %get-tuple-element.238), channel_id=1, source_target_pairs={{0,1},{1,0},{2,3},{3,2},{4,5},{5,4},{6,7},{7,6},{8,9},{9,8},{10,11... | collective-permute-start | bytes 3538952 | tf_op jit(solution)/shard_map/ppermute | solution.py:1128
  211.2 5.4 %collective-permute-start.13 = (bf16[2,4,48,1536]{3,2,1,0:T(8,128)(2,1)}, bf16[2,4,48,1536]{3,2,1,0:T(8,128)(2,1)}, u32[]{:S(2)}, u32[]{:S(2)}) collective-permute-start(bf16[2,4,48,1536]{3,2,1,0:T(8,128)(2,1)} %get-tuple-element.232), channel_id=1, source_target_pairs={{0,1},{1,0},{2,3},{3,2},{4,5},{5,4},{6,7},{7,6},{8,9},{9,8},{10,11... | collective-permute-start | bytes 3538952 | tf_op jit(solution)/shard_map/ppermute | solution.py:1128
  219.0 31.2 %collective-permute-start.15 = (bf16[4,48,3072]{2,1,0:T(8,128)(2,1)S(1)}, bf16[4,48,3072]{2,1,0:T(8,128)(2,1)S(1)}, u32[]{:S(2)}, u32[]{:S(2)}) collective-permute-start(bf16[4,48,3072]{2,1,0:T(8,128)(2,1)S(1)} %get-tuple-element.252), channel_id=1, source_target_pairs={{0,2},{1,3},{2,0},{3,1},{4,6},{5,7},{6,4},{7,5},{8,10},{9,11},{10,... | collective-permute-start | bytes 3538952 | tf_op jit(solution)/shard_map/ppermute | solution.py:1124
  220.4 29.6 %collective-permute-start.16 = (bf16[2,192,768]{2,1,0:T(8,128)(2,1)S(1)}, bf16[2,192,768]{2,1,0:T(8,128)(2,1)S(1)}, u32[]{:S(2)}, u32[]{:S(2)}) collective-permute-start(bf16[2,192,768]{2,1,0:T(8,128)(2,1)S(1)} %get-tuple-element.253), channel_id=1, source_target_pairs={{0,4},{4,0},{8,12},{12,8},{1,5},{5,1},{9,13},{13,9},{2,6},{6,2},{1... | collective-permute-start | bytes 1769480 | tf_op jit(solution)/shard_map/ppermute | solution.py:1132
  222.0 28.2 %collective-permute-start.17 = (bf16[2,48,3072]{2,1,0:T(8,128)(2,1)S(1)}, bf16[2,48,3072]{2,1,0:T(8,128)(2,1)S(1)}, u32[]{:S(2)}, u32[]{:S(2)}) collective-permute-start(bf16[2,48,3072]{2,1,0:T(8,128)(2,1)S(1)} %get-tuple-element.254), channel_id=1, source_target_pairs={{0,8},{4,12},{8,0},{12,4},{1,9},{5,13},{9,1},{13,5},{2,10},{6,14},... | collective-permute-start | bytes 1769480 | tf_op jit(solution)/shard_map/ppermute | solution.py:1132
  227.5 23.0 %copy-start.19 = (f32[512,768]{1,0:T(8,128)}, f32[512,768]{1,0:T(8,128)S(1)}, u32[]{:S(2)}) copy-start(f32[512,768]{1,0:T(8,128)S(1)} %get-tuple-element.261) | copy-start | bytes 4718596
  227.6 1.3 collective-permute-start.18
  228.9 20.6 %collective-permute-start.19 = (f32[12,768]{1,0:T(8,128)S(1)}, f32[12,768]{1,0:T(8,128)S(1)}, u32[]{:S(2)}, u32[]{:S(2)}) collective-permute-start(f32[12,768]{1,0:T(8,128)S(1)} %fusion.14), channel_id=1, source_target_pairs={{0,4},{4,0},{8,12},{12,8},{1,5},{5,1},{9,13},{13,9},{2,6},{6,2},{1... | collective-permute-start | bytes 110600 | tf_op jit(solution)/shard_map/ppermute | solution.py:1132
  250.5 22.0 %collective-permute-start.20 = (bf16[2,48,3072]{2,1,0:T(8,128)(2,1)S(1)}, bf16[2,48,3072]{2,1,0:T(8,128)(2,1)S(1)}, u32[]{:S(2)}, u32[]{:S(2)}) collective-permute-start(bf16[2,48,3072]{2,1,0:T(8,128)(2,1)S(1)} %get-tuple-element.265), channel_id=1, source_target_pairs={{0,4},{4,0},{8,12},{12,8},{1,5},{5,1},{9,13},{13,9},{2,6},{6,2},{1... | collective-permute-start | bytes 1769480 | tf_op jit(solution)/shard_map/ppermute | solution.py:1132
  252.3 18.8 %collective-permute-start.26 = (bf16[192,768]{1,0:T(8,128)(2,1)S(1)}, bf16[192,768]{1,0:T(8,128)(2,1)S(1)}, u32[]{:S(2)}, u32[]{:S(2)}) collective-permute-start(bf16[192,768]{1,0:T(8,128)(2,1)S(1)} %bitcast.117), channel_id=1, source_target_pairs={{0,8},{4,12},{8,0},{12,4},{1,9},{5,13},{9,1},{13,5},{2,10},{6,14},... | collective-permute-start | bytes 884744 | tf_op jit(solution)/shard_map/ppermute | solution.py:1132
  254.5 17.5 %collective-permute-start.21 = (bf16[48,3072]{1,0:T(8,128)(2,1)S(1)}, bf16[48,3072]{1,0:T(8,128)(2,1)S(1)}, u32[]{:S(2)}, u32[]{:S(2)}) collective-permute-start(bf16[48,3072]{1,0:T(8,128)(2,1)S(1)} %bitcast.116), channel_id=1, source_target_pairs={{0,2},{1,3},{2,0},{3,1},{4,6},{5,7},{6,4},{7,5},{8,10},{9,11},{10,... | collective-permute-start | bytes 884744 | tf_op jit(solution)/shard_map/ppermute | solution.py:1124
  255.2 21.9 %copy-start.62 = (bf16[512,768]{1,0:T(8,128)(2,1)S(1)}, bf16[512,768]{1,0:T(8,128)(2,1)}, u32[]{:S(2)}) copy-start(bf16[512,768]{1,0:T(8,128)(2,1)} %convert_element_type.48) | copy-start | bytes 2359300
  255.2 16.8 %collective-permute-start.22 = (f32[12,768]{1,0:T(8,128)}, f32[12,768]{1,0:T(8,128)S(1)}, u32[]{:S(2)}, u32[]{:S(2)}) collective-permute-start(f32[12,768]{1,0:T(8,128)} %add.105), channel_id=1, source_target_pairs={{0,8},{4,12},{8,0},{12,4},{1,9},{5,13},{9,1},{13,5},{2,10},{6,14},... | collective-permute-start | bytes 110600 | tf_op jit(solution)/shard_map/ppermute | solution.py:1132
  273.4 14.8 %collective-permute-start.25 = (bf16[48,3072]{1,0:T(8,128)(2,1)S(1)}, bf16[48,3072]{1,0:T(8,128)(2,1)}, u32[]{:S(2)}, u32[]{:S(2)}) collective-permute-start(bf16[48,3072]{1,0:T(8,128)(2,1)S(1)} %bitcast.115), channel_id=1, source_target_pairs={{0,8},{4,12},{8,0},{12,4},{1,9},{5,13},{9,1},{13,5},{2,10},{6,14},... | collective-permute-start | bytes 884744 | tf_op jit(solution)/shard_map/ppermute | solution.py:1132
  276.5 5.0 %collective-permute-start.24 = (f32[12,768]{1,0:T(8,128)S(1)}, f32[12,768]{1,0:T(8,128)S(1)}, u32[]{:S(2)}, u32[]{:S(2)}) collective-permute-start(f32[12,768]{1,0:T(8,128)S(1)} %add.106), channel_id=1, source_target_pairs={{0,2},{1,3},{2,0},{3,1},{4,6},{5,7},{6,4},{7,5},{8,10},{9,11},{10,... | collective-permute-start | bytes 110600 | tf_op jit(solution)/shard_map/ppermute | solution.py:1124
  277.1 14.3 %collective-permute-start.23 = (bf16[256,768]{1,0:T(8,128)(2,1)S(1)}, bf16[256,768]{1,0:T(8,128)(2,1)}, u32[]{:S(2)}, u32[]{:S(2)}) collective-permute-start(bf16[256,768]{1,0:T(8,128)(2,1)S(1)} %slice.60), channel_id=1, source_target_pairs={{0,2},{1,3},{2,0},{3,1},{4,6},{5,7},{6,4},{7,5},{8,10},{9,11},{10,... | collective-permute-start | bytes 1179656 | tf_op jit(solution)/shard_map/ppermute | solution.py:1124
  (56 other events, 285.7 us)

commit v4 on v3

--- a/solution.py
+++ b/solution.py
@@ -389,7 +389,7 @@
     )(value)
 
 
-def front_kernel(x_ref, gains, biases, w_ref, normed_ref, q_ref, kv_ref):
+def front_rows(x_ref, gains, biases, w_ref, normed_ref, q_ref, kv_ref):
     for part in row_chunks(x_ref.shape[0]):
         unit, _ = normalised(x_ref[part, :].astype(jnp.float32))
         normed = (unit * gains[0:1, :] + bias_part(biases, 0)).astype(jnp.bfloat16)
@@ -399,11 +399,36 @@
         q_ref[part, :] = (dot(normed, w_ref[0, :, tile(0)], NN) + bias_part(biases, 2)).astype(jnp.bfloat16)
 
 
+def choose(which, first_ref, second_ref, chosen_ref):
+    for index, source in ((1, first_ref), (0, second_ref)):
+
+        @pl.when(which[0] == index)
+        def _():
+            chosen_ref[...] = source[...]
+
+
+def chosen_front_kernel(which, first_ref, second_ref, gains, biases, w_ref, chosen_ref, normed_ref, q_ref, kv_ref):
+    choose(which, first_ref, second_ref, chosen_ref)
+    front_rows(chosen_ref, gains, biases, w_ref, normed_ref, q_ref, kv_ref)
+
+
+def front_outs(rows):
+    narrow = jnp.bfloat16
+    return [((rows, D), narrow), ((rows, D), narrow), ((rows, 2 * D), narrow)]
+
+
 def front(entry, gains, biases, w_qkv):
     rows = entry.shape[0]
-    narrow = jnp.bfloat16
-    outs = [((rows, D), narrow), ((rows, D), narrow), ((rows, 2 * D), narrow)]
-    return call(front_kernel, "front", 8, 6 * rows * D * D, outs, [], entry, gains, biases, w_qkv)
+    return call(front_rows, "front", 8, 6 * rows * D * D, front_outs(rows), [], entry, gains, biases, w_qkv)
+
+
+def chosen_front(which, first, second, gains, biases, w_qkv):
+    rows = first.shape[0]
+    outs = [((rows, D), jnp.bfloat16)] + front_outs(rows)
+    return call(
+        chosen_front_kernel, "chosen_front", 8, 6 * rows * D * D, outs, [],
+        which, first, second, gains, biases, w_qkv, smem=1,
+    )
 
 
 def middle_rows(x_ref, o_ref, w_out, biases, part):
@@ -492,9 +517,10 @@
 
 
 def down_back_kernel(
-    d_ref, slope_ref, middle_ref, gains, out_t, up_t, down_t,
-    hidden_ref, grad_ref, grad_att_ref, sums_ref, up_ref,
+    which, first_ref, second_ref, slope_ref, middle_ref, gains, out_t, up_t, down_t,
+    d_ref, hidden_ref, grad_ref, grad_att_ref, sums_ref, up_ref,
 ):
+    choose(which, first_ref, second_ref, d_ref)
     sums = [jnp.zeros((1, D), jnp.float32)] * 4
     steps = up_t.shape[0] // D
     up_sums = [jnp.zeros((1, D), jnp.float32)] * steps
@@ -519,17 +545,17 @@
     up_ref[...] = jnp.concatenate(up_sums, axis=0)
 
 
-def down_back(result_gradient, slope, middle, gains, out_t, up_t, down_t):
-    rows = result_gradient.shape[0]
+def down_back(which, first, second, slope, middle, gains, out_t, up_t, down_t):
+    rows = first.shape[0]
     wide, narrow = jnp.float32, jnp.bfloat16
     inner = up_t.shape[0]
     outs = [
-        ((rows, inner), narrow), ((rows, D), narrow), ((rows, D), narrow),
+        ((rows, D), narrow), ((rows, inner), narrow), ((rows, D), narrow), ((rows, D), narrow),
         ((4, D), wide), ((inner // D, D), wide),
     ]
     return call(
         down_back_kernel, "down_back", 8, 2 * rows * (D * D + 2 * up_t.size), outs, [],
-        result_gradient, slope, middle, gains, out_t, up_t, down_t,
+        which, first, second, slope, middle, gains, out_t, up_t, down_t, smem=1,
     )
 
 
@@ -564,104 +590,204 @@
     )
 
 
-def write_blocks(place, tile, order, kept_ref, sent_ref):
-    rows = kept_ref.shape[2]
-
-    def write(core):
-        for at, (z_at, y_at, core_at) in enumerate(order):
-            target = kept_ref if core_at == core else sent_ref
-            target[y_at, z_at] = tile[at * rows : (at + 1) * rows]
-
-    for core in range(2):
-        pl.when(place[0] == core)(functools.partial(write, core))
-
-
-def weight_grad_kernel(place, left_ref, right_ref, kept_ref, sent_ref, *, order):
-    tile = dot(left_ref[...], right_ref[...], NN).astype(jnp.bfloat16)
-    write_blocks(place, tile, order, kept_ref, sent_ref)
-
-
-def outer_grad_kernel(place, o_ref, normed_ref, d_ref, q_ref, kept_ref, sent_ref, *, order):
-    for step, (left, right) in enumerate(((o_ref, d_ref), (normed_ref, q_ref))):
-        pl.when(pl.program_id(0) == step)(
-            functools.partial(weight_grad_kernel, place, left, right, kept_ref, sent_ref, order=order)
-        )
-
-
-def inner_grad_kernel(place, normed_ref, own_ref, there_ref, kept_ref, sent_ref, *, order):
-    right = (own_ref[0].astype(jnp.float32) + there_ref[0].astype(jnp.float32)).astype(jnp.bfloat16)
-    tile = dot(normed_ref[...], right, NN).astype(jnp.bfloat16)
-    write_blocks(place, tile, order, kept_ref, sent_ref)
-
-
-def all_blocks(z_count):
-    return [(z_at, y_at, core) for z_at in range(z_count) for y_at in range(2) for core in range(2)]
-
-
-def blocks_call(
-    kernel, name, grid, order, in_specs, out_spec, block, width, z_count, flops, place, *operands, space=None
-):
-    shape = placed((2, z_count, block, width), jnp.bfloat16, space)
+def added(kept, arrived, dtype=jnp.bfloat16):
+    return (kept.astype(jnp.float32) + arrived.astype(jnp.float32)).astype(dtype)
+
+
+def core_rows(left_ref, core, order):
+    block = left_ref.shape[0] // (2 * len(order))
+    picked = [
+        left_ref[pl.ds(pl.multiple_of((2 * (2 * z_at + y_at) + core) * block, block), block), :] for z_at, y_at in order
+    ]
+    return jnp.concatenate(picked, axis=0)
+
+
+def by_y_then_z(z_count):
+    return [(z_at, y_at) for y_at in range(2) for z_at in range(z_count)]
+
+
+def down_sent_kernel(place, left_ref, right_ref, sent_ref):
+    block = sent_ref.shape[2]
+    rows = core_rows(left_ref, 1 - place[0], by_y_then_z(1))
+    total = dot(rows, right_ref[...], NN).astype(jnp.bfloat16)
+    for y_at in range(2):
+        sent_ref[y_at, 0] = total[y_at * block : (y_at + 1) * block]
+
+
+def down_kept_kernel(place, left_ref, right_ref, there_ref, keep_ref, send_ref):
+    block = keep_ref.shape[1]
+    total = dot(core_rows(left_ref, place[0], by_y_then_z(1)), right_ref[...], NN)
+    parts = [added(total[y_at * block : (y_at + 1) * block], there_ref[y_at, 0]) for y_at in range(2)]
+
+    def store(mine):
+        keep_ref[0] = parts[mine]
+        send_ref[0] = parts[1 - mine]
+
+    for mine in range(2):
+        pl.when(place[1] == mine)(functools.partial(store, mine))
+
+
+def grid_call(kernel, name, grid, in_specs, out_specs, shapes, scratch, flops, place, *operands, far=0):
     return pl.pallas_call(
-        functools.partial(kernel, order=order),
+        kernel,
         grid_spec=pltpu.PrefetchScalarGridSpec(
-            num_scalar_prefetch=1, grid=(grid,), in_specs=in_specs, out_specs=[out_spec, out_spec]
+            num_scalar_prefetch=1, grid=(grid,), in_specs=in_specs, out_specs=out_specs, scratch_shapes=scratch
         ),
-        out_shape=[shape, shape],
+        out_shape=[
+            placed(shape, jnp.bfloat16, pltpu.HBM if at < far else None) for at, shape in enumerate(shapes)
+        ],
         compiler_params=pltpu.CompilerParams(vmem_limit_bytes=9 * 1024 * 1024),
         cost_estimate=cost(flops),
         name=name,
     )(place, *operands)
 
 
-def column_blocks(block, z_count):
-    return pl.BlockSpec((2, z_count, block, D), lambda i, _: (0, 0, 0, i))
-
-
-def down_grad(place, active_t, back, z_count):
+def down_specs(active_t, z_count):
     height, rows = active_t.shape
     block = height // (4 * z_count)
-    specs = [pl.BlockSpec((height // z_count, rows), lambda i, _: (i, 0)), whole(rows, D)]
-    out_spec = pl.BlockSpec((2, 1, block, D), lambda i, _: (0, i, 0, 0))
-    order = [(0, y_at, core) for y_at in range(2) for core in range(2)]
-    return blocks_call(
-        weight_grad_kernel, "down_grad", z_count, order, specs, out_spec, block, D, z_count,
-        2 * rows * height * D, place, active_t, back, space=pltpu.HBM,
-    )
-
-
-def up_grad(place, normed_t, grad_hidden, z_count):
+    in_specs = [pl.BlockSpec((height // z_count, rows), lambda i, _: (i, 0)), whole(rows, D)]
+    return block, in_specs, pl.BlockSpec((2, 1, block, D), lambda i, _: (0, i, 0, 0))
+
+
+def down_sent(place, active_t, back, z_count):
+    block, in_specs, sent_spec = down_specs(active_t, z_count)
+    return grid_call(
+        down_sent_kernel, "down_sent", z_count, in_specs, [sent_spec], [(2, z_count, block, D)], [],
+        active_t.size * D, place, active_t, back,
+    )[0]
+
+
+def down_kept(place, active_t, back, there, z_count):
+    block, in_specs, sent_spec = down_specs(active_t, z_count)
+    out_spec = pl.BlockSpec((1, block, D), lambda i, _: (i, 0, 0))
+    return grid_call(
+        down_kept_kernel, "down_kept", z_count, in_specs + [sent_spec], [out_spec] * 2, [(z_count, block, D)] * 2, [],
+        active_t.size * D, place, active_t, back, there, far=1,
+    )
+
+
+def up_sent_kernel(place, left_ref, right_ref, sent_ref, rows):
+    z_count, block = sent_ref.shape[1:3]
+    order = by_y_then_z(z_count)
+
+    @pl.when(pl.program_id(0) == 0)
+    def _():
+        rows[...] = core_rows(left_ref, 1 - place[0], order)
+
+    total = dot(rows[...], right_ref[...], NN).astype(jnp.bfloat16)
+    for at, (z_at, y_at) in enumerate(order):
+        sent_ref[y_at, z_at] = total[at * block : (at + 1) * block]
+
+
+def up_kept_kernel(place, left_ref, right_ref, there_ref, keep_ref, send_ref, rows):
+    z_count, block = there_ref.shape[1:3]
+    order = by_y_then_z(z_count)
+
+    @pl.when(pl.program_id(0) == 0)
+    def _():
+        rows[...] = core_rows(left_ref, place[0], order)
+
+    total = dot(rows[...], right_ref[...], NN)
+    parts = [added(total[at * block : (at + 1) * block], there_ref[y_at, z_at]) for at, (z_at, y_at) in enumerate(order)]
+
+    def store(mine):
+        for part, (z_at, y_at) in zip(parts, order):
+            target = keep_ref if z_at % 2 == mine else send_ref
+            target[y_at, z_at // 2] = part
+
+    for mine in range(2):
+        pl.when(place[2] == mine)(functools.partial(store, mine))
+
+
+def half_rows(rows):
+    return pltpu.VMEM((D // 2, rows), jnp.bfloat16)
+
+
+def column_spec(z_count):
+    return pl.BlockSpec((2, z_count, D // (4 * z_count), D), lambda i, _: (0, 0, 0, i))
+
+
+def up_sent(place, normed_t, grad_hidden, z_count):
     rows, width = grad_hidden.shape
-    block = D // (4 * z_count)
-    specs = [whole(D, rows), pl.BlockSpec((rows, D), lambda i, _: (0, i))]
-    return blocks_call(
-        weight_grad_kernel, "up_grad", width // D, all_blocks(z_count), specs, column_blocks(block, z_count),
-        block, width, z_count, 2 * rows * width * D, place, normed_t, grad_hidden, space=pltpu.HBM,
-    )
-
-
-def outer_grad(place, attended_t, normed_t, grad_middle, grad_q, z_count):
-    rows = grad_q.shape[0]
-    block = D // (4 * z_count)
-    specs = [whole(D, rows)] * 2 + [whole(rows, D)] * 2
-    return blocks_call(
-        outer_grad_kernel, "outer_grad", 2, all_blocks(z_count), specs, column_blocks(block, z_count),
-        block, 2 * D, z_count, 4 * rows * D * D, place, attended_t, normed_t, grad_middle, grad_q,
-    )
-
-
-def inner_grad(place, normed_t, own, there, z_count):
-    rows = own.shape[1]
-    block = D // (4 * z_count)
-    part = pl.BlockSpec((1, rows, D), lambda i, _: (i, 0, 0))
-    return blocks_call(
-        inner_grad_kernel, "inner_grad", 2, all_blocks(z_count), [whole(D, rows), part, part],
-        column_blocks(block, z_count), block, 2 * D, z_count, 4 * rows * D * D, place, normed_t, own, there,
-    )
-
-
-def added(kept, arrived, dtype=jnp.bfloat16):
-    return (kept.astype(jnp.float32) + arrived.astype(jnp.float32)).astype(dtype)
+    in_specs = [whole(D, rows), pl.BlockSpec((rows, D), lambda i, _: (0, i))]
+    return grid_call(
+        up_sent_kernel, "up_sent", width // D, in_specs, [column_spec(z_count)],
+        [(2, z_count, D // (4 * z_count), width)], [half_rows(rows)], grad_hidden.size * D, place, normed_t, grad_hidden,
+    )[0]
+
+
+def up_kept(place, normed_t, grad_hidden, there, z_count):
+    rows, width = grad_hidden.shape
+    in_specs = [whole(D, rows), pl.BlockSpec((rows, D), lambda i, _: (0, i)), column_spec(z_count)]
+    shape = (2, z_count // 2, D // (4 * z_count), width)
+    out_spec = pl.BlockSpec(shape[:3] + (D,), lambda i, _: (0, 0, 0, i))
+    return grid_call(
+        up_kept_kernel, "up_kept", width // D, in_specs, [out_spec] * 2, [shape] * 2, [half_rows(rows)],
+        grad_hidden.size * D, place, normed_t, grad_hidden, there, far=1,
+    )
+
+
+def store_sent(sent_ref, at, total):
+    z_count, block = sent_ref.shape[1:3]
+    for row, (z_at, y_at) in enumerate(by_y_then_z(z_count)):
+        sent_ref[y_at, z_at, :, tile(at)] = total[row * block : (row + 1) * block].astype(jnp.bfloat16)
+
+
+def outer_sent_kernel(place, o_ref, normed_ref, d_ref, q_ref, sent_ref):
+    order = by_y_then_z(sent_ref.shape[1])
+    for at, (left, right) in enumerate(((o_ref, d_ref), (normed_ref, q_ref))):
+        store_sent(sent_ref, at, dot(core_rows(left, 1 - place[0], order), right[...], NN))
+
+
+def outer_sent(place, attended_t, normed_t, grad_middle, grad_q, z_count):
+    outs = [((2, z_count, D // (4 * z_count), 2 * D), jnp.bfloat16)]
+    return call(
+        outer_sent_kernel, "outer_sent", 6, 2 * D * grad_q.size, outs, [],
+        place, attended_t, normed_t, grad_middle, grad_q, smem=1,
+    )[0]
+
+
+def inner_sent_kernel(place, normed_ref, own_ref, there_ref, sent_ref):
+    rows = core_rows(normed_ref, 1 - place[0], by_y_then_z(sent_ref.shape[1]))
+    for at in range(2):
+        store_sent(sent_ref, at, dot(rows, added(own_ref[at], there_ref[at]), NN))
+
+
+def inner_sent(place, normed_t, own, there, z_count):
+    outs = [((2, z_count, D // (4 * z_count), 2 * D), jnp.bfloat16)]
+    return call(
+        inner_sent_kernel, "inner_sent", 6, D * own.size, outs, [], place, normed_t, own, there, smem=1
+    )[0]
+
+
+def rest_kept_kernel(
+    place, o_ref, normed_ref, d_ref, q_ref, own_ref, there_ref, outer_ref, inner_ref, keep_ref, send_ref
+):
+    z_count, block = keep_ref.shape[:2]
+    order = by_y_then_z(z_count)
+    attended, normed = [core_rows(left, place[0], order) for left in (o_ref, normed_ref)]
+
+    def run(mine):
+        for at in range(4):
+            left = normed if at else attended
+            right = (d_ref[...], q_ref[...])[at] if at < 2 else added(own_ref[at - 2], there_ref[at - 2])
+            total = dot(left, right, NN)
+            arrived = inner_ref if at > 1 else outer_ref
+            for row, (z_at, y_at) in enumerate(order):
+                target = keep_ref if y_at == mine else send_ref
+                part = total[row * block : (row + 1) * block]
+                target[z_at, :, tile(at)] = added(part, arrived[y_at, z_at, :, tile(at % 2)])
+
+    for mine in range(2):
+        pl.when(place[1] == mine)(functools.partial(run, mine))
+
+
+def rest_kept(place, attended_t, normed_t, grad_middle, grad_q, own, there, outer_there, inner_there, z_count):
+    outs = [((z_count, D // (4 * z_count), 4 * D), jnp.bfloat16)] * 2
+    return call(
+        rest_kept_kernel, "rest_kept", 10, 4 * D * grad_q.size, outs, [],
+        place, attended_t, normed_t, grad_middle, grad_q, own, there, outer_there, inner_there, smem=1,
+    )
 
 
 def fold_kernel(place, kept_ref, arrived_ref, keep_ref, send_ref):
@@ -681,54 +807,6 @@
     )
     left = kept.shape[:outer] + kept.shape[outer + 1 :]
     return keep.reshape(left), send.reshape(left)
-
-
-def fold_halves_kernel(place, kept_ref, arrived_ref, y_keep, y_send, z_keep, z_send):
-    y_at, z_at = place[0], place[1]
-    half = y_keep.shape[1]
-    first, second = slice(0, half), slice(half, 2 * half)
-    for target, chosen in ((y_send, 1 - y_at), (y_keep, y_at)):
-        for z_block in range(target.shape[0]):
-            target[z_block] = added(kept_ref[chosen, z_block, first], arrived_ref[chosen, z_block, first])
-    for target, chosen in ((z_send, 1 - z_at), (z_keep, z_at)):
-        for y_block in range(2):
-            for high in range(target.shape[1]):
-                at = 2 * high + chosen
-                target[y_block, high] = added(kept_ref[y_block, at, second], arrived_ref[y_block, at, second])
-
-
-def fold_halves(kept, arrived, place):
-    _, z_count, block, width = kept.shape
-    y_shape, z_shape = (z_count, block // 2, width), (2, z_count // 2, block // 2, width)
-    outs = [(shape, kept.dtype) for shape in (y_shape, y_shape, z_shape, z_shape)]
-    return call(fold_halves_kernel, "fold_halves", 6, 0, outs, [], place, kept, arrived, smem=1)
-
-
-def fold_columns_kernel(place, kept_a, arrived_a, kept_b, arrived_b, keep_ref, send_ref):
-    width = kept_a.shape[-1]
-    for target, chosen in ((send_ref, 1 - place[0]), (keep_ref, place[0])):
-        for at in range(target.shape[0]):
-            target[at, :, :width] = added(kept_a[chosen, at], arrived_a[chosen, at])
-            target[at, :, width:] = added(kept_b[chosen, at], arrived_b[chosen, at])
-
-
-def fold_columns(first, second, place):
-    _, z_count, block, width = first[0].shape
-    outs = [((z_count, block, 2 * width), jnp.bfloat16)] * 2
-    return call(fold_columns_kernel, "fold_columns", 6, 0, outs, [], place, *first, *second, smem=1)
-
-
-def fold_rows_kernel(place, kept_a, arrived_a, kept_b, arrived_b, keep_ref, send_ref):
-    rows = kept_a.shape[1]
-    for target, chosen in ((send_ref, 1 - place[0]), (keep_ref, place[0])):
-        target[:rows] = added(kept_a[chosen], arrived_a[chosen])
-        target[rows:] = added(kept_b[chosen], arrived_b[chosen])
-
-
-def fold_rows(first, second, place):
-    _, block, width = first[0].shape
-    outs = [((2 * block, width), jnp.bfloat16)] * 2
-    return call(fold_rows_kernel, "fold_rows", 4, 0, outs, [], place, *first, *second, smem=1)
 
 
 def stream_fold_kernel(place, kept_keep, kept_send, arrived_keep, arrived_send, keep_ref, send_ref):
@@ -1145,6 +1223,7 @@
     mine = ctx_at // half
     y_at, core_at = ctx_at // 2, ctx_at % 2
     signed = lax.axis_index("section") == 0
+    which = signed.astype(jnp.int32)[None]
     place = core_at[None].astype(jnp.int32)
     y_place = y_at[None].astype(jnp.int32)
     z_at = lax.axis_index("dp")
@@ -1170,30 +1249,23 @@
 
     meta = slot_meta(slots_of(ctx_at), slots_of(ctx_at ^ 1), signed)
 
-    def through_attention(entry, keep):
-        normed, queries, kv = front(entry, gain_pair, biases, w_qkv)
-        there = swap_cores(kv)
-        normed_t = None
-        if keep:
-            normed_t = flip(normed, pltpu.HBM)
-            there, normed_t = barrier((there, normed_t))
-        attended, lse = sorted_attend(meta, queries, kv, there)
-        return normed_t, queries, kv, there, attended, lse
-
     inputs, meta = barrier((inputs, meta))
     first = gathered(inputs[:, 0])
     qkv_t, out_t = flip(w_qkv, pltpu.HBM), flip(w_out, pltpu.HBM)
     first, qkv_t, out_t = barrier((first, qkv_t, out_t))
-    attended = through_attention(first, False)[4]
+    _, queries, kv = front(first, gain_pair, biases, w_qkv)
+    attended, _ = sorted_attend(meta, queries, kv, swap_cores(kv))
     sent = rest(first, attended, gain_pair, biases, w_out, w_up, w_down)
     sent, later = barrier((sent, (cotangent, w_up, w_down)))
     arrived = shifted(sent, "section", 1)
     given = gathered(later[0][:, 0])
     up_t, down_t = [flip(weight, pltpu.HBM) for weight in later[1:]]
     arrived, given, up_t, down_t = barrier((arrived, given, up_t, down_t))
-    entry = jnp.where(signed, first, arrived)
-
-    normed_t, queries, kv, kv_there, attended, lse = through_attention(entry, True)
+    entry, normed, queries, kv = chosen_front(which, first, arrived, gain_pair, biases, w_qkv)
+    kv_there = swap_cores(kv)
+    normed_t = flip(normed, pltpu.HBM)
+    kv_there, normed_t = barrier((kv_there, normed_t))
+    attended, lse = sorted_attend(meta, queries, kv, kv_there)
     middle, normed_two, active, slope, grad_middle, grad_att = turn(
         entry, attended, given, gain_pair, biases, w_out, w_up, out_t, up_t, down_t
     )
@@ -1214,7 +1286,6 @@
     up_t, down_t = [flip(in_hbm(weight), pltpu.VMEM) for weight in weights]
     active_t = flip(active, pltpu.VMEM)
     back, up_t, down_t, active_t = barrier((back, up_t, down_t, active_t))
-    back = jnp.where(signed, back, given)
 
     z_steps = [1 << at for at in range(z_count.bit_length() - 1)]
     split = [2] * len(z_steps)
@@ -1223,63 +1294,75 @@
     def bits(value, before):
         return value.reshape(value.shape[:before] + tuple(split) + value.shape[before + 1 :])
 
-    grad_hidden, grad_middle, grad_att, sums_two, up_sum = down_back(
-        back, slope, middle, gain_pair, out_t, up_t, down_t
+    places = jnp.concatenate([place, y_place, by_z[0]])
+    back, grad_hidden, grad_middle, grad_att, sums_two, up_sum = down_back(
+        which, back, given, slope, middle, gain_pair, out_t, up_t, down_t
     )
     back, grad_hidden = barrier((back, grad_hidden))
-    down_kept, down_sent = down_grad(place, active_t, back, z_count)
-    grad_hidden, down_sent = barrier((grad_hidden, down_sent))
-    down_there = swap_cores(down_sent)
-    up_kept, up_sent = up_grad(place, normed_two_t, grad_hidden, z_count)
-    down_there, up_sent = barrier((down_there, up_sent))
-    up_there = swap_cores(up_sent)
-    down_kept, down_sent = stream_fold(down_kept, down_there, y_place, 0)
-    up_there, down_sent = barrier((up_there, down_sent))
-    up_kept, up_sent = stream_fold(bits(up_kept, 1), bits(up_there, 1), by_z[0], len(split))
-    grad_att, down_sent, up_sent = barrier((grad_att, down_sent, up_sent))
-    down_there, up_there = swap_halves(down_sent), swap_z(up_sent, z_steps[0])
+    down_there = down_sent(places, active_t, back, z_count)
+    grad_hidden, down_there = barrier((grad_hidden, down_there))
+    down_there = swap_cores(down_there)
+    up_there = up_sent(places, normed_two_t, grad_hidden, z_count)
+    down_there, up_there = barrier((down_there, up_there))
+    up_there = swap_cores(up_there)
+    down_keep, down_send = down_kept(places, active_t, back, down_there, z_count)
+    up_there, down_send = barrier((up_there, down_send))
+    up_keep, up_send = up_kept(places, normed_two_t, grad_hidden, up_there, z_count)
+    grad_att, down_send, up_send = barrier((grad_att, down_send, up_send))
+    down_there, up_there = swap_halves(down_send), swap_z(up_send, z_steps[0])
     grad_q, own, sent = sorted_attend_back(meta, queries, kv, kv_there, attended, grad_att, lse)
 
     grad_q, own, sent, down_there, up_there = barrier((grad_q, own, sent, down_there, up_there))
     there = swap_cores(sent)
-    outer_kept, outer_sent = outer_grad(place, attended_t, normed_t, grad_middle, grad_q, z_count)
-    there, outer_sent = barrier((there, outer_sent))
-    outer_there = swap_cores(outer_sent)
-    inner_kept, inner_sent = inner_grad(place, normed_t, own, there, z_count)
-    inner_sent, down_there, up_there = barrier((inner_sent, down_there, up_there))
-    inner_there = swap_cores(inner_sent)
-    down_kept, down_sent = fold(bits(down_kept, 0), bits(down_there, 0), by_z[0], len(split) - 1)
-    up_kept, up_sent = fold(up_kept, up_there, by_z[1], 1)
-    outer_there, inner_there, down_sent, up_sent = barrier((outer_there, inner_there, down_sent, up_sent))
-    rest_kept, rest_sent = fold_columns((outer_kept, outer_there), (inner_kept, inner_there), y_place)
-    rest_sent, down_sent, up_sent, grad_q, own, there = barrier((rest_sent, down_sent, up_sent, grad_q, own, there))
-    rest_there, down_there, up_there = swap_halves(rest_sent), swap_z(down_sent, z_steps[0]), swap_z(up_sent, z_steps[1])
+    outer_there = outer_sent(places, attended_t, normed_t, grad_middle, grad_q, z_count)
+    there, outer_there = barrier((there, outer_there))
+    outer_there = swap_cores(outer_there)
+    inner_there = inner_sent(places, normed_t, own, there, z_count)
+    inner_there, down_there, up_there = barrier((inner_there, down_there, up_there))
+    inner_there = swap_cores(inner_there)
+    down_keep, down_send = stream_fold(bits(down_keep, 0), bits(down_there, 0), by_z[0], len(split) - 1)
+    up_keep, up_send = stream_fold(up_keep, up_there, by_z[1], 1)
+    outer_there, inner_there, down_send, up_send = barrier((outer_there, inner_there, down_send, up_send))
+    rest_keep, rest_send = rest_kept(
+        places, attended_t, normed_t, grad_middle, grad_q, own, there, outer_there, inner_there, z_count
+    )
+    rest_send, down_send, up_send, grad_q, own, there = barrier((rest_send, down_send, up_send, grad_q, own, there))
+    rest_there, down_there, up_there = swap_halves(rest_send), swap_z(down_send, z_steps[0]), swap_z(up_send, z_steps[1])
     input_gradient, sums_one = front_back(grad_q, own, there, entry, grad_middle, gain_pair, qkv_t, wide)
     small = jnp.concatenate([sums_one, sums_two, up_sum], axis=0)
     small = small + swap_cores(small)
     rounded = input_gradient.astype(narrow)
-    small, rounded = barrier((small, rounded))
-    small = small + swap_z(small, z_steps[0])
-    rest_there, down_there, up_there, small = barrier((rest_there, down_there, up_there, small))
-
-    rest_kept, rest_sent = fold(bits(rest_kept, 0), bits(rest_there, 0), by_z[0], len(split) - 1)
-    rest_there = swap_z(rest_sent, z_steps[0])
-    down_kept, down_sent = fold(down_kept, down_there, by_z[1], 0)
-    up_kept, up_sent = fold(up_kept, up_there, y_place, 0)
-    down_there, up_there = swap_z(down_sent, z_steps[1]), swap_halves(up_sent)
-    small_there = swap_z(small, z_steps[1])
-    rest_there, up_there, small_there, rounded = barrier((rest_there, up_there, small_there, rounded))
-    rest_kept, rest_sent = fold(rest_kept, rest_there, by_z[1], 0)
+    small_there = swap_halves(small)
+    down_there, rounded = barrier((down_there, rounded))
+    down_keep, down_send = fold(down_keep, down_there, by_z[1], 0)
+    down_send, rest_there, small_there = barrier((down_send, rest_there, small_there))
+    down_there = swap_z(down_send, z_steps[1])
+
+    rest_keep, rest_send = fold(bits(rest_keep, 0), bits(rest_there, 0), by_z[0], len(split) - 1)
     small = small + small_there
-    rest_sent, small, rounded, result, acts_there = barrier((rest_sent, small, rounded, result, acts_there))
-    rest_there = swap_z(rest_sent, z_steps[1])
-    small = small + swap_halves(small)
+    rest_send, up_there, small = barrier((rest_send, up_there, small))
+    rest_there, small_there = swap_z(rest_send, z_steps[0]), swap_z(small, z_steps[0])
+    up_keep, up_send = fold(up_keep, up_there, y_place, 0)
+    up_there = swap_halves(up_send)
+    rounded, up_send = barrier((rounded, up_send))
     grads_there = swap_halves(rounded[rows:])
-    wdown = wide_sum(down_kept, down_there)
-    wup = wide_sum(up_kept, up_there)
+    rest_there, up_there, small_there, down_there, grads_there = barrier(
+        (rest_there, up_there, small_there, down_there, grads_there)
+    )
+    rest_keep, rest_send = fold(rest_keep, rest_there, by_z[1], 0)
+    rest_send, small_there, grads_there, result, acts_there = barrier(
+        (rest_send, small_there, grads_there, result, acts_there)
+    )
+    rest_there = swap_z(rest_send, z_steps[1])
+    small = small + small_there
+    small = small + swap_z(small, z_steps[1])
+    wdown = wide_sum(down_keep, down_there)
+    wup = wide_sum(up_keep, up_there)
     grads_kept = jnp.where(signed, input_gradient[:rows], rounded[:rows].astype(wide))
-    wout = wide_sum(rest_kept[:, :D], rest_there[:, :D])
-    wqkv = wide_sum(rest_kept[:, D:], rest_there[:, D:])
+    grad_rows = returned(grads_kept, grads_there)
+    grad_rows, rest_there = barrier((grad_rows, rest_there))
+    wout = wide_sum(rest_keep[:, :D], rest_there[:, :D])
+    wqkv = wide_sum(rest_keep[:, D:], rest_there[:, D:])
     blocks = count * z_count
     block_at = lax.axis_index("dp") * count + ctx_at
     gain_piece = lax.dynamic_slice_in_dim(small[0:5:4], block_at * (D // blocks), D // blocks, 1)
@@ -1288,7 +1371,7 @@
     bias_piece = lax.dynamic_slice_in_dim(bias_row, block_at * width, width, 0)
     return (
         returned(result[:rows], acts_there)[None, :, None],
-        returned(grads_kept, grads_there)[None, :, None],
+        grad_rows[None, :, None],
         gain_piece[None],
         bias_piece[None],
         wqkv[None],

time: 297 us -> 287 us (0.966)
  local copies, waits for them, and re-layouts: 20.2 us -> 9.03 us
  waiting for transfers between devices: 78 us -> 83.3 us
  other arithmetic: 14 us -> 10.3 us
    unnamed x155 -> x133, local copies, waits for them, and re-layouts: 16.6 us -> 5.44 us
    pallas_call x13, Pallas kernels: 29.1 us -> 36 us  [call(): pl.pallas_call(kernel, in_specs=[SMEM_SPEC] * smem + [VMEM_SPEC] * (len(o...]
    ppermute x9, waiting for transfers between devices: 7.03 us -> 11.9 us  [swap_cores(): lax.ppermute(value, 'ctx', [(at, at ^ 1) for at in range(lax.axis_size('c...]
  transfers between devices with their start and end apart: 27 -> 27, of which waited for: 16 -> 20; matrix products, arithmetic and copies ran while one was open for 5% -> 5% of each run, Pallas kernels for 20% -> 21%
where the time goes in v4:
time: 287 us; the launch traced here: 284 us
  Pallas kernels  148 us (52%)
  waiting for transfers between devices  83.3 us (29%)
  starting transfers between devices  28.6 us (10%)
  other arithmetic  10.3 us (4%)
  local copies, waits for them, and re-layouts  9.03 us (3%)
    ppermute x8, waiting for transfers between devices, swap_z(): lax.ppermute(value, 'dp', [(at, at ^ step) for at in range(lax.axis_size(...  40.6 us
    pallas_call x13, Pallas kernels, call(): pl.pallas_call(kernel, in_specs=[SMEM_SPEC] * smem + [VMEM_SPEC] * (len(o...  36 us
    pallas_call x2, Pallas kernels, sorted_attend(): pl.pallas_call(functools.partial(forward_kernel, span=span), in_specs=[SM...  35.4 us
    pallas_call x2, Pallas kernels, sorted_attend_back(): pl.pallas_call(functools.partial(backward_kernel, span=span), in_specs=[S...  24.1 us
    pallas_call x10, Pallas kernels, flip(): pl.pallas_call(flip_kernel, grid=(grid,), in_specs=[in_spec], out_specs=o...  23.7 us
    ppermute x2, waiting for transfers between devices, shifted(): lax.ppermute(value, axis, [(source, source + steps) for source in range(i...  19.3 us
    pallas_call x4, Pallas kernels, grid_call(): pl.pallas_call(kernel, grid_spec=pltpu.PrefetchScalarGridSpec(num_scalar_...  13.2 us
    ppermute x8, starting transfers between devices, swap_z(): lax.ppermute(value, 'dp', [(at, at ^ step) for at in range(lax.axis_size(...  12.5 us
  transfers between devices with their start and end apart: 27, of which 20 were waited for; matrix products, arithmetic and copies ran while one was open for 5% of the time, Pallas kernels for 21%

profile of v4, /device:TPU:0, one launch (start us, length us, event | category | flops | bytes accessed | tf_op | source)
XLA Modules:
  0.0 283.8 jit_solution(16585721119822160825)
XLA Ops:
  3.1 3.0 %collective-permute-start = (bf16[256,768]{1,0:T(8,128)(2,1)S(1)}, bf16[256,768]{1,0:T(8,128)(2,1)S(1)}, u32[]{:S(2)}, u32[]{:S(2)}) collective-permute-start(bf16[256,768]{1,0:T(8,128)(2,1)S(1)} %get-tuple-element.321), channel_id=1, source_target_pairs={{0,2},{1,3},{2,0},{3,1},{4,6},{5,7},{6,4},{7,5},{8,10},{9,11},{10,... | collective-permute-start | bytes 1179656 | tf_op jit(solution)/shard_map/ppermute | solution.py:1202
  6.1 2.0 copy-done.2
  8.2 2.9 %flip.10.qkv_t = bf16[2304,768]{1,0:T(8,128)(2,1)} custom-call(bf16[1,768,2304]{2,1,0:T(8,128)(2,1)S(1)} %copy-done.2), custom_call_target="tpu_custom_call" | custom-call | tf_op jit(solution)/shard_map/flip/pallas_call | solution.py:380
  12.5 2.8 collective-permute-done
  15.4 2.4 front.1
  17.9 3.4 %collective-permute-done.1.kv2_ref = bf16[512,1536]{1,0:T(8,128)(2,1)S(1)} collective-permute-done((bf16[512,1536]{1,0:T(8,128)(2,1)S(1)}, bf16[512,1536]{1,0:T(8,128)(2,1)S(1)}, u32[]{:S(2)}, u32[]{:S(2)}) %collective-permute-start.1) | collective-permute-done | bytes 1572896 | tf_op jit(solution)/shard_map/ppermute | solution.py:1206
  21.3 12.1 %attend.2 = (bf16[512,768]{1,0:T(8,128)(2,1)S(1)}, f32[6,4,256]{2,1,0:T(4,128)}) custom-call(s32[17]{0:T(128)S(1)} %concatenate.26.meta, bf16[512,768]{1,0:T(8,128)(2,1)S(1)} %get-tuple-element.157.q_ref, bf16[512,1536]{1,0:T(8,128)(2,1)S(1)} %get-tuple-element.158.kv_ref, bf16[512,1536]{1,0:T(8,128)(2,1)S(1)} %collective-permute-done.1.kv2_ref), custom_call_target="tpu_custom_call" | custom-call | flops 4000000000 | tf_op jit(solution)/shard_map/attend/pallas_call | solution.py:160
  33.4 6.6 %rest.1 = bf16[512,768]{1,0:T(8,128)(2,1)S(1)} custom-call(bf16[512,768]{1,0:T(8,128)(2,1)S(1)} %pad_maximum_fusion.1.x_ref.first_ref, bf16[512,768]{1,0:T(8,128)(2,1)S(1)} %get-tuple-element.159.o_ref, f32[2,768]{1,0:T(2,128)S(1)} %bitcast.94, f32[1,7680]{1,0:T(1,128)S(1)} %copy-done.37, bf16[1,768,768]{2,1,0:T(8,128)(2,1)S(1)} %copy-done.12, ...), custom_call_target="tpu_custom_call" | custom-call | flops 679477248 | tf_op jit(solution)/shard_map/rest/pallas_call | solution.py:320
  41.5 1.8 collective-permute-start.3
  43.3 3.4 %flip.12.up_t = bf16[3072,768]{1,0:T(8,128)(2,1)} custom-call(bf16[1,768,3072]{2,1,0:T(8,128)(2,1)S(1)} %bitcast.76), custom_call_target="tpu_custom_call" | custom-call | tf_op jit(solution)/shard_map/flip/pallas_call | solution.py:380
  46.7 3.3 %flip.13.down_t = bf16[768,3072]{1,0:T(8,128)(2,1)} custom-call(bf16[1,3072,768]{2,1,0:T(8,128)(2,1)S(1)} %bitcast.80), custom_call_target="tpu_custom_call" | custom-call | tf_op jit(solution)/shard_map/flip/pallas_call | solution.py:380
  50.0 2.7 collective-permute-done.3
  52.8 5.9 %collective-permute-done.2.second_ref = bf16[512,768]{1,0:T(8,128)(2,1)S(1)} collective-permute-done((bf16[512,768]{1,0:T(8,128)(2,1)S(1)}, bf16[512,768]{1,0:T(8,128)(2,1)S(1)}, u32[]{:S(2)}, u32[]{:S(2)}) %collective-permute-start.2) | collective-permute-done | bytes 786464 | tf_op jit(solution)/shard_map/ppermute | solution.py:848
  58.7 3.2 %chosen_front.1 = (bf16[512,768]{1,0:T(8,128)(2,1)S(1)}, bf16[512,768]{1,0:T(8,128)(2,1)S(1)}, bf16[512,768]{1,0:T(8,128)(2,1)S(1)}, bf16[512,1536]{1,0:T(8,128)(2,1)}) custom-call(s32[1]{0:T(128)} %bitcast.8.which, bf16[512,768]{1,0:T(8,128)(2,1)S(1)} %pad_maximum_fusion.1.x_ref.first_ref, bf16[512,768]{1,0:T(8,128)(2,1)S(1)} %collective-permute-done.2.second_ref, ...), custom_call_target="tpu_custom_call" | custom-call | flops 226492416 | tf_op jit(solution)/shard_map/chosen_front/pallas_call | solution.py:320
  64.0 2.6 collective-permute-done.4.kv2_ref
  66.6 23.4 %attend.3 = (bf16[512,768]{1,0:T(8,128)(2,1)S(1)}, f32[6,4,256]{2,1,0:T(4,128)S(1)}) custom-call(s32[17]{0:T(128)S(1)} %concatenate.26.meta, bf16[512,768]{1,0:T(8,128)(2,1)S(1)} %copy-done.45, bf16[512,1536]{1,0:T(8,128)(2,1)} %get-tuple-element.166.kv_ref, bf16[512,1536]{1,0:T(8,128)(2,1)} %collective-permute-done.4.kv2_ref), custom_call_target="tpu_custom_call" | custom-call | flops 4000000000 | tf_op jit(solution)/shard_map/attend/pallas_call | solution.py:160
  90.1 11.9 %turn.1 = (f32[512,768]{1,0:T(8,128)}, bf16[512,768]{1,0:T(8,128)(2,1)}, bf16[512,3072]{1,0:T(8,128)(2,1)}, bf16[512,3072]{1,0:T(8,128)(2,1)}, bf16[512,768]{1,0...) custom-call(bf16[512,768]{1,0:T(8,128)(2,1)S(1)} %get-tuple-element.170.x_ref, ...), custom_call_target="tpu_custom_call" | custom-call | flops 1056964608 | tf_op jit(solution)/shard_map/turn/pallas_call | solution.py:501
  102.0 2.9 %attend_back.2 = (bf16[512,768]{1,0:T(8,128)(2,1)S(1)}, bf16[2,512,768]{2,1,0:T(8,128)(2,1)S(1)}, bf16[2,512,768]{2,1,0:T(8,128)(2,1)S(1)}) custom-call(s32[17]{0:T(128)S(1)} %constant_dynamic-update-slice_fusion.meta, bf16[512,768]{1,0:T(8,128)(2,1)S(1)} %copy-done.45, bf16[512,1536]{1,0:T(8,128)(2,1)} %get-tuple-element.166.kv_ref, ...), custom_call_target="tpu_custom_call" | custom-call | flops 8000000000 | tf_op jit(solution)/shard_map/attend_back/pallas_call | solution.py:251
  108.4 3.7 %front_back.2 = (bf16[512,768]{1,0:T(8,128)(2,1)}, f32[4,768]{1,0:T(4,128)}) custom-call(bf16[512,768]{1,0:T(8,128)(2,1)S(1)} %get-tuple-element.185.q_ref, bf16[2,512,768]{2,1,0:T(8,128)(2,1)S(1)} %get-tuple-element.186.own_ref, bf16[2,512,768]{2,1,0:T(8,128)(2,1)S(1)} %collective-permute-done.5.there_ref, bf16[512,768]{1,0:T(8,128)(2,1)S(1)} %copy-done.25, ...), custom_call_target="tpu_custom_call" | custom-call | flops 226492416 | tf_op jit(solution)/shard_map/front_back/pallas_call | solution.py:320
  113.4 2.6 add_convert_fusion
  117.8 1.7 collective-permute-start.7
  119.6 3.7 %flip.17.up_t = bf16[3072,768]{1,0:T(8,128)(2,1)S(1)} custom-call(bf16[1,768,3072]{2,1,0:T(8,128)(2,1)} %in_ref.6), custom_call_target="tpu_custom_call" | custom-call | tf_op jit(solution)/shard_map/flip/pallas_call | solution.py:380
  123.4 4.3 %flip.18.down_t = bf16[768,3072]{1,0:T(8,128)(2,1)S(1)} custom-call(bf16[1,3072,768]{2,1,0:T(8,128)(2,1)} %in_ref.7), custom_call_target="tpu_custom_call" | custom-call | tf_op jit(solution)/shard_map/flip/pallas_call | solution.py:380
  130.6 13.3 %collective-permute-done.6.first_ref = bf16[512,768]{1,0:T(8,128)(2,1)} collective-permute-done((bf16[512,768]{1,0:T(8,128)(2,1)}, bf16[512,768]{1,0:T(8,128)(2,1)}, u32[]{:S(2)}, u32[]{:S(2)}) %collective-permute-start.6) | collective-permute-done | bytes 786464 | tf_op jit(solution)/shard_map/ppermute | solution.py:848
  143.9 8.2 %down_back.1 = (bf16[512,768]{1,0:T(8,128)(2,1)S(1)}, bf16[512,3072]{1,0:T(8,128)(2,1)S(1)}, bf16[512,768]{1,0:T(8,128)(2,1)S(1)}, bf16[512,768]{1,0:T(8,128)(2,...) custom-call(s32[1]{0:T(128)} %bitcast.8.which, bf16[512,768]{1,0:T(8,128)(2,1)} %collective-permute-done.6.first_ref, ...), custom_call_target="tpu_custom_call" | custom-call | flops 679477248 | tf_op jit(solution)/shard_map/down_back/pallas_call | solution.py:320
  152.2 2.6 down_sent.1
  154.9 2.9 %up_sent.1 = bf16[2,4,48,3072]{3,2,1,0:T(8,128)(2,1)S(1)} custom-call(s32[3]{0:T(128)S(1)} %pad_add_fusion.place, bf16[768,512]{1,0:T(8,128)(2,1)S(1)} %copy-done.21, bf16[512,3072]{1,0:T(8,128)(2,1)S(1)} %get-tuple-element.213.right_ref), custom_call_target="tpu_custom_call" | custom-call | flops 150994944 | tf_op jit(solution)/shard_map/up_sent/pallas_call | solution.py:631
  157.7 1.6 collective-permute-done.8.there_ref
  159.5 3.7 %down_kept.1 = (bf16[4,192,768]{2,1,0:T(8,128)(2,1)}, bf16[4,192,768]{2,1,0:T(8,128)(2,1)S(1)}) custom-call(s32[3]{0:T(128)S(1)} %pad_add_fusion.place, bf16[3072,512]{1,0:T(8,128)(2,1)S(1)} %flip.19.left_ref, bf16[512,768]{1,0:T(8,128)(2,1)S(1)} %get-tuple-element.210.right_ref, bf16[2,4,192,768]{3,2,1,0:T(8,128)(2,1)S(1)} %collective-permute-done.8.there_ref), custom_call_target="tpu_custom_call" | custom-call | flops 150994944 | tf_op jit(solution)/shard_map/down_kept/pallas_call | solution.py:631
  163.9 4.0 %up_kept.1 = (bf16[2,2,48,3072]{3,2,1,0:T(8,128)(2,1)}, bf16[2,2,48,3072]{3,2,1,0:T(8,128)(2,1)S(1)}) custom-call(s32[3]{0:T(128)S(1)} %pad_add_fusion.place, bf16[768,512]{1,0:T(8,128)(2,1)S(1)} %copy-done.21, bf16[512,3072]{1,0:T(8,128)(2,1)S(1)} %get-tuple-element.213.right_ref, bf16[2,4,48,3072]{3,2,1,0:T(8,128)(2,1)S(1)} %collective-permute-done.9.there_ref), custom_call_target="tpu_custom_call" | custom-call | flops 150994944 | tf_op jit(solution)/shard_map/up_kept/pallas_call | solution.py:631
  167.9 1.7 collective-permute-start.10
  171.3 21.2 %attend_back.3 = (bf16[512,768]{1,0:T(8,128)(2,1)S(1)}, bf16[2,512,768]{2,1,0:T(8,128)(2,1)S(1)}, bf16[2,512,768]{2,1,0:T(8,128)(2,1)S(1)}) custom-call(s32[17]{0:T(128)S(1)} %concatenate.26.meta, bf16[512,768]{1,0:T(8,128)(2,1)S(1)} %copy-done.46, bf16[512,1536]{1,0:T(8,128)(2,1)} %get-tuple-element.166.kv_ref, ...), custom_call_target="tpu_custom_call" | custom-call | flops 8000000000 | tf_op jit(solution)/shard_map/attend_back/pallas_call | solution.py:251
  192.5 3.5 %collective-permute-done.10 = bf16[4,192,768]{2,1,0:T(8,128)(2,1)S(1)} collective-permute-done((bf16[4,192,768]{2,1,0:T(8,128)(2,1)S(1)}, bf16[4,192,768]{2,1,0:T(8,128)(2,1)S(1)}, u32[]{:S(2)}, u32[]{:S(2)}) %collective-permute-start.10) | collective-permute-done | bytes 1179680 | tf_op jit(solution)/shard_map/ppermute | solution.py:1202
  197.4 2.4 outer_sent.1
  200.8 2.4 inner_sent.1
  203.8 1.9 stream_fold.2
  205.7 1.9 stream_fold.3
  208.7 3.6 %rest_kept.1 = (bf16[4,48,3072]{2,1,0:T(8,128)(2,1)S(1)}, bf16[4,48,3072]{2,1,0:T(8,128)(2,1)S(1)}) custom-call(s32[3]{0:T(128)S(1)} %pad_add_fusion.place, bf16[768,512]{1,0:T(8,128)(2,1)S(1)} %copy-done.16, bf16[768,512]{1,0:T(8,128)(2,1)S(1)} %copy-done.11, bf16[512,768]{1,0:T(8,128)(2,1)S(1)} %copy-done.18, bf16[512,768]{1,0:T(8,128)(2,1)S(1)} %copy-done.23, ...), custom_call_target="tpu_custom_call" | custom-call | flops 150994944 | tf_op jit(solution)/shard_map/rest_kept/pallas_call | solution.py:320
  212.7 1.7 collective-permute-start.15
  214.5 2.6 collective-permute-start.19
  217.1 2.7 front_back.3
  222.9 17.5 %collective-permute-done.15 = bf16[2,192,768]{2,1,0:T(8,128)(2,1)S(1)} collective-permute-done((bf16[2,192,768]{2,1,0:T(8,128)(2,1)S(1)}, bf16[2,192,768]{2,1,0:T(8,128)(2,1)S(1)}, u32[]{:S(2)}, u32[]{:S(2)}) %collective-permute-start.15) | collective-permute-done | bytes 589856 | tf_op jit(solution)/shard_map/ppermute | solution.py:1210
  245.7 2.6 collective-permute-start.23
  248.7 15.0 %collective-permute-done.22 = f32[12,768]{1,0:T(8,128)S(1)} collective-permute-done((f32[12,768]{1,0:T(8,128)S(1)}, f32[12,768]{1,0:T(8,128)S(1)}, u32[]{:S(2)}, u32[]{:S(2)}) %collective-permute-start.22) | collective-permute-done | bytes 36896 | tf_op jit(solution)/shard_map/ppermute | solution.py:1210
  263.9 2.7 collective-permute-start.25
  266.9 1.8 fusion.6
  268.8 1.8 fusion.7
  275.1 5.5 %collective-permute-done.26 = f32[12,768]{1,0:T(8,128)S(1)} collective-permute-done((f32[12,768]{1,0:T(8,128)S(1)}, f32[12,768]{1,0:T(8,128)S(1)}, u32[]{:S(2)}, u32[]{:S(2)}) %collective-permute-start.26) | collective-permute-done | bytes 36896 | tf_op jit(solution)/shard_map/ppermute | solution.py:1210
  (217 shorter events, 40.5 us)
Async XLA Ops:
  3.1 12.1 %collective-permute-start = (bf16[256,768]{1,0:T(8,128)(2,1)S(1)}, bf16[256,768]{1,0:T(8,128)(2,1)S(1)}, u32[]{:S(2)}, u32[]{:S(2)}) collective-permute-start(bf16[256,768]{1,0:T(8,128)(2,1)S(1)} %get-tuple-element.321), channel_id=1, source_target_pairs={{0,2},{1,3},{2,0},{3,1},{4,6},{5,7},{6,4},{7,5},{8,10},{9,11},{10,... | collective-permute-start | bytes 1179656 | tf_op jit(solution)/shard_map/ppermute | solution.py:1202
  15.3 18.0 %slice-start = ((s8[4718592]{0:T(1024)(128)(4,1)}), s8[4194304]{0:T(1024)(128)(4,1)S(1)}, s32[]{:S(2)}) async-start(s8[4718592]{0:T(1024)(128)(4,1)} %bitcast.75), calls=%async_computation | async-start | bytes 8388608
  15.4 18.0 %slice-start.4 = ((s8[4718592]{0:T(1024)(128)(4,1)}), s8[4194304]{0:T(1024)(128)(4,1)S(1)}, s32[]{:S(2)}) async-start(s8[4718592]{0:T(1024)(128)(4,1)} %bitcast.79), calls=%async_computation.4 | async-start | bytes 8388608
  17.8 3.5 %collective-permute-start.1 = (bf16[512,1536]{1,0:T(8,128)(2,1)S(1)}, bf16[512,1536]{1,0:T(8,128)(2,1)S(1)}, u32[]{:S(2)}, u32[]{:S(2)}) collective-permute-start(bf16[512,1536]{1,0:T(8,128)(2,1)S(1)} %get-tuple-element.158.kv_ref), channel_id=1, source_target_pairs={{0,1},{1,0},{2,3},{3,2},{4,5},{5,4},{6,7},{7,6},{8,9},{9,8},{10,11... | collective-permute-start | bytes 4718600 | tf_op jit(solution)/shard_map/ppermute | solution.py:1206
  40.0 18.7 %collective-permute-start.2 = (bf16[512,768]{1,0:T(8,128)(2,1)S(1)}, bf16[512,768]{1,0:T(8,128)(2,1)S(1)}, u32[]{:S(2)}, u32[]{:S(2)}) collective-permute-start(bf16[512,768]{1,0:T(8,128)(2,1)S(1)} %rest.1), channel_id=1, source_target_pairs={{0,16},{1,17},{2,18},{3,19},{4,20},{5,21},{6,22},{7,23},{8,24},{9,... | collective-permute-start | bytes 2359304 | tf_op jit(solution)/shard_map/ppermute | solution.py:848
  41.5 11.2 %collective-permute-start.3 = (bf16[256,768]{1,0:T(8,128)(2,1)S(1)}, bf16[256,768]{1,0:T(8,128)(2,1)S(1)}, u32[]{:S(2)}, u32[]{:S(2)}) collective-permute-start(bf16[256,768]{1,0:T(8,128)(2,1)S(1)} %get-tuple-element.319), channel_id=1, source_target_pairs={{0,2},{1,3},{2,0},{3,1},{4,6},{5,7},{6,4},{7,5},{8,10},{9,11},{10,... | collective-permute-start | bytes 1179656 | tf_op jit(solution)/shard_map/ppermute | solution.py:1202
  52.8 37.2 %copy-start.19 = (bf16[512,768]{1,0:T(8,128)(2,1)}, bf16[512,768]{1,0:T(8,128)(2,1)S(1)}, u32[]{:S(2)}) copy-start(bf16[512,768]{1,0:T(8,128)(2,1)S(1)} %pad_maximum_fusion.2.d_ref.second_ref) | copy-start | bytes 2359300
  62.8 27.2 %copy-start.24 = (bf16[512,768]{1,0:T(8,128)(2,1)}, bf16[512,768]{1,0:T(8,128)(2,1)S(1)}, u32[]{:S(2)}) copy-start(bf16[512,768]{1,0:T(8,128)(2,1)S(1)} %get-tuple-element.170.x_ref) | copy-start | bytes 2359300
  62.8 3.8 %collective-permute-start.4 = (bf16[512,1536]{1,0:T(8,128)(2,1)}, bf16[512,1536]{1,0:T(8,128)(2,1)}, u32[]{:S(2)}, u32[]{:S(2)}) collective-permute-start(bf16[512,1536]{1,0:T(8,128)(2,1)} %get-tuple-element.166.kv_ref), channel_id=1, source_target_pairs={{0,1},{1,0},{2,3},{3,2},{4,5},{5,4},{6,7},{7,6},{8,9},{9,8},{10,11... | collective-permute-start | bytes 4718600 | tf_op jit(solution)/shard_map/ppermute | solution.py:1206
  62.8 27.2 %copy-start.13 = (bf16[768,768]{1,0:T(8,128)(2,1)S(1)}, bf16[768,768]{1,0:T(8,128)(2,1)}, u32[]{:S(2)}) copy-start(bf16[768,768]{1,0:T(8,128)(2,1)} %flip.11.out_t) | copy-start | bytes 3538948
  66.6 23.5 %slice-start.2 = ((s8[4718592]{0:T(1024)(128)(4,1)}), s8[4194304]{0:T(1024)(128)(4,1)S(1)}, s32[]{:S(2)}) async-start(s8[4718592]{0:T(1024)(128)(4,1)} %bitcast.77), calls=%async_computation.2 | async-start | bytes 8388608
  66.6 23.5 %slice-start.8 = ((s8[4718592]{0:T(1024)(128)(4,1)}), s8[4194304]{0:T(1024)(128)(4,1)S(1)}, s32[]{:S(2)}) async-start(s8[4718592]{0:T(1024)(128)(4,1)} %bitcast.83), calls=%async_computation.8 | async-start | bytes 8388608
  66.6 23.5 %slice-start.3 = ((s8[4718592]{0:T(1024)(128)(4,1)}), s8[524288]{0:T(1024)(128)(4,1)S(1)}, s32[]{:S(2)}) async-start(s8[4718592]{0:T(1024)(128)(4,1)} %bitcast.77), calls=%async_computation.3 | async-start | bytes 1048576
  66.6 23.5 %slice-start.9 = ((s8[4718592]{0:T(1024)(128)(4,1)}), s8[524288]{0:T(1024)(128)(4,1)S(1)}, s32[]{:S(2)}) async-start(s8[4718592]{0:T(1024)(128)(4,1)} %bitcast.83), calls=%async_computation.9 | async-start | bytes 1048576
  66.6 23.5 %copy-start.5 = (bf16[768,3072]{1,0:T(8,128)(2,1)S(1)}, bf16[768,3072]{1,0:T(8,128)(2,1)}, u32[]{:S(2)}) copy-start(bf16[768,3072]{1,0:T(8,128)(2,1)} %flip.13.down_t) | copy-start | bytes 14155780
  66.6 23.5 %copy-start.38 = (f32[1,7680]{1,0:T(1,128)S(1)}, f32[1,7680]{1,0:T(1,128)}, u32[]{:S(2)}) copy-start(f32[1,7680]{1,0:T(1,128)} %biases.7) | copy-start | bytes 92164
  90.0 15.2 %copy-start.32 = (bf16[512,768]{1,0:T(8,128)(2,1)}, bf16[512,768]{1,0:T(8,128)(2,1)S(1)}, u32[]{:S(2)}) copy-start(bf16[512,768]{1,0:T(8,128)(2,1)S(1)} %get-tuple-element.181.o_ref.in_ref) | copy-start | bytes 2359300
  104.9 3.5 %collective-permute-start.5 = (bf16[2,512,768]{2,1,0:T(8,128)(2,1)S(1)}, bf16[2,512,768]{2,1,0:T(8,128)(2,1)S(1)}, u32[]{:S(2)}, u32[]{:S(2)}) collective-permute-start(bf16[2,512,768]{2,1,0:T(8,128)(2,1)S(1)} %get-tuple-element.180), channel_id=1, source_target_pairs={{0,1},{1,0},{2,3},{3,2},{4,5},{5,4},{6,7},{7,6},{8,9},{9,8},{10,11... | collective-permute-start | bytes 4718600 | tf_op jit(solution)/shard_map/ppermute | solution.py:1206
  112.1 31.8 %collective-permute-start.6 = (bf16[512,768]{1,0:T(8,128)(2,1)}, bf16[512,768]{1,0:T(8,128)(2,1)}, u32[]{:S(2)}, u32[]{:S(2)}) collective-permute-start(bf16[512,768]{1,0:T(8,128)(2,1)} %get-tuple-element.193), channel_id=1, source_target_pairs={{16,0},{17,1},{18,2},{19,3},{20,4},{21,5},{22,6},{23,7},{24,8},{25... | collective-permute-start | bytes 2359304 | tf_op jit(solution)/shard_map/ppermute | solution.py:848
  117.8 11.5 %collective-permute-start.7 = (bf16[256,768]{1,0:T(8,128)(2,1)}, bf16[256,768]{1,0:T(8,128)(2,1)}, u32[]{:S(2)}, u32[]{:S(2)}) collective-permute-start(bf16[256,768]{1,0:T(8,128)(2,1)} %slice.70), channel_id=1, source_target_pairs={{0,2},{1,3},{2,0},{3,1},{4,6},{5,7},{6,4},{7,5},{8,10},{9,11},{10,... | collective-permute-start | bytes 1179656 | tf_op jit(solution)/shard_map/ppermute | solution.py:1202
  123.3 20.5 %copy-start.35 = (f32[512,768]{1,0:T(8,128)S(1)}, f32[512,768]{1,0:T(8,128)}, u32[]{:S(2)}) copy-start(f32[512,768]{1,0:T(8,128)} %get-tuple-element.201.middle_ref) | copy-start | bytes 4718596
  127.6 16.2 %copy-start.14 = (bf16[768,768]{1,0:T(8,128)(2,1)S(1)}, bf16[768,768]{1,0:T(8,128)(2,1)}, u32[]{:S(2)}) copy-start(bf16[768,768]{1,0:T(8,128)(2,1)} %flip.11.out_t) | copy-start | bytes 3538948
  127.6 16.2 %copy-start.20 = (bf16[512,768]{1,0:T(8,128)(2,1)S(1)}, bf16[512,768]{1,0:T(8,128)(2,1)}, u32[]{:S(2)}) copy-start(bf16[512,768]{1,0:T(8,128)(2,1)} %copy-done.19) | copy-start | bytes 2359300
  129.3 14.6 %copy-start.29 = (bf16[512,3072]{1,0:T(8,128)(2,1)S(1)}, bf16[512,3072]{1,0:T(8,128)(2,1)}, u32[]{:S(2)}) copy-start(bf16[512,3072]{1,0:T(8,128)(2,1)} %get-tuple-element.200.slope_ref) | copy-start | bytes 9437188
  152.2 45.3 %copy-start.17 = (bf16[512,768]{1,0:T(8,128)(2,1)}, bf16[512,768]{1,0:T(8,128)(2,1)S(1)}, u32[]{:S(2)}) copy-start(bf16[512,768]{1,0:T(8,128)(2,1)S(1)} %get-tuple-element.204.d_ref.grad_ref) | copy-start | bytes 2359300
  154.8 4.6 %collective-permute-start.8 = (bf16[2,4,192,768]{3,2,1,0:T(8,128)(2,1)S(1)}, bf16[2,4,192,768]{3,2,1,0:T(8,128)(2,1)S(1)}, u32[]{:S(2)}, u32[]{:S(2)}) collective-permute-start(bf16[2,4,192,768]{3,2,1,0:T(8,128)(2,1)S(1)} %down_sent.1), channel_id=1, source_target_pairs={{0,1},{1,0},{2,3},{3,2},{4,5},{5,4},{6,7},{7,6},{8,9},{9,8},{10,11... | collective-permute-start | bytes 7077896 | tf_op jit(solution)/shard_map/ppermute | solution.py:1206
  159.4 4.5 %collective-permute-start.9 = (bf16[2,4,48,3072]{3,2,1,0:T(8,128)(2,1)S(1)}, bf16[2,4,48,3072]{3,2,1,0:T(8,128)(2,1)S(1)}, u32[]{:S(2)}, u32[]{:S(2)}) collective-permute-start(bf16[2,4,48,3072]{3,2,1,0:T(8,128)(2,1)S(1)} %up_sent.1), channel_id=1, source_target_pairs={{0,1},{1,0},{2,3},{3,2},{4,5},{5,4},{6,7},{7,6},{8,9},{9,8},{10,11... | collective-permute-start | bytes 7077896 | tf_op jit(solution)/shard_map/ppermute | solution.py:1206
  167.9 29.5 %copy-start.10 = (bf16[768,512]{1,0:T(8,128)(2,1)S(1)}, bf16[768,512]{1,0:T(8,128)(2,1)}, u32[]{:S(2)}) copy-start(bf16[768,512]{1,0:T(8,128)(2,1)} %flip.14.normed_ref) | copy-start | bytes 2359300
  167.9 29.5 %copy-start.15 = (bf16[768,512]{1,0:T(8,128)(2,1)S(1)}, bf16[768,512]{1,0:T(8,128)(2,1)}, u32[]{:S(2)}) copy-start(bf16[768,512]{1,0:T(8,128)(2,1)} %flip.15.o_ref) | copy-start | bytes 2359300
  167.9 28.0 %collective-permute-start.10 = (bf16[4,192,768]{2,1,0:T(8,128)(2,1)S(1)}, bf16[4,192,768]{2,1,0:T(8,128)(2,1)S(1)}, u32[]{:S(2)}, u32[]{:S(2)}) collective-permute-start(bf16[4,192,768]{2,1,0:T(8,128)(2,1)S(1)} %get-tuple-element.224), channel_id=1, source_target_pairs={{0,2},{1,3},{2,0},{3,1},{4,6},{5,7},{6,4},{7,5},{8,10},{9,11},{10,... | collective-permute-start | bytes 3538952 | tf_op jit(solution)/shard_map/ppermute | solution.py:1202
  169.7 27.7 %collective-permute-start.11 = (bf16[2,2,48,3072]{3,2,1,0:T(8,128)(2,1)S(1)}, bf16[2,2,48,3072]{3,2,1,0:T(8,128)(2,1)S(1)}, u32[]{:S(2)}, u32[]{:S(2)}) collective-permute-start(bf16[2,2,48,3072]{3,2,1,0:T(8,128)(2,1)S(1)} %get-tuple-element.225), channel_id=1, source_target_pairs={{0,4},{4,0},{8,12},{12,8},{1,5},{5,1},{9,13},{13,9},{2,6},{6,2},{1... | collective-permute-start | bytes 3538952 | tf_op jit(solution)/shard_map/ppermute | solution.py:1210
  197.4 3.4 %collective-permute-start.12 = (bf16[2,512,768]{2,1,0:T(8,128)(2,1)S(1)}, bf16[2,512,768]{2,1,0:T(8,128)(2,1)S(1)}, u32[]{:S(2)}, u32[]{:S(2)}) collective-permute-start(bf16[2,512,768]{2,1,0:T(8,128)(2,1)S(1)} %get-tuple-element.228), channel_id=1, source_target_pairs={{0,1},{1,0},{2,3},{3,2},{4,5},{5,4},{6,7},{7,6},{8,9},{9,8},{10,11... | collective-permute-start | bytes 4718600 | tf_op jit(solution)/shard_map/ppermute | solution.py:1206
  203.2 4.4 %collective-permute-start.14 = (bf16[2,4,48,1536]{3,2,1,0:T(8,128)(2,1)}, bf16[2,4,48,1536]{3,2,1,0:T(8,128)(2,1)}, u32[]{:S(2)}, u32[]{:S(2)}) collective-permute-start(bf16[2,4,48,1536]{3,2,1,0:T(8,128)(2,1)} %inner_sent.1), channel_id=1, source_target_pairs={{0,1},{1,0},{2,3},{3,2},{4,5},{5,4},{6,7},{7,6},{8,9},{9,8},{10,11... | collective-permute-start | bytes 3538952 | tf_op jit(solution)/shard_map/ppermute | solution.py:1206
  203.4 4.7 %collective-permute-start.13 = (bf16[2,4,48,1536]{3,2,1,0:T(8,128)(2,1)}, bf16[2,4,48,1536]{3,2,1,0:T(8,128)(2,1)}, u32[]{:S(2)}, u32[]{:S(2)}) collective-permute-start(bf16[2,4,48,1536]{3,2,1,0:T(8,128)(2,1)} %outer_sent.1), channel_id=1, source_target_pairs={{0,1},{1,0},{2,3},{3,2},{4,5},{5,4},{6,7},{7,6},{8,9},{9,8},{10,11... | collective-permute-start | bytes 3538952 | tf_op jit(solution)/shard_map/ppermute | solution.py:1206
  212.3 29.1 %collective-permute-start.16 = (bf16[4,48,3072]{2,1,0:T(8,128)(2,1)S(1)}, bf16[4,48,3072]{2,1,0:T(8,128)(2,1)S(1)}, u32[]{:S(2)}, u32[]{:S(2)}) collective-permute-start(bf16[4,48,3072]{2,1,0:T(8,128)(2,1)S(1)} %get-tuple-element.254), channel_id=1, source_target_pairs={{0,2},{1,3},{2,0},{3,1},{4,6},{5,7},{6,4},{7,5},{8,10},{9,11},{10,... | collective-permute-start | bytes 3538952 | tf_op jit(solution)/shard_map/ppermute | solution.py:1202
  212.7 27.6 %collective-permute-start.15 = (bf16[2,192,768]{2,1,0:T(8,128)(2,1)S(1)}, bf16[2,192,768]{2,1,0:T(8,128)(2,1)S(1)}, u32[]{:S(2)}, u32[]{:S(2)}) collective-permute-start(bf16[2,192,768]{2,1,0:T(8,128)(2,1)S(1)} %get-tuple-element.247), channel_id=1, source_target_pairs={{0,4},{4,0},{8,12},{12,8},{1,5},{5,1},{9,13},{13,9},{2,6},{6,2},{1... | collective-permute-start | bytes 1769480 | tf_op jit(solution)/shard_map/ppermute | solution.py:1210
  214.5 28.4 %collective-permute-start.19 = (bf16[2,48,3072]{2,1,0:T(8,128)(2,1)S(1)}, bf16[2,48,3072]{2,1,0:T(8,128)(2,1)S(1)}, u32[]{:S(2)}, u32[]{:S(2)}) collective-permute-start(bf16[2,48,3072]{2,1,0:T(8,128)(2,1)S(1)} %get-tuple-element.261), channel_id=1, source_target_pairs={{0,8},{4,12},{8,0},{12,4},{1,9},{5,13},{9,1},{13,5},{2,10},{6,14},... | collective-permute-start | bytes 1769480 | tf_op jit(solution)/shard_map/ppermute | solution.py:1210
  219.8 20.7 %copy-start.27 = (f32[512,768]{1,0:T(8,128)}, f32[512,768]{1,0:T(8,128)S(1)}, u32[]{:S(2)}) copy-start(f32[512,768]{1,0:T(8,128)S(1)} %get-tuple-element.251) | copy-start | bytes 4718596
  219.9 1.3 collective-permute-start.17
  221.2 20.3 %collective-permute-start.18 = (f32[12,768]{1,0:T(8,128)S(1)}, f32[12,768]{1,0:T(8,128)S(1)}, u32[]{:S(2)}, u32[]{:S(2)}) collective-permute-start(f32[12,768]{1,0:T(8,128)S(1)} %fusion.14), channel_id=1, source_target_pairs={{0,2},{1,3},{2,0},{3,1},{4,6},{5,7},{6,4},{7,5},{8,10},{9,11},{10,... | collective-permute-start | bytes 110600 | tf_op jit(solution)/shard_map/ppermute | solution.py:1202
  222.9 20.7 %copy-start.51 = (bf16[512,768]{1,0:T(8,128)(2,1)}, bf16[512,768]{1,0:T(8,128)(2,1)S(1)}, u32[]{:S(2)}) copy-start(bf16[512,768]{1,0:T(8,128)(2,1)S(1)} %convert_element_type.49) | copy-start | bytes 2359300
  242.8 20.9 %collective-permute-start.20 = (bf16[2,48,3072]{2,1,0:T(8,128)(2,1)S(1)}, bf16[2,48,3072]{2,1,0:T(8,128)(2,1)S(1)}, u32[]{:S(2)}, u32[]{:S(2)}) collective-permute-start(bf16[2,48,3072]{2,1,0:T(8,128)(2,1)S(1)} %get-tuple-element.263), channel_id=1, source_target_pairs={{0,4},{4,0},{8,12},{12,8},{1,5},{5,1},{9,13},{13,9},{2,6},{6,2},{1... | collective-permute-start | bytes 1769480 | tf_op jit(solution)/shard_map/ppermute | solution.py:1210
  243.6 20.1 %collective-permute-start.24 = (bf16[256,768]{1,0:T(8,128)(2,1)S(1)}, bf16[256,768]{1,0:T(8,128)(2,1)}, u32[]{:S(2)}, u32[]{:S(2)}) collective-permute-start(bf16[256,768]{1,0:T(8,128)(2,1)S(1)} %slice.57), channel_id=1, source_target_pairs={{0,2},{1,3},{2,0},{3,1},{4,6},{5,7},{6,4},{7,5},{8,10},{9,11},{10,... | collective-permute-start | bytes 1179656 | tf_op jit(solution)/shard_map/ppermute | solution.py:1202
  245.1 18.6 %collective-permute-start.21 = (bf16[48,3072]{1,0:T(8,128)(2,1)S(1)}, bf16[48,3072]{1,0:T(8,128)(2,1)}, u32[]{:S(2)}, u32[]{:S(2)}) collective-permute-start(bf16[48,3072]{1,0:T(8,128)(2,1)S(1)} %bitcast.104), channel_id=1, source_target_pairs={{0,2},{1,3},{2,0},{3,1},{4,6},{5,7},{6,4},{7,5},{8,10},{9,11},{10,... | collective-permute-start | bytes 884744 | tf_op jit(solution)/shard_map/ppermute | solution.py:1202
  245.7 18.0 %collective-permute-start.23 = (bf16[192,768]{1,0:T(8,128)(2,1)S(1)}, bf16[192,768]{1,0:T(8,128)(2,1)}, u32[]{:S(2)}, u32[]{:S(2)}) collective-permute-start(bf16[192,768]{1,0:T(8,128)(2,1)S(1)} %bitcast.102), channel_id=1, source_target_pairs={{0,8},{4,12},{8,0},{12,4},{1,9},{5,13},{9,1},{13,5},{2,10},{6,14},... | collective-permute-start | bytes 884744 | tf_op jit(solution)/shard_map/ppermute | solution.py:1210
  248.3 15.5 %collective-permute-start.22 = (f32[12,768]{1,0:T(8,128)S(1)}, f32[12,768]{1,0:T(8,128)S(1)}, u32[]{:S(2)}, u32[]{:S(2)}) collective-permute-start(f32[12,768]{1,0:T(8,128)S(1)} %add.105), channel_id=1, source_target_pairs={{0,4},{4,0},{8,12},{12,8},{1,5},{5,1},{9,13},{13,9},{2,6},{6,2},{1... | collective-permute-start | bytes 110600 | tf_op jit(solution)/shard_map/ppermute | solution.py:1210
  263.9 18.2 %collective-permute-start.25 = (bf16[48,3072]{1,0:T(8,128)(2,1)S(1)}, bf16[48,3072]{1,0:T(8,128)(2,1)S(1)}, u32[]{:S(2)}, u32[]{:S(2)}) collective-permute-start(bf16[48,3072]{1,0:T(8,128)(2,1)S(1)} %bitcast.103), channel_id=1, source_target_pairs={{0,8},{4,12},{8,0},{12,4},{1,9},{5,13},{9,1},{13,5},{2,10},{6,14},... | collective-permute-start | bytes 884744 | tf_op jit(solution)/shard_map/ppermute | solution.py:1210
  266.6 14.1 %collective-permute-start.26 = (f32[12,768]{1,0:T(8,128)S(1)}, f32[12,768]{1,0:T(8,128)S(1)}, u32[]{:S(2)}, u32[]{:S(2)}) collective-permute-start(f32[12,768]{1,0:T(8,128)S(1)} %add.106), channel_id=1, source_target_pairs={{0,8},{4,12},{8,0},{12,4},{1,9},{5,13},{9,1},{13,5},{2,10},{6,14},... | collective-permute-start | bytes 110600 | tf_op jit(solution)/shard_map/ppermute | solution.py:1210
  (45 other events, 232.7 us)
